TPU v7x, 256 devices: a whole 4x4x8 slice. The times are simulated.
256 devices in a mesh: ctx: 32 (over y, z_hi, core), tp: 8 (over x, z_lo).
Axes of the slice: x: 4, y: 4, z: 8 (z_hi: 4, z_lo: 2; z = z_hi * 2 + z_lo), core: 2. Of those that a mesh axis runs over, the one named last changes fastest.
Arguments:
- projections: bfloat16 [32768, 3, 1024], P('ctx', None, 'tp'), may hold values from -71 to 71
- short_filter: float32 [3, 3, 1024], P(None, None, 'tp'), may hold values from -3.5 to 3.5
- residues: float32 [16, 1024], P(None, 'tp'), may hold values from -1.5 to 1.5
- decays: float32 [16, 1024], P(None, 'tp'), may hold values from 1.5258789e-05 to 0.05
- skip: float32 [1024], P('tp'), may hold values from -3 to 3
- gain: float32 [1024], P('tp'), may hold values from 0.5 to 1.5
Outputs:
- mixed: bfloat16 [32768, 1024], P('ctx', 'tp')
All inputs are finite; a program needn't handle non-finite values.
Results may differ from a plain program's by a relative error of at most 0.009.
Values may be sent and summed in bfloat16 or wider, within the bound.
No kernel may reach another device: no remote copies, remote signals or barrier semaphores. Data moves between devices by JAX's collectives and lax.ppermute only.
A program may use at most 64 MiB of HBM per device.

v0:
```python
import math

import jax
import jax.numpy as jnp
from jax import lax
from jax.sharding import PartitionSpec as P

HIGHEST = lax.Precision.HIGHEST


def passed_along(block, axis, distance):
    devices = range(lax.axis_size(axis))
    route = [(i - distance, i) for i in devices if i - distance in devices]
    return lax.ppermute(block, axis, route)


def angle_table(left_count, right_count, modulus):
    left_index = lax.iota(jnp.int32, left_count)[:, None]
    right_index = lax.iota(jnp.int32, right_count)[None, :]
    return (left_index * right_index % modulus).astype(jnp.float32) * (2.0 * math.pi / modulus)


def make_tables(length):
    extent = 2 * length
    outer_size = 2
    while extent % (4 * outer_size) == 0 and 2 * outer_size * (2 * outer_size) <= extent:
        outer_size = 2 * outer_size
    inner_size = extent // outer_size
    outer_angle = angle_table(outer_size, outer_size, outer_size)
    inner_angle = angle_table(inner_size, inner_size, inner_size)
    twist = angle_table(outer_size, inner_size, extent)
    inner_cos = jnp.cos(inner_angle)
    inner_sin = jnp.sin(inner_angle)
    forward_mix = jnp.concatenate(
        [jnp.concatenate([inner_cos, -inner_sin], 1), jnp.concatenate([inner_sin, inner_cos], 1)], 0
    )
    backward_mix = jnp.concatenate(
        [jnp.concatenate([inner_cos, inner_sin], 1), jnp.concatenate([-inner_sin, inner_cos], 1)], 0
    )
    return (
        jnp.cos(outer_angle),
        jnp.sin(outer_angle),
        jnp.cos(twist),
        jnp.sin(twist),
        forward_mix,
        backward_mix,
        outer_size,
        inner_size,
    )


def to_spectrum(signal, tables):
    (
        outer_cos,
        outer_sin,
        twist_cos,
        twist_sin,
        forward_mix,
        backward_mix,
        outer_size,
        inner_size,
    ) = tables
    lower_rows = outer_size // 2
    blocks = signal.reshape(signal.shape[0], lower_rows, inner_size)
    part_re = jnp.einsum("ka,cab->ckb", outer_cos[:, :lower_rows], blocks, precision=HIGHEST)
    part_im = -jnp.einsum("ka,cab->ckb", outer_sin[:, :lower_rows], blocks, precision=HIGHEST)
    turned = jnp.concatenate(
        [part_re * twist_cos + part_im * twist_sin, part_im * twist_cos - part_re * twist_sin], 2
    )
    return jnp.einsum("ckb,bj->ckj", turned, forward_mix, precision=HIGHEST)


def from_spectrum(spectrum, tables):
    (
        outer_cos,
        outer_sin,
        twist_cos,
        twist_sin,
        forward_mix,
        backward_mix,
        outer_size,
        inner_size,
    ) = tables
    lower_rows = outer_size // 2
    sectioned = jnp.einsum("ckj,jb->ckb", spectrum, backward_mix, precision=HIGHEST)
    sectioned_re = sectioned[:, :, :inner_size]
    sectioned_im = sectioned[:, :, inner_size:]
    back_re = sectioned_re * twist_cos - sectioned_im * twist_sin
    back_im = sectioned_im * twist_cos + sectioned_re * twist_sin
    signal = jnp.einsum("ak,ckb->cab", outer_cos[:lower_rows], back_re, precision=HIGHEST)
    signal = signal - jnp.einsum("ak,ckb->cab", outer_sin[:lower_rows], back_im, precision=HIGHEST)
    return signal.reshape(signal.shape[0], -1) / (outer_size * inner_size)


def time_response(decay_rates, mode_weights, length):
    positions = jnp.arange(length, dtype=jnp.float32)
    return jnp.sum(
        mode_weights[:, :, None] * jnp.exp(-decay_rates[:, :, None] * positions[None, None, :]), 0
    )


def convolve(values, decay_rates, mode_weights, tables, length):
    inner_size = tables[7]
    filter_spec = to_spectrum(time_response(decay_rates, mode_weights, length), tables)
    signal_spec = to_spectrum(values, tables)
    signal_re = signal_spec[:, :, :inner_size]
    signal_im = signal_spec[:, :, inner_size:]
    filter_re = filter_spec[:, :, :inner_size]
    filter_im = filter_spec[:, :, inner_size:]
    joined = jnp.concatenate(
        [
            signal_re * filter_re - signal_im * filter_im,
            signal_re * filter_im + signal_im * filter_re,
        ],
        2,
    )
    return from_spectrum(joined, tables)


def owned_filters(residues, decays, first_channel, channel_count):
    decay_rates = lax.dynamic_slice_in_dim(decays, first_channel, channel_count, 1)
    mode_weights = lax.dynamic_slice_in_dim(residues, first_channel, channel_count, 1) * jnp.sqrt(
        2.0 * decay_rates
    )
    return (decay_rates, mode_weights)


def per_device(projections, short_filter, residues, decays, skip, gain):
    local_rows = projections.shape[0]
    local_width = projections.shape[2]
    tap_count = short_filter.shape[1]
    earlier = passed_along(projections[local_rows - (tap_count - 1) :], "ctx", 1)
    padded = jnp.concatenate([earlier, projections], 0).astype(jnp.float32)
    filtered = short_filter[:, 0, :][None] * padded[tap_count - 1 :]
    for offset in range(1, tap_count):
        filtered = (
            filtered
            + short_filter[:, offset, :][None]
            * padded[tap_count - 1 - offset : tap_count - 1 - offset + local_rows]
        )
    product = filtered[:, 1, :] * filtered[:, 2, :]
    ctx_count = lax.axis_size("ctx")
    owned_count = local_width // ctx_count
    length = local_rows * ctx_count
    first_owned = lax.axis_index("ctx") * owned_count
    tables = make_tables(length)
    across = product.T
    arrived = lax.all_to_all(across, "ctx", split_axis=0, concat_axis=1, tiled=True)
    decay_rates, mode_weights = owned_filters(residues, decays, first_owned, owned_count)
    result = convolve(arrived, decay_rates, mode_weights, tables, length)
    returned = lax.all_to_all(
        result.astype(jnp.bfloat16), "ctx", split_axis=1, concat_axis=0, tiled=True
    ).astype(result.dtype)
    gated_out = filtered[:, 0, :] * (returned.T + skip[None, :] * product)
    squares = lax.psum(jnp.sum(gated_out * gated_out, 1), "tp")
    channels = local_width * lax.axis_size("tp")
    mixed_out = gain[None, :] * gated_out * lax.rsqrt(squares[:, None] / channels + 1e-05)
    return mixed_out.astype(jnp.bfloat16)


def solution(mesh):
    in_specs = (
        P("ctx", None, "tp"),
        P(None, None, "tp"),
        P(None, "tp"),
        P(None, "tp"),
        P("tp"),
        P("tp"),
    )
    out_specs = P("ctx", "tp")
    return jax.shard_map(
        per_device, mesh=mesh, in_specs=in_specs, out_specs=out_specs, check_vma=False
    )
```

profile of v0, /device:TPU:2, one launch (start us, length us, event | category | flops | bytes accessed | tf_op | source)
XLA Modules:
  0.0 97.9 jit_solution(280312657711967042)
XLA Ops:
  0.0 0.7 slice.67
  0.7 0.2 copy.63
  0.9 1.7 %collective-permute-start = (bf16[2,3,128]{0,2,1:T(8,128)(2,1)S(1)}, bf16[2,3,128]{0,2,1:T(8,128)(2,1)S(1)}, u32[]{:S(2)}, u32[]{:S(2)}) collective-permute-start(bf16[2,3,128]{0,2,1:T(8,128)(2,1)S(1)} %copy.63), channel_id=1, source_target_pairs={{0,8},{8,16},{16,24},{24,32},{32,40},{40,48},{48,56},{56,64},{64,7... | collective-permute-start | bytes 4616 | tf_op jit(solution)/shard_map/ppermute | solution.py:14
  2.6 1.0 fusion.63
  3.6 0.8 fusion.69
  4.4 0.8 constant_dynamic-slice_fusion
  5.2 0.1 copy.92
  5.3 0.1 copy.91
  5.4 1.0 fusion.61
  6.3 1.4 %copy.64 = bf16[1024,3,128]{0,2,1:T(8,128)(2,1)S(1)} copy(bf16[1024,3,128]{2,0,1:T(8,128)(2,1)} %param.6) | data formatting | bytes 1572864 | tf_op args[0]
  7.8 0.0 collective-permute-done
  7.8 0.4 maximum_convert_fusion
  8.1 1.2 %fusion.12 = f32[1024,3,128]{0,2,1:T(8,128)S(1)} fusion(f32[1026,3,128]{0,2,1:T(8,128)S(1)} %maximum_convert_fusion, f32[3,128]{1,0:T(4,128)S(1)} %get-tuple-element.22, f32[3,128]{1,0:T(4,128)S(1)} %get-tuple-element.23, f32[3,128]{1,0:T(4,128)S(1)} %bitcast.72), kind=kLoop, calls=%fused_computation.14 | loop fusion | flops 1966080 | bytes 6296064 | tf_op jit(solution)/shard_map/add | solution.py:137
  9.3 0.1 fusion.59
  9.4 0.9 all_to_all.20
  10.3 13.0 %all-to-all-start = ((f32[32,4,1024]{2,1,0:T(4,128)}), f32[32,4,1024]{2,1,0:T(4,128)S(1)}, u32[]{:S(2)}, u32[]{:S(2)}) async-start(f32[32,4,1024]{2,1,0:T(4,128)} %all_to_all.20), calls=%async_computation | async-start | bytes 1048576 | tf_op jit(solution)/shard_map/all_to_all | solution.py:148
  23.4 1.0 fusion.60
  24.3 0.1 copy.67
  24.5 0.1 copy.69
  24.6 1.0 %fusion.62 = (f32[256,256]{1,0:T(8,128)S(1)}, f32[256,256]{1,0:T(8,128)S(1)}) fusion(), kind=kLoop, calls=%fused_computation.96 | loop fusion | flops 983040 | bytes 524288 | tf_op jit(solution)/shard_map/sin | solution.py:42
  25.6 2.6 %multiply_reduce_fusion = f32[4,32768]{1,0:T(4,128)S(1)} fusion(f32[16,4]{0,1:T(4,128)S(1)} %get-tuple-element.19, f32[16,4]{0,1:T(4,128)S(1)} %get-tuple-element.18), kind=kLoop, calls=%fused_computation | loop fusion | flops 6160384 | bytes 524800 | tf_op jit(solution)/shard_map/reduce_sum | solution.py:97
  28.2 2.0 %fusion.14 = f32[4,256,256]{1,2,0:T(8,128)} fusion(f32[1,4,128,256]{3,1,2,0:T(4,128)S(1)} %bitcast.70, f32[256,256]{1,0:T(8,128)S(1)} %get-tuple-element.24), kind=kOutput, calls=%fused_computation.23 | convolution fusion | flops 402915328 | bytes 1703936 | tf_op jit(solution)/shard_map/ka,cab->ckb/dot_general | solution.py:66
  30.2 2.0 %convolution_bitcast_fusion = f32[4,256,256]{1,2,0:T(8,128)} fusion(f32[1,4,128,256]{3,1,2,0:T(4,128)S(1)} %bitcast.71, f32[256,256]{1,0:T(8,128)S(1)} %fusion.63), kind=kOutput, calls=%fused_computation.24 | convolution fusion | flops 402653184 | bytes 1703936 | tf_op jit(solution)/shard_map/ka,cab->ckb/dot_general | solution.py:65
  32.2 8.6 %all-to-all-done = f32[32,4,1024]{2,1,0:T(4,128)S(1)} async-done(((f32[32,4,1024]{2,1,0:T(4,128)}), f32[32,4,1024]{2,1,0:T(4,128)S(1)}, u32[]{:S(2)}, u32[]{:S(2)}) %all-to-all-start) | async-done | bytes 524320 | tf_op jit(solution)/shard_map/all_to_all | solution.py:148
  40.9 1.1 %copy.65 = f32[4,32,1024]{2,1,0:T(8,128)} copy(f32[4,32,1024]{2,0,1:T(4,128)S(1)} %bitcast.69) | data formatting | bytes 1048576 | tf_op jit(solution)/shard_map/all_to_all | solution.py:148
  42.0 1.2 %reshape.69 = f32[4,128,256]{2,1,0:T(8,128)S(1)} reshape(f32[4,32,1024]{2,1,0:T(8,128)} %copy.65) | data formatting | bytes 1048576 | tf_op jit(solution)/shard_map/reshape | solution.py:64
  43.2 0.0 copy-start
  43.2 1.0 %convolution_bitcast_fusion.1 = f32[4,256,256]{1,2,0:T(8,128)S(1)} fusion(f32[4,128,256]{2,1,0:T(8,128)S(1)} %reshape.69, f32[256,256]{1,0:T(8,128)S(1)} %fusion.63), kind=kOutput, calls=%fused_computation.27 | convolution fusion | flops 402653184 | bytes 1703936 | tf_op jit(solution)/shard_map/ka,cab->ckb/dot_general | solution.py:65
  44.2 0.2 copy-done
  44.4 2.6 %multiply_add_fusion.2 = (f32[4,256,256]{1,2,0:T(8,128)S(1)}, f32[4,256,256]{1,2,0:T(8,128)S(1)}, f32[4,256,256]{1,2,0:T(8,128)S(1)}, f32[4,256,256]{1,2,0:T(8,128)S(1)}) fusion(f32[4,256,256]{1,2,0:T(8,128)S(1)} %convolution_bitcast_fusion.1, f32[256,256]{0,1:T(8,128)S(1)} %copy.69, f32[256,256]{0,1:T(8,128)S(1)} %copy.67, ...), kind=kOutput, calls=%fused_computation.50 | convolution fusion | flops 406061056 | bytes 8519680 | tf_op jit(solution)/shard_map/ka,cab->ckb/dot_general | solution.py:66
  47.0 3.7 %fusion = f32[4,256,512]{2,1,0:T(8,128)S(1)} fusion(f32[4,256,256]{1,2,0:T(8,128)S(1)} %get-tuple-element.10, f32[4,256,256]{1,2,0:T(8,128)S(1)} %get-tuple-element.9, f32[256,256]{1,0:T(8,128)S(1)} %fusion.63, f32[256,256]{1,0:T(8,128)S(1)} %get-tuple-element.24, f32[256,256]{1,0:T(8,128)S(1)} %get-tuple-element.25), kind=kOutput, calls=%fused_computation.1 | convolution fusion | flops 3222536192 | bytes 4980736 | tf_op jit(solution)/shard_map/ckb,bj->ckj/dot_general | solution.py:70
  50.8 3.5 %fusion.4 = f32[4,256,512]{2,1,0:T(8,128)S(1)} fusion(f32[4,256,256]{1,2,0:T(8,128)S(1)} %get-tuple-element.13, f32[4,256,256]{1,2,0:T(8,128)S(1)} %get-tuple-element.14, f32[256,256]{1,0:T(8,128)S(1)} %fusion.63, f32[256,256]{1,0:T(8,128)S(1)} %get-tuple-element.24, f32[256,256]{1,0:T(8,128)S(1)} %get-tuple-element.25), kind=kOutput, calls=%fused_computation.5 | convolution fusion | flops 3222536192 | bytes 4980736 | tf_op jit(solution)/shard_map/ckb,bj->ckj/dot_general | solution.py:70
  54.3 0.3 multiply_subtract_fusion
  54.6 3.5 %fusion.8 = f32[4,256,512]{1,2,0:T(8,128)S(1)} fusion(f32[4,256,256]{2,1,0:T(8,128)S(1)} %get-tuple-element.8, f32[4,256,256]{2,1,0:T(8,128)S(1)} %get-tuple-element.7, f32[256,256]{1,0:T(8,128)S(1)} %fusion.63, f32[256,256]{1,0:T(8,128)S(1)} %get-tuple-element.25, f32[256,256]{1,0:T(8,128)S(1)} %get-tuple-element.24), kind=kOutput, calls=%fused_computation.9 | convolution fusion | flops 3222536192 | bytes 4980736 | tf_op jit(solution)/shard_map/ckj,jb->ckb/dot_general | solution.py:85
  58.1 1.1 %fusion.29 = f32[4,256,128]{2,1,0:T(8,128)S(1)} fusion(f32[4,256,512]{1,2,0:T(8,128)S(1)} %fusion.8, f32[256,256]{0,1:T(8,128)S(1)} %copy.69, f32[256,256]{0,1:T(8,128)S(1)} %copy.67, f32[256,256]{1,0:T(8,128)S(1)} %fusion.63), kind=kOutput, calls=%fused_computation.41 | convolution fusion | flops 403439616 | bytes 3276800 | tf_op jit(solution)/shard_map/ak,ckb->cab/dot_general | solution.py:90
  59.2 1.1 %fusion.18 = bf16[4,128,256]{1,2,0:T(8,128)(2,1)S(1)} fusion(f32[4,256,128]{2,1,0:T(8,128)S(1)} %fusion.29, f32[4,256,512]{1,2,0:T(8,128)S(1)} %fusion.8, f32[256,256]{0,1:T(8,128)S(1)} %copy.69, f32[256,256]{0,1:T(8,128)S(1)} %copy.67, f32[256,256]{1,0:T(8,128)S(1)} %get-tuple-element.24), kind=kOutput, calls=%fused_computation.31 | convolution fusion | flops 403832832 | bytes 3538944 | tf_op jit(solution)/shard_map/ak,ckb->cab/dot_general | solution.py:91
  60.3 0.0 copy-start.2
  60.3 0.1 copy.78
  60.4 0.2 convert_element_type.90
  60.6 0.2 copy.79
  60.8 17.9 %all_to_all.26 = bf16[4,32,1024]{2,0,1:T(4,128)(2,1)S(1)} all-to-all(bf16[4,32,1024]{2,0,1:T(4,128)(2,1)S(1)} %copy.79), channel_id=1, replica_groups=mesh['ctx'=32,'tp'=8] {'ctx'}, dimensions={1} | all-to-all | bytes 524288 | tf_op jit(solution)/shard_map/all_to_all | solution.py:151
  78.7 0.1 convert_bitcast_fusion
  78.7 0.2 reshape.71
  78.9 0.0 copy-done.2
  78.9 0.2 multiply_reduce_fusion.1
  79.1 17.8 %psum.7 = f32[1024]{0:T(1024)S(1)} all-reduce(f32[1024]{0:T(1024)S(1)} %get-tuple-element.5), channel_id=1, replica_groups=mesh['ctx'=32,'tp'=8] {'tp'}, use_global_device_ids=true, to_apply=%region_2.3 | all-reduce | flops 1024 | bytes 8192 | tf_op jit(solution)/shard_map/psum | solution.py:155
  97.0 0.1 multiply_convert_fusion
  97.1 0.8 copy.80
  (6 shorter events, 0.0 us)
Async XLA Ops:
  0.9 6.9 %collective-permute-start = (bf16[2,3,128]{0,2,1:T(8,128)(2,1)S(1)}, bf16[2,3,128]{0,2,1:T(8,128)(2,1)S(1)}, u32[]{:S(2)}, u32[]{:S(2)}) collective-permute-start(bf16[2,3,128]{0,2,1:T(8,128)(2,1)S(1)} %copy.63), channel_id=1, source_target_pairs={{0,8},{8,16},{16,24},{24,32},{32,40},{40,48},{48,56},{56,64},{64,7... | collective-permute-start | bytes 4616 | tf_op jit(solution)/shard_map/ppermute | solution.py:14
  10.3 30.5 %all-to-all-start = ((f32[32,4,1024]{2,1,0:T(4,128)}), f32[32,4,1024]{2,1,0:T(4,128)S(1)}, u32[]{:S(2)}, u32[]{:S(2)}) async-start(f32[32,4,1024]{2,1,0:T(4,128)} %all_to_all.20), calls=%async_computation | async-start | bytes 1048576 | tf_op jit(solution)/shard_map/all_to_all | solution.py:148
  43.2 1.2 %copy-start = (f32[4,256,256]{1,2,0:T(8,128)S(1)}, f32[4,256,256]{1,2,0:T(8,128)}, u32[]{:S(2)}) copy-start(f32[4,256,256]{1,2,0:T(8,128)} %fusion.14) | copy-start | bytes 3145732
  60.3 18.7 %copy-start.2 = (f32[128]{0:T(128)S(1)}, f32[128]{0:T(128)}, u32[]{:S(2)}) copy-start(f32[128]{0:T(128)} %param.10) | copy-start | bytes 1540
  78.7 18.3 %copy-start.1 = (f32[128]{0:T(128)S(1)}, f32[128]{0:T(128)}, u32[]{:S(2)}) copy-start(f32[128]{0:T(128)} %param.11) | copy-start | bytes 1540
where the time goes:
time: 98.9 us; the launch traced here: 97.9 us
  blocking collectives  35.7 us (36%)
  matrix products  20.6 us (21%)
  starting transfers between devices  14.8 us (15%)
  local copies, waits for them, and re-layouts  9.26 us (9%)
  other arithmetic  8.7 us (9%)
  waiting for transfers between devices  8.62 us (9%)
    all_to_all x1, blocking collectives, per_device(): lax.all_to_all(result.astype(jnp.bfloat16), 'ctx', split_axis=1, concat_a...  17.9 us
    psum x1, blocking collectives, per_device(): squares = lax.psum(jnp.sum(gated_out * gated_out, 1), 'tp')  17.8 us
    all_to_all x1, starting transfers between devices, per_device(): lax.all_to_all(across, 'ctx', split_axis=0, concat_axis=1, tiled=True)  13 us
    all_to_all x1, waiting for transfers between devices, per_device(): lax.all_to_all(across, 'ctx', split_axis=0, concat_axis=1, tiled=True)  8.61 us
    dot_general x2, matrix products, to_spectrum(): return jnp.einsum('ckb,bj->ckj', turned, forward_mix, precision=HIGHEST)  7.25 us
    dot_general x2, matrix products, to_spectrum(): jnp.einsum('ka,cab->ckb', outer_sin[:, :lower_rows], blocks, precision=HI...  4.68 us
    dot_general x1, matrix products, from_spectrum(): jnp.einsum('ckj,jb->ckb', spectrum, backward_mix, precision=HIGHEST)  3.54 us
    dot_general x2, matrix products, to_spectrum(): jnp.einsum('ka,cab->ckb', outer_cos[:, :lower_rows], blocks, precision=HI...  3.03 us
  transfers between devices with their start and end apart: 2, of which 1 were waited for; matrix products, arithmetic and copies ran while one was open for 14% of the time, Pallas kernels for 0%

commit v1 on v0

v1 whole, which is shorter than its diff:
```python
import functools

import jax
import jax.numpy as jnp
from jax import lax
from jax.experimental import pallas as pl
from jax.experimental.pallas import tpu as pltpu
from jax.sharding import PartitionSpec as P

F32 = jnp.float32
BF16 = jnp.bfloat16
CHUNKS = 8
LANES = 128
VMEM_LIMIT = 32 * 1024 * 1024
VMEM = pl.BlockSpec(memory_space=pltpu.VMEM)

LAST = 0
FIRST = 6
EXTRA = 16


def over_sublanes(row):
    return jnp.broadcast_to(row, (CHUNKS, LANES))


def sublane_index():
    return lax.broadcasted_iota(jnp.int32, (CHUNKS, LANES), 0)


def next_chunk(block, distance=1):
    rolled = pltpu.roll(block, distance, 0)
    return jnp.where(sublane_index() >= distance, rolled, 0.0)


def strided(ref, step, run):
    return ref[pl.ds(step, CHUNKS, stride=run), :]


def added(terms):
    while len(terms) > 1:
        pairs = [terms[i] + terms[i + 1] for i in range(0, len(terms) - 1, 2)]
        terms = pairs + terms[2 * len(pairs) :]
    return terms[0]


def states_kernel(modes, x_ref, taps_ref, decays_ref, sent_ref, product_ref, state_ref, k_ref, v_ref, rows_ref):
    positions = x_ref.shape[1]
    run = positions // CHUNKS
    k_ref[...] = x_ref[1].astype(F32)
    v_ref[...] = x_ref[2].astype(F32)
    k_taps = [over_sublanes(taps_ref[1, i : i + 1, :]) for i in range(3)]
    v_taps = [over_sublanes(taps_ref[2, i : i + 1, :]) for i in range(3)]
    factors = [over_sublanes(jnp.exp(-decays_ref[m : m + 1, :])) for m in range(modes)]

    def step(j, carry):
        k1, k2, v1, v2, states = carry
        k0 = strided(k_ref, j, run)
        v0 = strided(v_ref, j, run)
        k = k_taps[0] * k0 + k_taps[1] * k1 + k_taps[2] * k2
        v = v_taps[0] * v0 + v_taps[1] * v1 + v_taps[2] * v2
        product = k * v
        product_ref[j] = product
        states = tuple(a * h + product for a, h in zip(factors, states))
        return k0, k1, v0, v1, states

    start = (
        next_chunk(strided(k_ref, run - 1, run)),
        next_chunk(strided(k_ref, run - 2, run)),
        next_chunk(strided(v_ref, run - 1, run)),
        next_chunk(strided(v_ref, run - 2, run)),
        tuple(jnp.zeros((CHUNKS, LANES), F32) for _ in range(modes)),
    )
    states = lax.fori_loop(0, run, step, start, unroll=8)[4]
    for m in range(modes):
        total = states[m]
        distance = 1
        while distance < CHUNKS:
            factor = over_sublanes(jnp.exp(-float(run * distance) * decays_ref[m : m + 1, :]))
            total = total + factor * next_chunk(total, distance)
            distance *= 2
        state_ref[m] = next_chunk(total)
        rows_ref[m : m + 1, :] = total[CHUNKS - 1 : CHUNKS, :]
    rows_ref[modes : modes + 2, :] = k_ref[positions - 2 : positions, :]
    rows_ref[modes + 2 : modes + 4, :] = v_ref[positions - 2 : positions, :]
    rows_ref[modes + 4 : modes + 6, :] = x_ref[0, positions - 16 : positions, :].astype(F32)[14:16]
    rows_ref[modes + 6 : modes + 8, :] = k_ref[0:2, :]
    rows_ref[modes + 8 : modes + 10, :] = v_ref[0:2, :]
    rows_ref[modes + 10 :, :] = jnp.zeros((EXTRA - 10, LANES), F32)
    rows = rows_ref[...].astype(BF16)
    sent_ref[...] = jnp.broadcast_to(rows[None], sent_ref.shape)


def local_kernel(modes, x_ref, product_ref, taps_ref, decays_ref, residues_ref, skip_ref, gate_ref, base_ref, q_ref):
    positions = x_ref.shape[1]
    run = positions // CHUNKS
    q_ref[...] = x_ref[0].astype(F32)
    taps = [over_sublanes(taps_ref[0, i : i + 1, :]) for i in range(3)]
    skip = over_sublanes(skip_ref[...])
    rates = decays_ref[...]
    weights = residues_ref[...] * jnp.sqrt(2.0 * rates)
    factors = [over_sublanes(jnp.exp(-rates[m : m + 1, :])) for m in range(modes)]
    weights = [over_sublanes(weights[m : m + 1, :]) for m in range(modes)]

    def step(j, carry):
        q1, q2, states = carry
        q0 = strided(q_ref, j, run)
        gate_ref[j] = taps[0] * q0 + taps[1] * q1 + taps[2] * q2
        product = product_ref[j]
        states = tuple(a * h + product for a, h in zip(factors, states))
        base_ref[j] = added([skip * product] + [w * h for w, h in zip(weights, states)])
        return q0, q1, states

    start = (
        next_chunk(strided(q_ref, run - 1, run)),
        next_chunk(strided(q_ref, run - 2, run)),
        tuple(jnp.zeros((CHUNKS, LANES), F32) for _ in range(modes)),
    )
    lax.fori_loop(0, run, step, start, unroll=4)


def carry_kernel(
    modes, axis, count, received_ref, gate_ref, base_ref, state_ref, taps_ref, decays_ref, residues_ref, skip_ref,
    power_ref, gated_ref, rows_ref, first_ref, second_ref,
):
    run = gate_ref.shape[0]
    positions = run * CHUNKS
    device = lax.axis_index(axis)
    pitch = modes + EXTRA
    rows_ref[0:pitch, :] = jnp.zeros((pitch, LANES), F32)
    for e in range(count):
        rows_ref[pitch * (e + 1) : pitch * (e + 2), :] = received_ref[e].astype(F32)

    def of_all(row, shift):
        return rows_ref[pl.ds(pitch * (1 - shift) + modes + row, count, stride=pitch), :]

    products = []
    for j in (1, 2):
        tap = [taps_ref[j, i : i + 1, :] for i in range(3)]
        far = of_all(LAST + 2 * (j - 1), 1)
        near = of_all(LAST + 2 * (j - 1) + 1, 1)
        zero = of_all(FIRST + 2 * (j - 1), 0)
        one = of_all(FIRST + 2 * (j - 1) + 1, 0)
        own = (tap[0] * zero, tap[0] * one + tap[1] * zero)
        whole = (own[0] + tap[1] * near + tap[2] * far, own[1] + tap[2] * near)
        products.append((own, whole))
    (k_own, k_whole), (v_own, v_whole) = products
    first_ref[...] = k_whole[0] * v_whole[0] - k_own[0] * v_own[0]
    second_ref[...] = k_whole[1] * v_whole[1] - k_own[1] * v_own[1]

    rates = decays_ref[...]
    across = jnp.exp(-float(positions) * rates)
    state = jnp.zeros((modes, LANES), F32)
    late_first = jnp.exp(-float(positions - 1) * rates)
    late_second = jnp.exp(-float(positions - 2) * rates)
    for e in range(count - 1):
        arrived = rows_ref[pitch * (e + 1) : pitch * (e + 1) + modes, :]
        arrived = arrived + late_first * first_ref[e : e + 1, :] + late_second * second_ref[e : e + 1, :]
        state = jnp.where(e < device, across * state + arrived, state)
    first = first_ref[pl.ds(device, 1), :]
    second = second_ref[pl.ds(device, 1), :]
    weights = residues_ref[...] * jnp.sqrt(2.0 * rates)
    state = state + jnp.exp(rates) * first + jnp.exp(2.0 * rates) * second
    early = jnp.sum(weights * jnp.exp(rates), 0, keepdims=True) * second

    chunk = sublane_index()
    top = chunk == 0
    behind = chunk.astype(F32) * float(run)
    factors = []
    carried = []
    for m in range(modes):
        rate = over_sublanes(rates[m : m + 1, :])
        factors.append(jnp.exp(-rate))
        begin = state_ref[m] + jnp.exp(-rate * behind) * over_sublanes(state[m : m + 1, :])
        carried.append(over_sublanes(weights[m : m + 1, :]) * begin)

    edge = [rows_ref[pl.ds(device * pitch + modes + LAST + 4 + i, 1), :] for i in range(2)]
    gate_edge = (
        taps_ref[0, 1:2, :] * edge[1] + taps_ref[0, 2:3, :] * edge[0],
        taps_ref[0, 2:3, :] * edge[1],
    )
    skip = skip_ref[...]
    base_edge = (skip * first - early, skip * second)
    lane = lax.broadcasted_iota(jnp.int32, (CHUNKS, LANES), 1)

    def step(j, held, gate_extra=None, base_extra=None):
        carried, power = held
        carried = tuple(a * g for a, g in zip(factors, carried))
        gate, base = gate_ref[j], base_ref[j]
        if gate_extra is not None:
            gate = gate + jnp.where(top, over_sublanes(gate_extra), 0.0)
            base = base + jnp.where(top, over_sublanes(base_extra), 0.0)
        gated = gate * added([base] + list(carried))
        gated_ref[pl.ds(j, CHUNKS, stride=run), :] = gated
        square = jnp.sum(gated * gated, 1, keepdims=True)
        return carried, jnp.where(lane == j, square, power)

    held = (tuple(carried), jnp.zeros((CHUNKS, LANES), F32))
    for j in range(2):
        held = step(j, held, gate_edge[j], base_edge[j])
    power = lax.fori_loop(2, run, step, held, unroll=6)[1]
    power_ref[...] = jnp.broadcast_to(power[None], power_ref.shape)


def finish_kernel(channels, power_ref, gated_ref, gain_ref, mixed_ref):
    positions = gated_ref.shape[0]
    run = positions // CHUNKS
    inverse = lax.rsqrt(jnp.sum(power_ref[...], 0) / channels + 1e-05)
    turned = inverse.T
    gain = gain_ref[...]
    for s in range(CHUNKS):
        block = gated_ref[s * run : (s + 1) * run, :] * gain * turned[:, s : s + 1]
        mixed_ref[s * run : (s + 1) * run, :] = block.astype(BF16)


def per_device(projections, short_filter, residues, decays, skip, gain):
    positions, _, width = projections.shape
    modes = decays.shape[0]
    ctx_count = lax.axis_size("ctx")
    tp_count = lax.axis_size("tp")
    run = positions // CHUNKS
    x = jnp.swapaxes(projections, 0, 1)
    skip = skip[None, :]
    gain = gain[None, :]
    params = pltpu.CompilerParams(vmem_limit_bytes=VMEM_LIMIT)
    block = jax.ShapeDtypeStruct((run, CHUNKS, width), F32)

    sent, product, state = pl.pallas_call(
        functools.partial(states_kernel, modes),
        out_shape=(
            jax.ShapeDtypeStruct((ctx_count, modes + EXTRA, width), BF16),
            block,
            jax.ShapeDtypeStruct((modes, CHUNKS, width), F32),
        ),
        in_specs=[VMEM] * 3,
        out_specs=(VMEM,) * 3,
        scratch_shapes=[
            pltpu.VMEM((positions, width), F32),
            pltpu.VMEM((positions, width), F32),
            pltpu.VMEM((modes + EXTRA, width), F32),
        ],
        compiler_params=params,
        name="states",
    )(x, short_filter, decays)
    received = lax.all_to_all(sent, "ctx", split_axis=0, concat_axis=0, tiled=True)

    gate, base = pl.pallas_call(
        functools.partial(local_kernel, modes),
        out_shape=(block, block),
        in_specs=[VMEM] * 6,
        out_specs=(VMEM,) * 2,
        scratch_shapes=[pltpu.VMEM((positions, width), F32)],
        compiler_params=params,
        name="local",
    )(x, product, short_filter, decays, residues, skip)

    power, gated = pl.pallas_call(
        functools.partial(carry_kernel, modes, "ctx", ctx_count),
        out_shape=(
            jax.ShapeDtypeStruct((tp_count, CHUNKS, run), F32),
            jax.ShapeDtypeStruct((positions, width), F32),
        ),
        in_specs=[VMEM] * 8,
        out_specs=(VMEM,) * 2,
        scratch_shapes=[
            pltpu.VMEM(((ctx_count + 1) * (modes + EXTRA), width), F32),
            pltpu.VMEM((ctx_count, width), F32),
            pltpu.VMEM((ctx_count, width), F32),
        ],
        compiler_params=params,
        name="carry",
    )(received, gate, base, state, short_filter, decays, residues, skip)
    powers = lax.all_to_all(power, "tp", split_axis=0, concat_axis=0, tiled=True)

    return pl.pallas_call(
        functools.partial(finish_kernel, width * tp_count),
        out_shape=jax.ShapeDtypeStruct((positions, width), BF16),
        in_specs=[VMEM] * 3,
        out_specs=VMEM,
        compiler_params=params,
        name="finish",
    )(powers, gated, gain)


def solution(mesh):
    in_specs = (
        P("ctx", None, "tp"),
        P(None, None, "tp"),
        P(None, "tp"),
        P(None, "tp"),
        P("tp"),
        P("tp"),
    )
    return jax.shard_map(per_device, mesh=mesh, in_specs=in_specs, out_specs=P("ctx", "tp"), check_vma=False)
```

time: 98.9 us -> 45.3 us (0.46)
  the two profiles are of different devices: /device:TPU:2 before, /device:TPU:1 now
where the time goes in v1:
time: 45.3 us; the launch traced here: 44.9 us
  starting transfers between devices  12.9 us (28%)
  waiting for transfers between devices  11 us (24%)
  blocking collectives  9.63 us (21%)
  Pallas kernels  7.59 us (17%)
  local copies, waits for them, and re-layouts  3.8 us (8%)
    all_to_all x1, starting transfers between devices, per_device(): lax.all_to_all(sent, 'ctx', split_axis=0, concat_axis=0, tiled=True)  12.9 us
    all_to_all x1, waiting for transfers between devices, per_device(): lax.all_to_all(sent, 'ctx', split_axis=0, concat_axis=0, tiled=True)  11 us
    all_to_all x1, blocking collectives, per_device(): lax.all_to_all(power, 'tp', split_axis=0, concat_axis=0, tiled=True)  9.63 us
    unnamed x18, local copies, waits for them, and re-layouts  3.8 us
    pallas_call x1, Pallas kernels, per_device(): pl.pallas_call(functools.partial(carry_kernel, modes, 'ctx', ctx_count),...  2.64 us
    pallas_call x1, Pallas kernels, per_device(): pl.pallas_call(functools.partial(states_kernel, modes), out_shape=(jax.Sh...  2.13 us
    pallas_call x1, Pallas kernels, per_device(): pl.pallas_call(functools.partial(local_kernel, modes), out_shape=(block,...  1.78 us
    pallas_call x1, Pallas kernels, per_device(): pl.pallas_call(functools.partial(finish_kernel, width * tp_count), out_sh...  1.04 us
  transfers between devices with their start and end apart: 1, of which 1 were waited for; matrix products, arithmetic and copies ran while one was open for 0% of the time, Pallas kernels for 4%

profile of v1, /device:TPU:1, one launch (start us, length us, event | category | flops | bytes accessed | tf_op | source)
XLA Modules:
  0.0 44.9 jit_solution(4502901228840506849)
XLA Ops:
  0.0 0.0 copy-start
  0.0 1.1 %copy-done = bf16[1024,3,128]{2,0,1:T(8,128)(2,1)S(1)} copy-done((bf16[1024,3,128]{2,0,1:T(8,128)(2,1)S(1)}, bf16[1024,3,128]{2,0,1:T(8,128)(2,1)}, u32[]{:S(2)}) %copy-start) | copy-done | bytes 786456
  1.1 0.0 copy-start.2
  1.1 0.7 %copy-done.2 = f32[16,128]{1,0:T(8,128)S(1)} copy-done((f32[16,128]{1,0:T(8,128)S(1)}, f32[16,128]{1,0:T(8,128)}, u32[]{:S(2)}) %copy-start.2) | copy-done | bytes 8216
  1.8 0.0 copy-start.4
  1.8 0.7 %copy-done.4 = f32[3,3,128]{2,1,0:T(4,128)S(1)} copy-done((f32[3,3,128]{2,1,0:T(4,128)S(1)}, f32[3,3,128]{2,1,0:T(4,128)}, u32[]{:S(2)}) %copy-start.4) | copy-done | bytes 4632
  2.5 0.0 copy-start.1
  2.5 2.1 %states.1 = (bf16[32,32,128]{2,1,0:T(8,128)(2,1)}, f32[128,8,128]{2,1,0:T(8,128)S(1)}, f32[16,8,128]{2,1,0:T(8,128)S(1)}) custom-call(bf16[3,1024,128]{2,1,0:T(8,128)(2,1)S(1)} %bitcast.3, f32[3,3,128]{2,1,0:T(4,128)S(1)} %copy-done.4, f32[16,128]{1,0:T(8,128)S(1)} %copy-done.2), custom_call_target="tpu_custom_call" | custom-call | tf_op jit(solution)/shard_map/states/pallas_call | solution.py:227
  4.7 0.0 copy-start.3
  4.7 0.0 copy-start.5
  4.7 0.0 copy-start.6
  4.7 12.9 %all-to-all-start = ((bf16[32,32,128]{2,1,0:T(8,128)(2,1)}), bf16[32,32,128]{2,1,0:T(8,128)(2,1)S(1)}, u32[]{:S(2)}, u32[]{:S(2)}) async-start(bf16[32,32,128]{2,1,0:T(8,128)(2,1)} %get-tuple-element.12), calls=%async_computation | async-start | bytes 524288 | tf_op jit(solution)/shard_map/all_to_all | solution.py:244
  17.6 0.0 copy-start.7
  17.6 0.0 copy-done.1
  17.6 0.0 copy-done.3
  17.6 0.0 copy-done.5
  17.6 0.0 copy-done.6
  17.6 0.6 %copy-done.7 = f32[128]{0:T(128)S(1)} copy-done((f32[128]{0:T(128)S(1)}, f32[128]{0:T(128)}, u32[]{:S(2)}) %copy-start.7) | copy-done | bytes 536
  18.2 1.8 %local.1 = (f32[128,8,128]{2,1,0:T(8,128)S(1)}, f32[128,8,128]{2,1,0:T(8,128)S(1)}) custom-call(bf16[3,1024,128]{2,1,0:T(8,128)(2,1)S(1)} %bitcast.4, f32[128,8,128]{2,1,0:T(8,128)S(1)} %get-tuple-element.13.product_ref, f32[3,3,128]{2,1,0:T(4,128)S(1)} %copy-done.5, f32[16,128]{1,0:T(8,128)S(1)} %copy-done.3, f32[16,128]{1,0:T(8,128)S(1)} %copy-done.6, ...), custom_call_target="tpu_custom_call" | custom-call | tf_op jit(solution)/shard_map/local/pallas_call | solution.py:246
  20.0 11.0 %all-to-all-done.received_ref = bf16[32,32,128]{2,1,0:T(8,128)(2,1)S(1)} async-done(((bf16[32,32,128]{2,1,0:T(8,128)(2,1)}), bf16[32,32,128]{2,1,0:T(8,128)(2,1)S(1)}, u32[]{:S(2)}, u32[]{:S(2)}) %all-to-all-start) | async-done | bytes 262176 | tf_op jit(solution)/shard_map/all_to_all | solution.py:244
  31.0 2.6 %carry.1 = (f32[8,8,128]{2,1,0:T(8,128)S(1)}, f32[1024,128]{1,0:T(8,128)S(1)}) custom-call(bf16[32,32,128]{2,1,0:T(8,128)(2,1)S(1)} %all-to-all-done.received_ref, f32[128,8,128]{2,1,0:T(8,128)S(1)} %get-tuple-element.14.gate_ref, f32[128,8,128]{2,1,0:T(8,128)S(1)} %get-tuple-element.15.base_ref, f32[16,8,128]{2,1,0:T(8,128)S(1)} %get-tuple-element.16.state_ref, ...), custom_call_target="tpu_custom_call" | custom-call | tf_op jit(solution)/shard_map/carry/pallas_call | solution.py:256
  33.6 9.6 %all_to_all.10.power_ref = f32[8,8,128]{2,1,0:T(8,128)S(1)} all-to-all(f32[8,8,128]{2,1,0:T(8,128)S(1)} %get-tuple-element.17), channel_id=1, replica_groups=mesh['ctx'=32,'tp'=8] {'tp'}, dimensions={0} | all-to-all | bytes 65536 | tf_op jit(solution)/shard_map/all_to_all | solution.py:272
  43.2 0.0 copy-start.8
  43.2 0.7 %copy-done.8 = f32[128]{0:T(128)S(1)} copy-done((f32[128]{0:T(128)S(1)}, f32[128]{0:T(128)}, u32[]{:S(2)}) %copy-start.8) | copy-done | bytes 536
  43.9 1.0 %finish.1 = bf16[1024,128]{1,0:T(8,128)(2,1)} custom-call(f32[8,8,128]{2,1,0:T(8,128)S(1)} %all_to_all.10.power_ref, f32[1024,128]{1,0:T(8,128)S(1)} %get-tuple-element.18.gated_ref, f32[1,128]{1,0:T(1,128)S(1)} %bitcast.7), custom_call_target="tpu_custom_call" | custom-call | tf_op jit(solution)/shard_map/finish/pallas_call | solution.py:274
Async XLA Ops:
  0.0 1.1 %copy-start = (bf16[1024,3,128]{2,0,1:T(8,128)(2,1)S(1)}, bf16[1024,3,128]{2,0,1:T(8,128)(2,1)}, u32[]{:S(2)}) copy-start(bf16[1024,3,128]{2,0,1:T(8,128)(2,1)} %param.6) | copy-start | bytes 2359300
  1.1 0.7 %copy-start.2 = (f32[16,128]{1,0:T(8,128)S(1)}, f32[16,128]{1,0:T(8,128)}, u32[]{:S(2)}) copy-start(f32[16,128]{1,0:T(8,128)} %decays_ref.5) | copy-start | bytes 24580
  1.8 0.7 %copy-start.4 = (f32[3,3,128]{2,1,0:T(4,128)S(1)}, f32[3,3,128]{2,1,0:T(4,128)}, u32[]{:S(2)}) copy-start(f32[3,3,128]{2,1,0:T(4,128)} %taps_ref.5) | copy-start | bytes 13828
  2.5 15.0 %copy-start.1 = (bf16[1024,3,128]{2,0,1:T(8,128)(2,1)S(1)}, bf16[1024,3,128]{2,0,1:T(8,128)(2,1)}, u32[]{:S(2)}) copy-start(bf16[1024,3,128]{2,0,1:T(8,128)(2,1)} %param.6) | copy-start | bytes 2359300
  4.7 12.9 %copy-start.3 = (f32[16,128]{1,0:T(8,128)S(1)}, f32[16,128]{1,0:T(8,128)}, u32[]{:S(2)}) copy-start(f32[16,128]{1,0:T(8,128)} %decays_ref.5) | copy-start | bytes 24580
  4.7 12.9 %copy-start.5 = (f32[3,3,128]{2,1,0:T(4,128)S(1)}, f32[3,3,128]{2,1,0:T(4,128)}, u32[]{:S(2)}) copy-start(f32[3,3,128]{2,1,0:T(4,128)} %taps_ref.5) | copy-start | bytes 13828
  4.7 12.9 %copy-start.6 = (f32[16,128]{1,0:T(8,128)S(1)}, f32[16,128]{1,0:T(8,128)}, u32[]{:S(2)}) copy-start(f32[16,128]{1,0:T(8,128)} %residues_ref.3) | copy-start | bytes 24580
  4.7 26.3 %all-to-all-start = ((bf16[32,32,128]{2,1,0:T(8,128)(2,1)}), bf16[32,32,128]{2,1,0:T(8,128)(2,1)S(1)}, u32[]{:S(2)}, u32[]{:S(2)}) async-start(bf16[32,32,128]{2,1,0:T(8,128)(2,1)} %get-tuple-element.12), calls=%async_computation | async-start | bytes 524288 | tf_op jit(solution)/shard_map/all_to_all | solution.py:244
  17.6 0.7 %copy-start.7 = (f32[128]{0:T(128)S(1)}, f32[128]{0:T(128)}, u32[]{:S(2)}) copy-start(f32[128]{0:T(128)} %param.10) | copy-start | bytes 1540
  43.2 0.7 %copy-start.8 = (f32[128]{0:T(128)S(1)}, f32[128]{0:T(128)}, u32[]{:S(2)}) copy-start(f32[128]{0:T(128)} %param.11) | copy-start | bytes 1540

commit v2 on v1

v2 whole, which is shorter than its diff:
```python
import functools

import jax
import jax.numpy as jnp
from jax import lax
from jax.experimental import pallas as pl
from jax.experimental.pallas import tpu as pltpu
from jax.sharding import PartitionSpec as P

F32 = jnp.float32
BF16 = jnp.bfloat16
CHUNKS = 8
LANES = 128
PAIR = 2
VMEM_LIMIT = 40 * 1024 * 1024
VMEM = pl.BlockSpec(memory_space=pltpu.VMEM)
ANY = pl.BlockSpec(memory_space=pl.ANY)

K_LAST, V_LAST, Q_LAST, K_FIRST, V_FIRST = 0, 2, 4, 6, 8
EXTRA = 16


def over_sublanes(row):
    return jnp.broadcast_to(row, (CHUNKS, LANES))


def sublane_index():
    return lax.broadcasted_iota(jnp.int32, (CHUNKS, LANES), 0)


def next_chunk(block, distance=1):
    rolled = pltpu.roll(block, distance, 0)
    return jnp.where(sublane_index() >= distance, rolled, 0.0)


def strided(ref, step, run):
    return ref[pl.ds(step, CHUNKS, stride=run), :]


def added(terms):
    while len(terms) > 1:
        pairs = [terms[i] + terms[i + 1] for i in range(0, len(terms) - 1, 2)]
        terms = pairs + terms[2 * len(pairs) :]
    return terms[0]


def boundary(taps_ref, last, first):
    products = []
    for j in (1, 2):
        tap = [taps_ref[j, i : i + 1, :] for i in range(3)]
        (far, near), (zero, one) = last[j - 1], first[j - 1]
        own = (tap[0] * zero, tap[0] * one + tap[1] * zero)
        gained = (tap[1] * near + tap[2] * far, tap[2] * near)
        products.append((own, gained))
    (k_own, k_gained), (v_own, v_gained) = products
    return [k_own[i] * v_gained[i] + k_gained[i] * (v_own[i] + v_gained[i]) for i in range(2)]


def two_rows(ref, row):
    return ref[row : row + 1, :], ref[row + 1 : row + 2, :]


def pair_boundary(modes, taps_ref, lower_ref, upper_ref):
    last = [two_rows(lower_ref, modes + row) for row in (K_LAST, V_LAST)]
    first = [two_rows(upper_ref, modes + row) for row in (K_FIRST, V_FIRST)]
    return boundary(taps_ref, last, first)


def gate_gain(taps_ref, far, near):
    return taps_ref[0, 1:2, :] * near + taps_ref[0, 2:3, :] * far, taps_ref[0, 2:3, :] * near


def states_kernel(modes, *refs):
    sources, refs = refs[:6], refs[6:]
    x_hbm = sources[0]
    (rows_ref, product_ref, state_ref, q_ref), refs = refs[:4], refs[4:]
    params, refs = refs[:5], refs[5:]
    taps_ref, decays_ref = params[0], params[1]
    k_half, v_half, k_ref, v_ref, semaphores = refs
    copies = [pltpu.make_async_copy(s, d, semaphores.at[i]) for i, (s, d) in enumerate(zip(sources[1:], params))]
    streams = [
        pltpu.make_async_copy(x_hbm.at[j], d, semaphores.at[5 + j]) for j, d in enumerate((q_ref, k_half, v_half))
    ]
    for copy in (streams[1], streams[2], copies[1], copies[0], streams[0], copies[2], copies[3], copies[4]):
        copy.start()
    positions = k_ref.shape[0]
    run = positions // CHUNKS
    copies[1].wait()
    copies[0].wait()
    k_taps = [over_sublanes(taps_ref[1, i : i + 1, :]) for i in range(3)]
    v_taps = [over_sublanes(taps_ref[2, i : i + 1, :]) for i in range(3)]
    factors = [over_sublanes(jnp.exp(-decays_ref[m : m + 1, :])) for m in range(modes)]
    streams[1].wait()
    k_ref[...] = k_half[...].astype(F32)
    streams[2].wait()
    v_ref[...] = v_half[...].astype(F32)

    def step(j, carry):
        k1, k2, v1, v2, states = carry
        k0 = strided(k_ref, j, run)
        v0 = strided(v_ref, j, run)
        k = k_taps[0] * k0 + k_taps[1] * k1 + k_taps[2] * k2
        v = v_taps[0] * v0 + v_taps[1] * v1 + v_taps[2] * v2
        product = k * v
        product_ref[j] = product
        states = tuple(a * h + product for a, h in zip(factors, states))
        return k0, k1, v0, v1, states

    start = (
        next_chunk(strided(k_ref, run - 1, run)),
        next_chunk(strided(k_ref, run - 2, run)),
        next_chunk(strided(v_ref, run - 1, run)),
        next_chunk(strided(v_ref, run - 2, run)),
        tuple(jnp.zeros((CHUNKS, LANES), F32) for _ in range(modes)),
    )
    states = lax.fori_loop(0, run, step, start, unroll=8)[4]
    for m in range(modes):
        total = states[m]
        distance = 1
        while distance < CHUNKS:
            factor = over_sublanes(jnp.exp(-float(run * distance) * decays_ref[m : m + 1, :]))
            total = total + factor * next_chunk(total, distance)
            distance *= 2
        state_ref[m] = next_chunk(total)
        rows_ref[m : m + 1, :] = total[CHUNKS - 1 : CHUNKS, :]
    streams[0].wait()
    rows_ref[modes + K_LAST : modes + K_LAST + 2, :] = k_ref[positions - 2 : positions, :]
    rows_ref[modes + V_LAST : modes + V_LAST + 2, :] = v_ref[positions - 2 : positions, :]
    rows_ref[modes + Q_LAST : modes + Q_LAST + 2, :] = q_ref[positions - 16 : positions, :].astype(F32)[14:16]
    rows_ref[modes + K_FIRST : modes + K_FIRST + 2, :] = k_ref[0:2, :]
    rows_ref[modes + V_FIRST : modes + V_FIRST + 2, :] = v_ref[0:2, :]
    rows_ref[modes + V_FIRST + 2 :, :] = jnp.zeros((EXTRA - V_FIRST - 2, LANES), F32)
    for i in (2, 3, 4):
        copies[i].wait()


def join_kernel(modes, positions, axis, own_ref, other_ref, taps_ref, decays_ref, sent_ref, pair_ref):
    upper = lax.rem(lax.axis_index(axis), PAIR) == 1
    own = own_ref[...]
    other = other_ref[...]
    below = jnp.where(upper, other, own)
    above = jnp.where(upper, own, other)
    pair_ref[0] = below
    pair_ref[1] = above
    first, second = pair_boundary(modes, taps_ref, pair_ref.at[0], pair_ref.at[1])
    rates = decays_ref[...]
    state = jnp.exp(-float(positions) * rates) * below[:modes] + above[:modes]
    state = state + jnp.exp(-float(positions - 1) * rates) * first + jnp.exp(-float(positions - 2) * rates) * second
    row = lax.broadcasted_iota(jnp.int32, (EXTRA, LANES), 0)
    beside = jnp.where(row < K_FIRST, above[modes:], below[modes:])
    rows = jnp.concatenate([state, beside], 0).astype(BF16)
    sent_ref[...] = jnp.broadcast_to(rows[None], sent_ref.shape)


def local_kernel(
    modes, axis, pairs, q_half, product_ref, state_ref, pair_ref, taps_ref, decays_ref, residues_ref, skip_ref,
    gate_ref, base_ref, begin_ref, reach_ref, factor_ref, weight_ref, late_ref, q_ref,
):
    positions = q_ref.shape[0]
    run = positions // CHUNKS
    device = lax.axis_index(axis)
    pair = device // PAIR
    upper = lax.rem(device, PAIR)
    inside = upper.astype(F32)
    q_ref[...] = q_half[...].astype(F32)
    taps = [over_sublanes(taps_ref[0, i : i + 1, :]) for i in range(3)]
    skip = over_sublanes(skip_ref[...])
    rates = decays_ref[...]
    weights = residues_ref[...] * jnp.sqrt(2.0 * rates)
    factors = [over_sublanes(jnp.exp(-rates[m : m + 1, :])) for m in range(modes)]
    spread = [over_sublanes(weights[m : m + 1, :]) for m in range(modes)]

    first, second = pair_boundary(modes, taps_ref, pair_ref.at[0], pair_ref.at[1])
    first, second = first * inside, second * inside
    arrived = inside * pair_ref[0, :modes, :] + jnp.exp(rates) * first + jnp.exp(2.0 * rates) * second
    early = jnp.sum(weights * jnp.exp(rates), 0, keepdims=True) * second
    gain = gate_gain(taps_ref, *two_rows(pair_ref.at[0], modes + Q_LAST))

    def step(j, carry):
        q1, q2, states = carry
        q0 = strided(q_ref, j, run)
        gate_ref[j] = taps[0] * q0 + taps[1] * q1 + taps[2] * q2
        product = product_ref[j]
        states = tuple(a * h + product for a, h in zip(factors, states))
        base_ref[j] = added([skip * product] + [w * h for w, h in zip(spread, states)])
        return q0, q1, states

    start = (
        next_chunk(strided(q_ref, run - 1, run)),
        next_chunk(strided(q_ref, run - 2, run)),
        tuple(jnp.zeros((CHUNKS, LANES), F32) for _ in range(modes)),
    )
    lax.fori_loop(0, run, step, start, unroll=4)
    top = sublane_index() == 0
    base_gain = (skip_ref[...] * first - early, skip_ref[...] * second)
    for j in range(2):
        gate_ref[j] = gate_ref[j] + jnp.where(top, over_sublanes(gain[j] * inside), 0.0)
        base_ref[j] = base_ref[j] + jnp.where(top, over_sublanes(base_gain[j]), 0.0)

    behind = sublane_index().astype(F32) * float(run)
    for m in range(modes):
        rate = over_sublanes(rates[m : m + 1, :])
        fade = jnp.exp(-rate * behind)
        begin_ref[m] = spread[m] * (state_ref[m] + fade * over_sublanes(arrived[m : m + 1, :]))
        reach_ref[m] = spread[m] * fade * jnp.exp(-rate * (inside * float(positions)))
        factor_ref[m] = factors[m]
    length = PAIR * positions
    for e in range(pairs):
        distance = (jnp.maximum(pair - 1 - e, 0) * length).astype(F32)
        weight_ref[e] = jnp.where(e < pair, jnp.exp(-rates * distance), 0.0)
        distance = (jnp.maximum(pair - e, 0) * length - 1).astype(F32)
        late_ref[e] = jnp.where(e <= pair, jnp.exp(-rates * distance), 0.0)


def carry_kernel(
    modes, axis, received_ref, gate_ref, base_ref, begin_ref, reach_ref, factor_ref, weight_ref, late_ref,
    taps_ref, decays_ref, residues_ref, skip_ref, power_ref, gated_ref, rows_ref, first_ref, second_ref,
):
    run = gate_ref.shape[0]
    pairs = received_ref.shape[0]
    device = lax.axis_index(axis)
    pair = device // PAIR
    lower = 1.0 - lax.rem(device, PAIR).astype(F32)
    pitch = modes + EXTRA
    rows_ref[0:pitch, :] = jnp.zeros((pitch, LANES), F32)
    for e in range(pairs):
        rows_ref[pitch * (e + 1) : pitch * (e + 2), :] = received_ref[e].astype(F32)

    def of_all(row, block):
        return tuple(rows_ref[pl.ds(pitch * block + modes + row + i, pairs, stride=pitch), :] for i in range(2))

    last = [of_all(row, 0) for row in (K_LAST, V_LAST)]
    begun = [of_all(row, 1) for row in (K_FIRST, V_FIRST)]
    first_ref[...], second_ref[...] = boundary(taps_ref, last, begun)

    rates = decays_ref[...]
    states, firsts, seconds = [], [], []
    for e in range(pairs):
        states.append(weight_ref[e] * rows_ref[pitch * (e + 1) : pitch * (e + 1) + modes, :])
        firsts.append(late_ref[e] * first_ref[e : e + 1, :])
        seconds.append(late_ref[e] * second_ref[e : e + 1, :])
    state = added(states) + added(firsts) + jnp.exp(rates) * added(seconds)

    first = first_ref[pl.ds(pair, 1), :] * lower
    second = second_ref[pl.ds(pair, 1), :] * lower
    weights = residues_ref[...] * jnp.sqrt(2.0 * rates)
    early = jnp.sum(weights * jnp.exp(rates), 0, keepdims=True) * second
    edge = [rows_ref[pl.ds(pair * pitch + modes + Q_LAST + i, 1), :] * lower for i in range(2)]
    gate_extra = gate_gain(taps_ref, *edge)
    skip = skip_ref[...]
    base_extra = (skip * first - early, skip * second)
    top = sublane_index() == 0
    factors = [factor_ref[m] for m in range(modes)]
    carried = [begin_ref[m] + reach_ref[m] * over_sublanes(state[m : m + 1, :]) for m in range(modes)]

    def step(j, carried, gate_more=None, base_more=None):
        carried = tuple(a * g for a, g in zip(factors, carried))
        gate, base = gate_ref[j], base_ref[j]
        if gate_more is not None:
            gate = gate + jnp.where(top, over_sublanes(gate_more), 0.0)
            base = base + jnp.where(top, over_sublanes(base_more), 0.0)
        gated_ref[pl.ds(j, CHUNKS, stride=run), :] = gate * added([base] + list(carried))
        return carried

    carried = tuple(carried)
    for j in range(2):
        carried = step(j, carried, gate_extra[j], base_extra[j])
    lax.fori_loop(2, run, step, carried, unroll=6)

    gated = gated_ref[...]
    square = gated * gated
    high = square.astype(BF16)
    low = (square - high.astype(F32)).astype(BF16)
    ones = jnp.ones((LANES, LANES), BF16)
    sums = jnp.dot(high, ones, preferred_element_type=F32) + jnp.dot(low, ones, preferred_element_type=F32)
    lane = lax.broadcasted_iota(jnp.int32, (CHUNKS, LANES), 1)
    power = jnp.zeros((CHUNKS, LANES), F32)
    for i in range(run):
        power = jnp.where(lane == i, sums[i * CHUNKS : (i + 1) * CHUNKS, :], power)
    power_ref[...] = jnp.broadcast_to(power[None], power_ref.shape)


def finish_kernel(channels, power_ref, gated_ref, gain_ref, mixed_ref):
    run = gated_ref.shape[0] // CHUNKS
    inverse = lax.rsqrt(jnp.sum(power_ref[...], 0) / channels + 1e-05)
    gain = over_sublanes(gain_ref[...])
    for i in range(0, run, 2):
        halves = [
            gated_ref[(i + h) * CHUNKS : (i + h + 1) * CHUNKS, :] * gain * inverse[:, i + h : i + h + 1] for h in range(2)
        ]
        mixed_ref[i * CHUNKS : (i + 2) * CHUNKS, :] = jnp.concatenate(halves, 0).astype(BF16)


def per_device(projections, short_filter, residues, decays, skip, gain):
    positions, _, width = projections.shape
    modes = decays.shape[0]
    ctx_count = lax.axis_size("ctx")
    tp_count = lax.axis_size("tp")
    pairs = ctx_count // PAIR
    run = positions // CHUNKS
    x = jnp.swapaxes(projections, 0, 1)

    def shape(*extent, kind=F32):
        return jax.ShapeDtypeStruct(extent, kind)

    def call(kernel, name, out_shape, in_specs, scratch, *operands):
        return pl.pallas_call(
            kernel,
            out_shape=out_shape,
            in_specs=in_specs,
            out_specs=jax.tree.map(lambda _: VMEM, out_shape),
            scratch_shapes=scratch,
            compiler_params=pltpu.CompilerParams(vmem_limit_bytes=VMEM_LIMIT),
            name=name,
        )(*operands)

    block = shape(run, CHUNKS, width)
    table = shape(modes, CHUNKS, width)
    sources = (x, short_filter, decays, residues, skip[None, :], gain[None, :])
    rows, product, state, q, short_filter, decays, residues, skip, gain = call(
        functools.partial(states_kernel, modes),
        "states",
        (shape(modes + EXTRA, width), block, table, shape(positions, width, kind=BF16))
        + tuple(shape(*s.shape) for s in sources[1:]),
        [ANY] * 6,
        [
            pltpu.VMEM((positions, width), BF16),
            pltpu.VMEM((positions, width), BF16),
            pltpu.VMEM((positions, width), F32),
            pltpu.VMEM((positions, width), F32),
            pltpu.SemaphoreType.DMA((8,)),
        ],
        *sources,
    )
    other = lax.ppermute(rows, "ctx", [(i, i + 1 - 2 * (i % PAIR)) for i in range(ctx_count)])
    sent, joined = call(
        functools.partial(join_kernel, modes, positions, "ctx"),
        "join",
        (shape(pairs, modes + EXTRA, width, kind=BF16), shape(PAIR, modes + EXTRA, width)),
        [VMEM] * 4,
        [],
        rows,
        other,
        short_filter,
        decays,
    )
    groups = [[PAIR * i + h for i in range(pairs)] for h in range(PAIR)]
    received = lax.all_to_all(sent, "ctx", split_axis=0, concat_axis=0, tiled=True, axis_index_groups=groups)

    gate, base, begin, reach, factor, weight, late = call(
        functools.partial(local_kernel, modes, "ctx", pairs),
        "local",
        (block, block, table, table, table, shape(pairs, modes, width), shape(pairs, modes, width)),
        [VMEM] * 8,
        [pltpu.VMEM((positions, width), F32)],
        q,
        product,
        state,
        joined,
        short_filter,
        decays,
        residues,
        skip,
    )
    power, gated = call(
        functools.partial(carry_kernel, modes, "ctx"),
        "carry",
        (shape(tp_count, CHUNKS, run), shape(positions, width)),
        [VMEM] * 12,
        [
            pltpu.VMEM(((pairs + 1) * (modes + EXTRA), width), F32),
            pltpu.VMEM((pairs, width), F32),
            pltpu.VMEM((pairs, width), F32),
        ],
        received,
        gate,
        base,
        begin,
        reach,
        factor,
        weight,
        late,
        short_filter,
        decays,
        residues,
        skip,
    )
    powers = lax.all_to_all(power, "tp", split_axis=0, concat_axis=0, tiled=True)
    return call(
        functools.partial(finish_kernel, width * tp_count),
        "finish",
        shape(positions, width, kind=BF16),
        [VMEM] * 3,
        [],
        powers,
        gated,
        gain,
    )


def solution(mesh):
    in_specs = (
        P("ctx", None, "tp"),
        P(None, None, "tp"),
        P(None, "tp"),
        P(None, "tp"),
        P("tp"),
        P("tp"),
    )
    return jax.shard_map(per_device, mesh=mesh, in_specs=in_specs, out_specs=P("ctx", "tp"), check_vma=False)
```

time: 45.3 us -> 42.1 us (0.929)
  the two profiles are of different devices: /device:TPU:1 before, /device:TPU:2 now
where the time goes in v2:
time: 42.1 us; the launch traced here: 41.7 us
  starting transfers between devices  11.3 us (27%)
  waiting for transfers between devices  10.2 us (24%)
  blocking collectives  9.97 us (24%)
  Pallas kernels  6.32 us (15%)
  local copies, waits for them, and re-layouts  3.89 us (9%)
    all_to_all x1, starting transfers between devices, per_device(): lax.all_to_all(sent, 'ctx', split_axis=0, concat_axis=0, tiled=True, axis...  11.2 us
    all_to_all x1, blocking collectives, per_device(): lax.all_to_all(power, 'tp', split_axis=0, concat_axis=0, tiled=True)  9.97 us
    all_to_all x1, waiting for transfers between devices, per_device(): lax.all_to_all(sent, 'ctx', split_axis=0, concat_axis=0, tiled=True, axis...  9.05 us
    pallas_call x5, Pallas kernels, call(): pl.pallas_call(kernel, out_shape=out_shape, in_specs=in_specs, out_specs=...  6.32 us
    unnamed x12, local copies, waits for them, and re-layouts  3.89 us
    ppermute x1, waiting for transfers between devices, per_device(): lax.ppermute(rows, 'ctx', [(i, i + 1 - 2 * (i % PAIR)) for i in range(ctx...  1.17 us
  transfers between devices with their start and end apart: 2, of which 2 were waited for; matrix products, arithmetic and copies ran while one was open for 0% of the time, Pallas kernels for 5%

profile of v2, /device:TPU:2, one launch (start us, length us, event | category | flops | bytes accessed | tf_op | source)
XLA Modules:
  0.0 41.7 jit_solution(12321029841653792966)
XLA Ops:
  0.0 0.0 copy-start.4
  0.0 0.0 copy-start.5
  0.0 0.7 %copy-done.4 = f32[128]{0:T(128)S(1)} copy-done((f32[128]{0:T(128)S(1)}, f32[128]{0:T(128)}, u32[]{:S(2)}) %copy-start.4) | copy-done | bytes 536
  0.7 0.0 copy-done.5
  0.7 0.0 copy-start
  0.7 1.1 %copy-done = bf16[1024,3,128]{2,0,1:T(8,128)(2,1)S(1)} copy-done((bf16[1024,3,128]{2,0,1:T(8,128)(2,1)S(1)}, bf16[1024,3,128]{2,0,1:T(8,128)(2,1)}, u32[]{:S(2)}) %copy-start) | copy-done | bytes 786456
  1.8 0.0 copy-start.1
  1.8 0.7 %copy-done.1 = f32[16,128]{1,0:T(8,128)S(1)} copy-done((f32[16,128]{1,0:T(8,128)S(1)}, f32[16,128]{1,0:T(8,128)}, u32[]{:S(2)}) %copy-start.1) | copy-done | bytes 8216
  2.5 0.0 copy-start.2
  2.5 0.7 %copy-done.2 = f32[16,128]{1,0:T(8,128)S(1)} copy-done((f32[16,128]{1,0:T(8,128)S(1)}, f32[16,128]{1,0:T(8,128)}, u32[]{:S(2)}) %copy-start.2) | copy-done | bytes 8216
  3.2 0.0 copy-start.3
  3.2 0.7 %copy-done.3 = f32[3,3,128]{2,1,0:T(4,128)S(1)} copy-done((f32[3,3,128]{2,1,0:T(4,128)S(1)}, f32[3,3,128]{2,1,0:T(4,128)}, u32[]{:S(2)}) %copy-start.3) | copy-done | bytes 4632
  3.9 1.6 %states.1 = (f32[32,128]{1,0:T(8,128)S(1)}, f32[128,8,128]{2,1,0:T(8,128)S(1)}, f32[16,8,128]{2,1,0:T(8,128)S(1)}, bf16[1024,128]{1,0:T(8,128)(2,1)S(1)}, f32[3,...) custom-call(bf16[3,1024,128]{2,1,0:T(8,128)(2,1)S(1)} %bitcast.3, ...), custom_call_target="tpu_custom_call" | custom-call | tf_op jit(solution)/shard_map/states/pallas_call | solution.py:307
  5.5 0.1 collective-permute-start
  5.6 1.2 %collective-permute-done.other_ref = f32[32,128]{1,0:T(8,128)S(1)} collective-permute-done((f32[32,128]{1,0:T(8,128)S(1)}, f32[32,128]{1,0:T(8,128)S(1)}, u32[]{:S(2)}, u32[]{:S(2)}) %collective-permute-start) | collective-permute-done | bytes 16416 | tf_op jit(solution)/shard_map/ppermute | solution.py:335
  6.7 0.7 %join.1 = (bf16[16,32,128]{2,1,0:T(8,128)(2,1)}, f32[2,32,128]{2,1,0:T(8,128)S(1)}) custom-call(f32[32,128]{1,0:T(8,128)S(1)} %get-tuple-element.25.own_ref, f32[32,128]{1,0:T(8,128)S(1)} %collective-permute-done.other_ref, f32[3,3,128]{2,1,0:T(4,128)S(1)} %get-tuple-element.26.taps_ref, f32[16,128]{1,0:T(8,128)S(1)} %get-tuple-element.27.decays_ref), custom_call_target="tpu_custom_call" | custom-call | tf_op jit(solution)/shard_map/join/pallas_call | solution.py:307
  7.4 11.2 %all-to-all-start = ((bf16[16,32,128]{2,1,0:T(8,128)(2,1)}), bf16[16,32,128]{2,1,0:T(8,128)(2,1)S(1)}, u32[]{:S(2)}, u32[]{:S(2)}) async-start(bf16[16,32,128]{2,1,0:T(8,128)(2,1)} %get-tuple-element.28), calls=%async_computation | async-start | bytes 262144 | tf_op jit(solution)/shard_map/all_to_all | solution.py:348
  18.6 1.9 %local.1 = (f32[128,8,128]{2,1,0:T(8,128)S(1)}, f32[128,8,128]{2,1,0:T(8,128)S(1)}, f32[16,8,128]{2,1,0:T(8,128)S(1)}, f32[16,8,128]{2,1,0:T(8,128)S(1)}, f32[16...) custom-call(bf16[1024,128]{1,0:T(8,128)(2,1)S(1)} %get-tuple-element.29.q_half, ...), custom_call_target="tpu_custom_call" | custom-call | tf_op jit(solution)/shard_map/local/pallas_call | solution.py:307
  20.6 9.1 %all-to-all-done.received_ref = bf16[16,32,128]{2,1,0:T(8,128)(2,1)S(1)} async-done(((bf16[16,32,128]{2,1,0:T(8,128)(2,1)}), bf16[16,32,128]{2,1,0:T(8,128)(2,1)S(1)}, u32[]{:S(2)}, u32[]{:S(2)}) %all-to-all-start) | async-done | bytes 131104 | tf_op jit(solution)/shard_map/all_to_all | solution.py:348
  29.6 1.1 %carry.1 = (f32[8,8,128]{2,1,0:T(8,128)S(1)}, f32[1024,128]{1,0:T(8,128)S(1)}) custom-call(bf16[16,32,128]{2,1,0:T(8,128)(2,1)S(1)} %all-to-all-done.received_ref, f32[128,8,128]{2,1,0:T(8,128)S(1)} %get-tuple-element.35.gate_ref, f32[128,8,128]{2,1,0:T(8,128)S(1)} %get-tuple-element.36.base_ref, f32[16,8,128]{2,1,0:T(8,128)S(1)} %get-tuple-element.37.begin_ref, ...), custom_call_target="tpu_custom_call" | custom-call | tf_op jit(solution)/shard_map/carry/pallas_call | solution.py:307
  30.8 10.0 %all_to_all.10.power_ref = f32[8,8,128]{2,1,0:T(8,128)S(1)} all-to-all(f32[8,8,128]{2,1,0:T(8,128)S(1)} %get-tuple-element.42), channel_id=1, replica_groups=mesh['ctx'=32,'tp'=8] {'tp'}, dimensions={0} | all-to-all | bytes 65536 | tf_op jit(solution)/shard_map/all_to_all | solution.py:388
  40.7 1.0 %finish.1 = bf16[1024,128]{1,0:T(8,128)(2,1)} custom-call(f32[8,8,128]{2,1,0:T(8,128)S(1)} %all_to_all.10.power_ref, f32[1024,128]{1,0:T(8,128)S(1)} %get-tuple-element.43.gated_ref, f32[1,128]{1,0:T(1,128)S(1)} %get-tuple-element.44.gain_ref), custom_call_target="tpu_custom_call" | custom-call | tf_op jit(solution)/shard_map/finish/pallas_call | solution.py:307
Async XLA Ops:
  0.0 0.7 %copy-start.4 = (f32[128]{0:T(128)S(1)}, f32[128]{0:T(128)}, u32[]{:S(2)}) copy-start(f32[128]{0:T(128)} %param.10) | copy-start | bytes 1540
  0.0 0.7 %copy-start.5 = (f32[128]{0:T(128)S(1)}, f32[128]{0:T(128)}, u32[]{:S(2)}) copy-start(f32[128]{0:T(128)} %param.11) | copy-start | bytes 1540
  0.7 1.1 %copy-start = (bf16[1024,3,128]{2,0,1:T(8,128)(2,1)S(1)}, bf16[1024,3,128]{2,0,1:T(8,128)(2,1)}, u32[]{:S(2)}) copy-start(bf16[1024,3,128]{2,0,1:T(8,128)(2,1)} %param.6) | copy-start | bytes 2359300
  1.8 0.7 %copy-start.1 = (f32[16,128]{1,0:T(8,128)S(1)}, f32[16,128]{1,0:T(8,128)}, u32[]{:S(2)}) copy-start(f32[16,128]{1,0:T(8,128)} %refs_2_.1) | copy-start | bytes 24580
  2.5 0.7 %copy-start.2 = (f32[16,128]{1,0:T(8,128)S(1)}, f32[16,128]{1,0:T(8,128)}, u32[]{:S(2)}) copy-start(f32[16,128]{1,0:T(8,128)} %refs_3_.1) | copy-start | bytes 24580
  3.2 0.7 %copy-start.3 = (f32[3,3,128]{2,1,0:T(4,128)S(1)}, f32[3,3,128]{2,1,0:T(4,128)}, u32[]{:S(2)}) copy-start(f32[3,3,128]{2,1,0:T(4,128)} %refs_1_.1) | copy-start | bytes 13828
  5.5 1.3 %collective-permute-start = (f32[32,128]{1,0:T(8,128)S(1)}, f32[32,128]{1,0:T(8,128)S(1)}, u32[]{:S(2)}, u32[]{:S(2)}) collective-permute-start(f32[32,128]{1,0:T(8,128)S(1)} %get-tuple-element.25.own_ref), channel_id=1, source_target_pairs={{0,8},{8,0},{16,24},{24,16},{32,40},{40,32},{48,56},{56,48},{64,72... | collective-permute-start | bytes 49160 | tf_op jit(solution)/shard_map/ppermute | solution.py:335
  7.4 22.2 %all-to-all-start = ((bf16[16,32,128]{2,1,0:T(8,128)(2,1)}), bf16[16,32,128]{2,1,0:T(8,128)(2,1)S(1)}, u32[]{:S(2)}, u32[]{:S(2)}) async-start(bf16[16,32,128]{2,1,0:T(8,128)(2,1)} %get-tuple-element.28), calls=%async_computation | async-start | bytes 262144 | tf_op jit(solution)/shard_map/all_to_all | solution.py:348

commit v3 on v2

--- a/solution.py
+++ b/solution.py
@@ -330,7 +330,7 @@
             pltpu.VMEM((positions, width), F32),
             pltpu.SemaphoreType.DMA((8,)),
         ],
-        *sources,
+        *[pltpu.with_memory_space_constraint(s, pltpu.HBM) for s in sources],
     )
     other = lax.ppermute(rows, "ctx", [(i, i + 1 - 2 * (i % PAIR)) for i in range(ctx_count)])
     sent, joined = call(

time: 42.1 us -> 39 us (0.926)
  local copies, waits for them, and re-layouts: 3.89 us -> 0 us
  Pallas kernels: 6.32 us -> 7.22 us
    unnamed x12 -> x0, local copies, waits for them, and re-layouts: 3.89 us -> none
    pallas_call x5, Pallas kernels: 6.32 us -> 7.22 us  [call(): pl.pallas_call(kernel, out_shape=out_shape, in_specs=in_specs, out_specs=...]
where the time goes in v3:
time: 39 us; the launch traced here: 38.7 us
  starting transfers between devices  11.3 us (29%)
  waiting for transfers between devices  10.2 us (26%)
  blocking collectives  9.97 us (26%)
  Pallas kernels  7.22 us (19%)
    all_to_all x1, starting transfers between devices, per_device(): lax.all_to_all(sent, 'ctx', split_axis=0, concat_axis=0, tiled=True, axis...  11.2 us
    all_to_all x1, blocking collectives, per_device(): lax.all_to_all(power, 'tp', split_axis=0, concat_axis=0, tiled=True)  9.97 us
    all_to_all x1, waiting for transfers between devices, per_device(): lax.all_to_all(sent, 'ctx', split_axis=0, concat_axis=0, tiled=True, axis...  9.05 us
    pallas_call x5, Pallas kernels, call(): pl.pallas_call(kernel, out_shape=out_shape, in_specs=in_specs, out_specs=...  7.22 us
    ppermute x1, waiting for transfers between devices, per_device(): lax.ppermute(rows, 'ctx', [(i, i + 1 - 2 * (i % PAIR)) for i in range(ctx...  1.17 us
  transfers between devices with their start and end apart: 2, of which 2 were waited for; matrix products, arithmetic and copies ran while one was open for 0% of the time, Pallas kernels for 5%

profile of v3, /device:TPU:2, one launch (start us, length us, event | category | flops | bytes accessed | tf_op | source)
XLA Modules:
  0.0 38.7 jit_solution(5170066479223651802)
XLA Ops:
  0.0 2.5 %states.1 = (f32[32,128]{1,0:T(8,128)S(1)}, f32[128,8,128]{2,1,0:T(8,128)S(1)}, f32[16,8,128]{2,1,0:T(8,128)S(1)}, bf16[1024,128]{1,0:T(8,128)(2,1)S(1)}, f32[3,...) custom-call(bf16[3,1024,128]{2,1,0:T(8,128)(2,1)} %bitcast.3, ...), custom_call_target="tpu_custom_call" | custom-call | tf_op jit(solution)/shard_map/states/pallas_call | solution.py:307
  2.5 0.1 collective-permute-start
  2.6 1.2 %collective-permute-done.other_ref = f32[32,128]{1,0:T(8,128)S(1)} collective-permute-done((f32[32,128]{1,0:T(8,128)S(1)}, f32[32,128]{1,0:T(8,128)S(1)}, u32[]{:S(2)}, u32[]{:S(2)}) %collective-permute-start) | collective-permute-done | bytes 16416 | tf_op jit(solution)/shard_map/ppermute | solution.py:335
  3.7 0.7 %join.1 = (bf16[16,32,128]{2,1,0:T(8,128)(2,1)}, f32[2,32,128]{2,1,0:T(8,128)S(1)}) custom-call(f32[32,128]{1,0:T(8,128)S(1)} %get-tuple-element.25.own_ref, f32[32,128]{1,0:T(8,128)S(1)} %collective-permute-done.other_ref, f32[3,3,128]{2,1,0:T(4,128)S(1)} %get-tuple-element.26.taps_ref, f32[16,128]{1,0:T(8,128)S(1)} %get-tuple-element.27.decays_ref), custom_call_target="tpu_custom_call" | custom-call | tf_op jit(solution)/shard_map/join/pallas_call | solution.py:307
  4.4 11.2 %all-to-all-start = ((bf16[16,32,128]{2,1,0:T(8,128)(2,1)}), bf16[16,32,128]{2,1,0:T(8,128)(2,1)S(1)}, u32[]{:S(2)}, u32[]{:S(2)}) async-start(bf16[16,32,128]{2,1,0:T(8,128)(2,1)} %get-tuple-element.28), calls=%async_computation | async-start | bytes 262144 | tf_op jit(solution)/shard_map/all_to_all | solution.py:348
  15.6 1.9 %local.1 = (f32[128,8,128]{2,1,0:T(8,128)S(1)}, f32[128,8,128]{2,1,0:T(8,128)S(1)}, f32[16,8,128]{2,1,0:T(8,128)S(1)}, f32[16,8,128]{2,1,0:T(8,128)S(1)}, f32[16...) custom-call(bf16[1024,128]{1,0:T(8,128)(2,1)S(1)} %get-tuple-element.29.q_half, ...), custom_call_target="tpu_custom_call" | custom-call | tf_op jit(solution)/shard_map/local/pallas_call | solution.py:307
  17.6 9.1 %all-to-all-done.received_ref = bf16[16,32,128]{2,1,0:T(8,128)(2,1)S(1)} async-done(((bf16[16,32,128]{2,1,0:T(8,128)(2,1)}), bf16[16,32,128]{2,1,0:T(8,128)(2,1)S(1)}, u32[]{:S(2)}, u32[]{:S(2)}) %all-to-all-start) | async-done | bytes 131104 | tf_op jit(solution)/shard_map/all_to_all | solution.py:348
  26.6 1.1 %carry.1 = (f32[8,8,128]{2,1,0:T(8,128)S(1)}, f32[1024,128]{1,0:T(8,128)S(1)}) custom-call(bf16[16,32,128]{2,1,0:T(8,128)(2,1)S(1)} %all-to-all-done.received_ref, f32[128,8,128]{2,1,0:T(8,128)S(1)} %get-tuple-element.35.gate_ref, f32[128,8,128]{2,1,0:T(8,128)S(1)} %get-tuple-element.36.base_ref, f32[16,8,128]{2,1,0:T(8,128)S(1)} %get-tuple-element.37.begin_ref, ...), custom_call_target="tpu_custom_call" | custom-call | tf_op jit(solution)/shard_map/carry/pallas_call | solution.py:307
  27.8 10.0 %all_to_all.10.power_ref = f32[8,8,128]{2,1,0:T(8,128)S(1)} all-to-all(f32[8,8,128]{2,1,0:T(8,128)S(1)} %get-tuple-element.42), channel_id=1, replica_groups=mesh['ctx'=32,'tp'=8] {'tp'}, dimensions={0} | all-to-all | bytes 65536 | tf_op jit(solution)/shard_map/all_to_all | solution.py:388
  37.7 1.0 %finish.1 = bf16[1024,128]{1,0:T(8,128)(2,1)} custom-call(f32[8,8,128]{2,1,0:T(8,128)S(1)} %all_to_all.10.power_ref, f32[1024,128]{1,0:T(8,128)S(1)} %get-tuple-element.43.gated_ref, f32[1,128]{1,0:T(1,128)S(1)} %get-tuple-element.44.gain_ref), custom_call_target="tpu_custom_call" | custom-call | tf_op jit(solution)/shard_map/finish/pallas_call | solution.py:307
Async XLA Ops:
  2.5 1.3 %collective-permute-start = (f32[32,128]{1,0:T(8,128)S(1)}, f32[32,128]{1,0:T(8,128)S(1)}, u32[]{:S(2)}, u32[]{:S(2)}) collective-permute-start(f32[32,128]{1,0:T(8,128)S(1)} %get-tuple-element.25.own_ref), channel_id=1, source_target_pairs={{0,8},{8,0},{16,24},{24,16},{32,40},{40,32},{48,56},{56,48},{64,72... | collective-permute-start | bytes 49160 | tf_op jit(solution)/shard_map/ppermute | solution.py:335
  4.4 22.2 %all-to-all-start = ((bf16[16,32,128]{2,1,0:T(8,128)(2,1)}), bf16[16,32,128]{2,1,0:T(8,128)(2,1)S(1)}, u32[]{:S(2)}, u32[]{:S(2)}) async-start(bf16[16,32,128]{2,1,0:T(8,128)(2,1)} %get-tuple-element.28), calls=%async_computation | async-start | bytes 262144 | tf_op jit(solution)/shard_map/all_to_all | solution.py:348

commit v4 on v3

--- a/solution.py
+++ b/solution.py
@@ -16,8 +16,31 @@
 VMEM = pl.BlockSpec(memory_space=pltpu.VMEM)
 ANY = pl.BlockSpec(memory_space=pl.ANY)
 
+FIRST_PAIR = 10
+FIRST_SLICE = 5
+GRID = 4
+
 K_LAST, V_LAST, Q_LAST, K_FIRST, V_FIRST = 0, 2, 4, 6, 8
 EXTRA = 16
+
+
+def first_then(first, members, distance):
+    return [first] + sorted((i for i in range(members) if i != first), key=lambda i: -distance(i, first))
+
+
+def around(a, b, size):
+    return min((a - b) % size, (b - a) % size)
+
+
+def pair_order(pairs):
+    def distance(a, b):
+        return around(a // GRID, b // GRID, max(pairs // GRID, 1)) + 2 * around(a % GRID, b % GRID, GRID)
+
+    return first_then(FIRST_PAIR % pairs, pairs, distance)
+
+
+def slice_order(slices):
+    return first_then(FIRST_SLICE % slices, slices, lambda a, b: 0)
 
 
 def over_sublanes(row):
@@ -223,8 +246,8 @@
     lower = 1.0 - lax.rem(device, PAIR).astype(F32)
     pitch = modes + EXTRA
     rows_ref[0:pitch, :] = jnp.zeros((pitch, LANES), F32)
-    for e in range(pairs):
-        rows_ref[pitch * (e + 1) : pitch * (e + 2), :] = received_ref[e].astype(F32)
+    for slot, e in enumerate(pair_order(pairs)):
+        rows_ref[pitch * (e + 1) : pitch * (e + 2), :] = received_ref[slot].astype(F32)
 
     def of_all(row, block):
         return tuple(rows_ref[pl.ds(pitch * block + modes + row + i, pairs, stride=pitch), :] for i in range(2))
@@ -344,7 +367,7 @@
         short_filter,
         decays,
     )
-    groups = [[PAIR * i + h for i in range(pairs)] for h in range(PAIR)]
+    groups = [[PAIR * i + h for i in pair_order(pairs)] for h in range(PAIR)]
     received = lax.all_to_all(sent, "ctx", split_axis=0, concat_axis=0, tiled=True, axis_index_groups=groups)
 
     gate, base, begin, reach, factor, weight, late = call(
@@ -385,7 +408,9 @@
         residues,
         skip,
     )
-    powers = lax.all_to_all(power, "tp", split_axis=0, concat_axis=0, tiled=True)
+    powers = lax.all_to_all(
+        power, "tp", split_axis=0, concat_axis=0, tiled=True, axis_index_groups=[slice_order(tp_count)]
+    )
     return call(
         functools.partial(finish_kernel, width * tp_count),
         "finish",

time: 39 us -> 32.3 us (0.83)
  waiting for transfers between devices: 10.2 us -> 2.74 us
  starting transfers between devices: 11.3 us -> 13.4 us
  blocking collectives: 9.97 us -> 8.65 us
    all_to_all x1, waiting for transfers between devices: 9.05 us -> 1.57 us  [per_device(): lax.all_to_all(sent, 'ctx', split_axis=0, concat_axis=0, tiled=True, axis...]
    all_to_all x1, starting transfers between devices: 11.2 us -> 13.3 us  [per_device(): lax.all_to_all(sent, 'ctx', split_axis=0, concat_axis=0, tiled=True, axis...]
    all_to_all x1, blocking collectives: 9.97 us -> 8.65 us  [per_device(): lax.all_to_all(power, 'tp', split_axis=0, concat_axis=0, tiled=True, axis...]
  transfers between devices with their start and end apart: 2 -> 2, of which waited for: 2 -> 2; matrix products, arithmetic and copies ran while one was open for 0% -> 0% of each run, Pallas kernels for 5% -> 6%
where the time goes in v4:
time: 32.3 us; the launch traced here: 32 us
  starting transfers between devices  13.4 us (41%)
  blocking collectives  8.65 us (27%)
  Pallas kernels  7.21 us (22%)
  waiting for transfers between devices  2.74 us (8%)
    all_to_all x1, starting transfers between devices, per_device(): lax.all_to_all(sent, 'ctx', split_axis=0, concat_axis=0, tiled=True, axis...  13.3 us
    all_to_all x1, blocking collectives, per_device(): lax.all_to_all(power, 'tp', split_axis=0, concat_axis=0, tiled=True, axis...  8.65 us
    pallas_call x5, Pallas kernels, call(): pl.pallas_call(kernel, out_shape=out_shape, in_specs=in_specs, out_specs=...  7.21 us
    all_to_all x1, waiting for transfers between devices, per_device(): lax.all_to_all(sent, 'ctx', split_axis=0, concat_axis=0, tiled=True, axis...  1.57 us
    ppermute x1, waiting for transfers between devices, per_device(): lax.ppermute(rows, 'ctx', [(i, i + 1 - 2 * (i % PAIR)) for i in range(ctx...  1.17 us
  transfers between devices with their start and end apart: 2, of which 2 were waited for; matrix products, arithmetic and copies ran while one was open for 0% of the time, Pallas kernels for 6%

profile of v4, /device:TPU:2, one launch (start us, length us, event | category | flops | bytes accessed | tf_op | source)
XLA Modules:
  0.0 32.0 jit_solution(981399863925998670)
XLA Ops:
  0.0 2.5 %states.1 = (f32[32,128]{1,0:T(8,128)S(1)}, f32[128,8,128]{2,1,0:T(8,128)S(1)}, f32[16,8,128]{2,1,0:T(8,128)S(1)}, bf16[1024,128]{1,0:T(8,128)(2,1)S(1)}, f32[3,...) custom-call(bf16[3,1024,128]{2,1,0:T(8,128)(2,1)} %bitcast.3, ...), custom_call_target="tpu_custom_call" | custom-call | tf_op jit(solution)/shard_map/states/pallas_call | solution.py:330
  2.5 0.1 collective-permute-start
  2.6 1.2 %collective-permute-done.other_ref = f32[32,128]{1,0:T(8,128)S(1)} collective-permute-done((f32[32,128]{1,0:T(8,128)S(1)}, f32[32,128]{1,0:T(8,128)S(1)}, u32[]{:S(2)}, u32[]{:S(2)}) %collective-permute-start) | collective-permute-done | bytes 16416 | tf_op jit(solution)/shard_map/ppermute | solution.py:358
  3.7 0.7 %join.1 = (bf16[16,32,128]{2,1,0:T(8,128)(2,1)}, f32[2,32,128]{2,1,0:T(8,128)S(1)}) custom-call(f32[32,128]{1,0:T(8,128)S(1)} %get-tuple-element.25.own_ref, f32[32,128]{1,0:T(8,128)S(1)} %collective-permute-done.other_ref, f32[3,3,128]{2,1,0:T(4,128)S(1)} %get-tuple-element.26.taps_ref, f32[16,128]{1,0:T(8,128)S(1)} %get-tuple-element.27.decays_ref), custom_call_target="tpu_custom_call" | custom-call | tf_op jit(solution)/shard_map/join/pallas_call | solution.py:330
  4.4 13.3 %all-to-all-start = ((bf16[16,32,128]{2,1,0:T(8,128)(2,1)}), bf16[16,32,128]{2,1,0:T(8,128)(2,1)S(1)}, u32[]{:S(2)}, u32[]{:S(2)}) async-start(bf16[16,32,128]{2,1,0:T(8,128)(2,1)} %get-tuple-element.28), calls=%async_computation | async-start | bytes 262144 | tf_op jit(solution)/shard_map/all_to_all | solution.py:371
  17.7 1.9 %local.1 = (f32[128,8,128]{2,1,0:T(8,128)S(1)}, f32[128,8,128]{2,1,0:T(8,128)S(1)}, f32[16,8,128]{2,1,0:T(8,128)S(1)}, f32[16,8,128]{2,1,0:T(8,128)S(1)}, f32[16...) custom-call(bf16[1024,128]{1,0:T(8,128)(2,1)S(1)} %get-tuple-element.29.q_half, ...), custom_call_target="tpu_custom_call" | custom-call | tf_op jit(solution)/shard_map/local/pallas_call | solution.py:330
  19.6 1.6 %all-to-all-done.received_ref = bf16[16,32,128]{2,1,0:T(8,128)(2,1)S(1)} async-done(((bf16[16,32,128]{2,1,0:T(8,128)(2,1)}), bf16[16,32,128]{2,1,0:T(8,128)(2,1)S(1)}, u32[]{:S(2)}, u32[]{:S(2)}) %all-to-all-start) | async-done | bytes 131104 | tf_op jit(solution)/shard_map/all_to_all | solution.py:371
  21.2 1.1 %carry.1 = (f32[8,8,128]{2,1,0:T(8,128)S(1)}, f32[1024,128]{1,0:T(8,128)S(1)}) custom-call(bf16[16,32,128]{2,1,0:T(8,128)(2,1)S(1)} %all-to-all-done.received_ref, f32[128,8,128]{2,1,0:T(8,128)S(1)} %get-tuple-element.35.gate_ref, f32[128,8,128]{2,1,0:T(8,128)S(1)} %get-tuple-element.36.base_ref, f32[16,8,128]{2,1,0:T(8,128)S(1)} %get-tuple-element.37.begin_ref, ...), custom_call_target="tpu_custom_call" | custom-call | tf_op jit(solution)/shard_map/carry/pallas_call | solution.py:330
  22.4 8.6 %all_to_all.10.power_ref = f32[8,8,128]{2,1,0:T(8,128)S(1)} all-to-all(f32[8,8,128]{2,1,0:T(8,128)S(1)} %get-tuple-element.42), channel_id=1, replica_groups={{5,0,1,2,3,4,6,7},{13,8,9,10,11,12,14,15},{21,16,17,18,19,20,22,23},{29..., dimensions={0} | all-to-all | bytes 65536 | tf_op jit(solution)/shard_map/all_to_all | solution.py:411
  31.0 1.0 %finish.1 = bf16[1024,128]{1,0:T(8,128)(2,1)} custom-call(f32[8,8,128]{2,1,0:T(8,128)S(1)} %all_to_all.10.power_ref, f32[1024,128]{1,0:T(8,128)S(1)} %get-tuple-element.43.gated_ref, f32[1,128]{1,0:T(1,128)S(1)} %get-tuple-element.44.gain_ref), custom_call_target="tpu_custom_call" | custom-call | tf_op jit(solution)/shard_map/finish/pallas_call | solution.py:330
Async XLA Ops:
  2.5 1.3 %collective-permute-start = (f32[32,128]{1,0:T(8,128)S(1)}, f32[32,128]{1,0:T(8,128)S(1)}, u32[]{:S(2)}, u32[]{:S(2)}) collective-permute-start(f32[32,128]{1,0:T(8,128)S(1)} %get-tuple-element.25.own_ref), channel_id=1, source_target_pairs={{0,8},{8,0},{16,24},{24,16},{32,40},{40,32},{48,56},{56,48},{64,72... | collective-permute-start | bytes 49160 | tf_op jit(solution)/shard_map/ppermute | solution.py:358
  4.4 16.8 %all-to-all-start = ((bf16[16,32,128]{2,1,0:T(8,128)(2,1)}), bf16[16,32,128]{2,1,0:T(8,128)(2,1)S(1)}, u32[]{:S(2)}, u32[]{:S(2)}) async-start(bf16[16,32,128]{2,1,0:T(8,128)(2,1)} %get-tuple-element.28), calls=%async_computation | async-start | bytes 262144 | tf_op jit(solution)/shard_map/all_to_all | solution.py:371

commit v5 on v4

v5 whole, which is shorter than its diff:
```python
import functools

import jax
import jax.numpy as jnp
from jax import lax
from jax.experimental import pallas as pl
from jax.experimental.pallas import tpu as pltpu
from jax.sharding import PartitionSpec as P

F32 = jnp.float32
BF16 = jnp.bfloat16
CHUNKS = 8
LANES = 128
PAIR = 2
VMEM_LIMIT = 40 * 1024 * 1024
VMEM = pl.BlockSpec(memory_space=pltpu.VMEM)
ANY = pl.BlockSpec(memory_space=pl.ANY)

FIRST_PAIR = 10
FIRST_SLICE = 5
GRID = 4
PITCH = 137
SPAN = 136

K_LAST, V_LAST, Q_LAST, K_FIRST, V_FIRST = 0, 2, 4, 6, 8
EXTRA = 16


def first_then(first, members, distance):
    return [first] + sorted((i for i in range(members) if i != first), key=lambda i: -distance(i, first))


def around(a, b, size):
    return min((a - b) % size, (b - a) % size)


def pair_order(pairs):
    def distance(a, b):
        return around(a // GRID, b // GRID, max(pairs // GRID, 1)) + 2 * around(a % GRID, b % GRID, GRID)

    return first_then(FIRST_PAIR % pairs, pairs, distance)


def slice_order(slices):
    return first_then(FIRST_SLICE % slices, slices, lambda a, b: 0)


def over_sublanes(row):
    return jnp.broadcast_to(row, (CHUNKS, LANES))


def sublane_index():
    return lax.broadcasted_iota(jnp.int32, (CHUNKS, LANES), 0)


def next_chunk(block, distance=1):
    rolled = pltpu.roll(block, distance, 0)
    return jnp.where(sublane_index() >= distance, rolled, 0.0)


def strided(ref, step, run):
    return ref[pl.ds(step, CHUNKS, stride=run), :]


def added(terms):
    while len(terms) > 1:
        pairs = [terms[i] + terms[i + 1] for i in range(0, len(terms) - 1, 2)]
        terms = pairs + terms[2 * len(pairs) :]
    return terms[0]


def boundary(taps_ref, last, first):
    products = []
    for j in (1, 2):
        tap = [taps_ref[j, i : i + 1, :] for i in range(3)]
        (far, near), (zero, one) = last[j - 1], first[j - 1]
        own = (tap[0] * zero, tap[0] * one + tap[1] * zero)
        gained = (tap[1] * near + tap[2] * far, tap[2] * near)
        products.append((own, gained))
    (k_own, k_gained), (v_own, v_gained) = products
    return [k_own[i] * v_gained[i] + k_gained[i] * (v_own[i] + v_gained[i]) for i in range(2)]


def two_rows(ref, row):
    return ref[row : row + 1, :], ref[row + 1 : row + 2, :]


def pair_boundary(modes, taps_ref, lower_ref, upper_ref):
    last = [two_rows(lower_ref, modes + row) for row in (K_LAST, V_LAST)]
    first = [two_rows(upper_ref, modes + row) for row in (K_FIRST, V_FIRST)]
    return boundary(taps_ref, last, first)


def states_kernel(modes, *refs):
    sources, refs = refs[:6], refs[6:]
    x_hbm = sources[0]
    (rows_ref, product_ref, state_ref, q_ref), refs = refs[:4], refs[4:]
    params, refs = refs[:5], refs[5:]
    taps_ref, decays_ref = params[0], params[1]
    k_half, v_half, k_ref, v_ref, jump_ref, semaphores = refs
    copies = [pltpu.make_async_copy(s, d, semaphores.at[i]) for i, (s, d) in enumerate(zip(sources[1:], params))]
    streams = [
        pltpu.make_async_copy(x_hbm.at[j], d, semaphores.at[5 + j]) for j, d in enumerate((q_ref, k_half, v_half))
    ]
    for copy in (streams[1], streams[2], copies[1], copies[0], streams[0], copies[2], copies[3], copies[4]):
        copy.start()
    positions = q_ref.shape[0]
    run = positions // CHUNKS
    copies[1].wait()
    copies[0].wait()
    k_taps = [over_sublanes(taps_ref[1, i : i + 1, :]) for i in range(3)]
    v_taps = [over_sublanes(taps_ref[2, i : i + 1, :]) for i in range(3)]
    rates = decays_ref[...]
    factor = jnp.exp(-rates)
    factors = [over_sublanes(factor[m : m + 1, :]) for m in range(modes)]
    for i in range(3):
        jump_ref[i] = jnp.exp(-float(run << i) * rates)
    streams[1].wait()
    for s in range(CHUNKS):
        k_ref[s * PITCH : s * PITCH + run, :] = k_half[s * run : (s + 1) * run, :].astype(F32)
    streams[2].wait()
    for s in range(CHUNKS):
        v_ref[s * PITCH : s * PITCH + run, :] = v_half[s * run : (s + 1) * run, :].astype(F32)

    def step(j, carry):
        k1, k2, v1, v2, states = carry
        k0 = strided(k_ref, j, PITCH)
        v0 = strided(v_ref, j, PITCH)
        k = k_taps[0] * k0 + k_taps[1] * k1 + k_taps[2] * k2
        v = v_taps[0] * v0 + v_taps[1] * v1 + v_taps[2] * v2
        product = k * v
        product_ref[j] = product
        states = tuple(a * h + product for a, h in zip(factors, states))
        return k0, k1, v0, v1, states

    start = (
        next_chunk(strided(k_ref, run - 1, PITCH)),
        next_chunk(strided(k_ref, run - 2, PITCH)),
        next_chunk(strided(v_ref, run - 1, PITCH)),
        next_chunk(strided(v_ref, run - 2, PITCH)),
        tuple(jnp.zeros((CHUNKS, LANES), F32) for _ in range(modes)),
    )
    states = lax.fori_loop(0, run, step, start, unroll=16)[4]
    for m in range(modes):
        total = states[m]
        for i in range(3):
            total = total + over_sublanes(jump_ref[i, m : m + 1, :]) * next_chunk(total, 1 << i)
        state_ref[m] = next_chunk(total)
        rows_ref[m : m + 1, :] = total[CHUNKS - 1 : CHUNKS, :]
    streams[0].wait()
    rows_ref[modes + K_LAST : modes + K_LAST + 2, :] = k_ref[7 * PITCH + run - 2 : 7 * PITCH + run, :]
    rows_ref[modes + V_LAST : modes + V_LAST + 2, :] = v_ref[7 * PITCH + run - 2 : 7 * PITCH + run, :]
    rows_ref[modes + Q_LAST : modes + Q_LAST + 2, :] = q_ref[positions - 16 : positions, :].astype(F32)[14:16]
    rows_ref[modes + K_FIRST : modes + K_FIRST + 2, :] = k_ref[0:2, :]
    rows_ref[modes + V_FIRST : modes + V_FIRST + 2, :] = v_ref[0:2, :]
    rows_ref[modes + V_FIRST + 2 :, :] = jnp.zeros((EXTRA - V_FIRST - 2, LANES), F32)
    for i in (2, 3, 4):
        copies[i].wait()


def starts_early(axis):
    pair = lax.axis_index(axis) // PAIR
    y, z = pair // GRID, lax.rem(pair, GRID)
    return jnp.logical_or(z < 1, jnp.logical_and(z < 2, y < 2))


def mode_weights(decays_ref, residues_ref):
    return residues_ref[...] * jnp.sqrt(2.0 * decays_ref[...])


def edge_gains(taps_ref, skip_ref, rates, weights, first, second, far, near):
    early = jnp.sum(weights * jnp.exp(rates), 0, keepdims=True) * second
    skip = skip_ref[...]
    gate = (taps_ref[0, 1:2, :] * near + taps_ref[0, 2:3, :] * far, taps_ref[0, 2:3, :] * near)
    return gate, (skip * first - early, skip * second)


def from_lower(modes, axis, pair_ref, taps_ref, decays_ref, residues_ref, skip_ref):
    inside = lax.rem(lax.axis_index(axis), PAIR).astype(F32)
    rates = decays_ref[...]
    first, second = (inside * p for p in pair_boundary(modes, taps_ref, pair_ref.at[0], pair_ref.at[1]))
    state = inside * pair_ref[0, :modes, :] + jnp.exp(rates) * first + jnp.exp(2.0 * rates) * second
    far, near = (inside * row for row in two_rows(pair_ref.at[0], modes + Q_LAST))
    weights = mode_weights(decays_ref, residues_ref)
    return state, *edge_gains(taps_ref, skip_ref, rates, weights, first, second, far, near)


def at_top(block, row):
    return block + jnp.where(sublane_index() == 0, over_sublanes(row), 0.0)


def fades(decays_ref, run, m):
    return jnp.exp(over_sublanes(decays_ref[m : m + 1, :]) * (sublane_index().astype(F32) * -float(run)))


def load_gate(q_ref, q_half, taps_ref):
    run = q_half.shape[0] // CHUNKS
    for s in range(CHUNKS):
        q_ref[s * PITCH : s * PITCH + run, :] = q_half[s * run : (s + 1) * run, :].astype(F32)
    taps = [over_sublanes(taps_ref[0, i : i + 1, :]) for i in range(3)]
    return taps, [next_chunk(strided(q_ref, run - 1 - i, PITCH)) for i in range(2)]


def split(table):
    return [over_sublanes(table[m : m + 1, :]) for m in range(table.shape[0])]


def local_work(
    modes, axis, q_half, product_ref, state_ref, pair_ref, taps_ref, decays_ref, residues_ref, skip_ref,
    gate_ref, base_ref, begin_ref, reach_ref, q_ref,
):
    run = product_ref.shape[0]
    positions = run * CHUNKS
    inside = lax.rem(lax.axis_index(axis), PAIR).astype(F32)
    rates = decays_ref[...]
    spread = split(mode_weights(decays_ref, residues_ref))
    factors = split(jnp.exp(-rates))
    skip = over_sublanes(skip_ref[...])
    taps, before = load_gate(q_ref, q_half, taps_ref)

    def step(j, carry):
        q1, q2, states = carry
        q0 = strided(q_ref, j, PITCH)
        gate_ref[j] = taps[0] * q0 + taps[1] * q1 + taps[2] * q2
        product = product_ref[j]
        states = tuple(a * h + product for a, h in zip(factors, states))
        base_ref[j] = added([skip * product] + [w * h for w, h in zip(spread, states)])
        return q0, q1, states

    start = (*before, tuple(jnp.zeros((CHUNKS, LANES), F32) for _ in range(modes)))
    lax.fori_loop(0, run, step, start, unroll=4)

    arrived, gate_gain, base_gain = from_lower(modes, axis, pair_ref, taps_ref, decays_ref, residues_ref, skip_ref)
    for j in range(2):
        gate_ref[j] = at_top(gate_ref[j], gate_gain[j])
        base_ref[j] = at_top(base_ref[j], base_gain[j])
    across = jnp.exp(-rates * (inside * float(positions)))
    for m in range(modes):
        fade = fades(decays_ref, run, m)
        begin_ref[m] = spread[m] * (state_ref[m] + fade * over_sublanes(arrived[m : m + 1, :]))
        reach_ref[m] = spread[m] * fade * over_sublanes(across[m : m + 1, :])


def join_kernel(
    modes, axis, own_ref, other_ref, q_half, product_ref, state_ref, taps_ref, decays_ref, residues_ref, skip_ref,
    sent_ref, pair_ref, *refs,
):
    positions = q_half.shape[0]
    upper = lax.rem(lax.axis_index(axis), PAIR) == 1
    own = own_ref[...]
    other = other_ref[...]
    below = jnp.where(upper, other, own)
    above = jnp.where(upper, own, other)
    pair_ref[0] = below
    pair_ref[1] = above
    first, second = pair_boundary(modes, taps_ref, pair_ref.at[0], pair_ref.at[1])
    rates = decays_ref[...]
    state = jnp.exp(-float(positions) * rates) * below[:modes] + above[:modes]
    state = state + jnp.exp(-float(positions - 1) * rates) * first + jnp.exp(-float(positions - 2) * rates) * second
    row = lax.broadcasted_iota(jnp.int32, (EXTRA, LANES), 0)
    beside = jnp.where(row < K_FIRST, above[modes:], below[modes:])
    rows = jnp.concatenate([state, beside], 0).astype(BF16)
    sent_ref[...] = jnp.broadcast_to(rows[None], sent_ref.shape)

    @pl.when(starts_early(axis))
    def _():
        params = (taps_ref, decays_ref, residues_ref, skip_ref)
        local_work(modes, axis, q_half, product_ref, state_ref, pair_ref, *params, *refs)


def carry_kernel(
    modes, axis, received_ref, gate_ref, base_ref, begin_ref, reach_ref, q_half, product_ref, state_ref, pair_ref,
    taps_ref, decays_ref, residues_ref, skip_ref, power_ref, gated_ref, rows_ref, first_ref, second_ref, q_ref,
):
    run = product_ref.shape[0]
    positions = run * CHUNKS
    pairs = received_ref.shape[0]
    device = lax.axis_index(axis)
    pair = device // PAIR
    inside = lax.rem(device, PAIR).astype(F32)
    pitch = modes + EXTRA
    rows_ref[0:pitch, :] = jnp.zeros((pitch, LANES), F32)
    for slot, e in enumerate(pair_order(pairs)):
        rows_ref[pitch * (e + 1) : pitch * (e + 2), :] = received_ref[slot].astype(F32)

    def of_all(row, block):
        return tuple(rows_ref[pl.ds(pitch * block + modes + row + i, pairs, stride=pitch), :] for i in range(2))

    last = [of_all(row, 0) for row in (K_LAST, V_LAST)]
    begun = [of_all(row, 1) for row in (K_FIRST, V_FIRST)]
    first_ref[...], second_ref[...] = boundary(taps_ref, last, begun)

    rates = decays_ref[...]
    length = PAIR * positions
    across = jnp.exp(-float(length) * rates)
    late_first = jnp.exp(-float(length - 1) * rates)
    late_second = jnp.exp(-float(length - 2) * rates)
    state = jnp.zeros((modes, LANES), F32)
    for e in range(pairs - 1):
        sent = rows_ref[pitch * (e + 1) : pitch * (e + 1) + modes, :]
        sent = sent + late_first * first_ref[e : e + 1, :] + late_second * second_ref[e : e + 1, :]
        state = jnp.where(e < pair, across * state + sent, state)
    first, second = first_ref[pl.ds(pair, 1), :], second_ref[pl.ds(pair, 1), :]
    state = state + jnp.exp(rates) * first + jnp.exp(2.0 * rates) * second

    weights = mode_weights(decays_ref, residues_ref)
    lower = 1.0 - inside
    far, near = (lower * rows_ref[pl.ds(pair * pitch + modes + Q_LAST + i, 1), :] for i in range(2))
    gate_more, base_more = edge_gains(taps_ref, skip_ref, rates, weights, lower * first, lower * second, far, near)
    factors = split(jnp.exp(-rates))

    def put(j, gate, base, terms, more):
        if more is not None:
            gate, base = at_top(gate, more[0]), at_top(base, more[1])
        gated_ref[pl.ds(j, CHUNKS, stride=SPAN), :] = gate * added([base] + terms)

    def over_steps(step, held, gains, unroll):
        for j in range(2):
            held = step(j, held, (gains[0][j], gains[1][j]))
        lax.fori_loop(2, run, lambda j, held: step(j, held, None), held, unroll=unroll)

    @pl.when(starts_early(axis))
    def _():
        def step(j, carried, more):
            carried = tuple(a * g for a, g in zip(factors, carried))
            put(j, gate_ref[j], base_ref[j], list(carried), more)
            return carried

        carried = tuple(begin_ref[m] + reach_ref[m] * over_sublanes(state[m : m + 1, :]) for m in range(modes))
        over_steps(step, carried, (gate_more, base_more), 14)

    @pl.when(jnp.logical_not(starts_early(axis)))
    def _():
        taps, before = load_gate(q_ref, q_half, taps_ref)
        skip = over_sublanes(skip_ref[...])
        spread = split(weights)
        arrived, gate_gain, base_gain = from_lower(modes, axis, pair_ref, taps_ref, decays_ref, residues_ref, skip_ref)
        arrived = arrived + jnp.exp(-rates * (inside * float(positions))) * state
        states = tuple(
            state_ref[m] + fades(decays_ref, run, m) * over_sublanes(arrived[m : m + 1, :]) for m in range(modes)
        )

        def step(j, held, more):
            q1, q2, states = held
            q0 = strided(q_ref, j, PITCH)
            product = product_ref[j]
            states = tuple(a * h + product for a, h in zip(factors, states))
            gate = taps[0] * q0 + taps[1] * q1 + taps[2] * q2
            put(j, gate, skip * product, [w * h for w, h in zip(spread, states)], more)
            return q0, q1, states

        gains = tuple([a + b for a, b in zip(*both)] for both in ((gate_gain, gate_more), (base_gain, base_more)))
        over_steps(step, (*before, states), gains, 6)

    ones = jnp.ones((LANES, LANES), BF16)
    lane = lax.broadcasted_iota(jnp.int32, (CHUNKS, LANES), 1)
    power = jnp.zeros((CHUNKS, LANES), F32)
    tiles = run // CHUNKS
    for s in range(CHUNKS):
        gated = gated_ref[s * SPAN : s * SPAN + run, :]
        square = gated * gated
        high = square.astype(BF16)
        low = (square - high.astype(F32)).astype(BF16)
        sums = jnp.dot(high, ones, preferred_element_type=F32) + jnp.dot(low, ones, preferred_element_type=F32)
        for i in range(tiles):
            power = jnp.where(lane == s * tiles + i, sums[i * CHUNKS : (i + 1) * CHUNKS, :], power)
    power_ref[...] = jnp.broadcast_to(power[None], power_ref.shape)


def finish_kernel(channels, power_ref, gated_ref, gain_ref, mixed_ref):
    run = mixed_ref.shape[0] // CHUNKS
    tiles = run // CHUNKS
    inverse = lax.rsqrt(jnp.sum(power_ref[...], 0) / channels + 1e-05)
    gain = over_sublanes(gain_ref[...])
    for s in range(CHUNKS):
        for i in range(0, tiles, 2):
            halves = []
            for h in (i, i + 1):
                gated = gated_ref[s * SPAN + h * CHUNKS : s * SPAN + (h + 1) * CHUNKS, :]
                halves.append(gated * gain * inverse[:, s * tiles + h : s * tiles + h + 1])
            mixed_ref[s * run + i * CHUNKS : s * run + (i + 2) * CHUNKS, :] = jnp.concatenate(halves, 0).astype(BF16)


def per_device(projections, short_filter, residues, decays, skip, gain):
    positions, _, width = projections.shape
    modes = decays.shape[0]
    ctx_count = lax.axis_size("ctx")
    tp_count = lax.axis_size("tp")
    pairs = ctx_count // PAIR
    run = positions // CHUNKS
    x = jnp.swapaxes(projections, 0, 1)

    def shape(*extent, kind=F32):
        return jax.ShapeDtypeStruct(extent, kind)

    def call(kernel, name, out_shape, in_specs, scratch, *operands):
        return pl.pallas_call(
            kernel,
            out_shape=out_shape,
            in_specs=in_specs,
            out_specs=jax.tree.map(lambda _: VMEM, out_shape),
            scratch_shapes=scratch,
            compiler_params=pltpu.CompilerParams(vmem_limit_bytes=VMEM_LIMIT),
            name=name,
        )(*operands)

    block = shape(run, CHUNKS, width)
    table = shape(modes, CHUNKS, width)
    sources = (x, short_filter, decays, residues, skip[None, :], gain[None, :])
    rows, product, state, q, short_filter, decays, residues, skip, gain = call(
        functools.partial(states_kernel, modes),
        "states",
        (shape(modes + EXTRA, width), block, table, shape(positions, width, kind=BF16))
        + tuple(shape(*s.shape) for s in sources[1:]),
        [ANY] * 6,
        [
            pltpu.VMEM((positions, width), BF16),
            pltpu.VMEM((positions, width), BF16),
            pltpu.VMEM((PITCH * CHUNKS, width), F32),
            pltpu.VMEM((PITCH * CHUNKS, width), F32),
            pltpu.VMEM((3, modes, width), F32),
            pltpu.SemaphoreType.DMA((8,)),
        ],
        *[pltpu.with_memory_space_constraint(s, pltpu.HBM) for s in sources],
    )
    other = lax.ppermute(rows, "ctx", [(i, i + 1 - 2 * (i % PAIR)) for i in range(ctx_count)])
    params = (short_filter, decays, residues, skip)
    pitched = pltpu.VMEM((PITCH * CHUNKS, width), F32)
    sent, joined, gate, base, begin, reach = call(
        functools.partial(join_kernel, modes, "ctx"),
        "join",
        (shape(pairs, modes + EXTRA, width, kind=BF16), shape(PAIR, modes + EXTRA, width), block, block, table, table),
        [VMEM] * 9,
        [pitched],
        rows,
        other,
        q,
        product,
        state,
        *params,
    )
    groups = [[PAIR * i + h for i in pair_order(pairs)] for h in range(PAIR)]
    received = lax.all_to_all(sent, "ctx", split_axis=0, concat_axis=0, tiled=True, axis_index_groups=groups)

    power, gated = call(
        functools.partial(carry_kernel, modes, "ctx"),
        "carry",
        (shape(tp_count, CHUNKS, run), shape(SPAN * CHUNKS, width)),
        [VMEM] * 13,
        [
            pltpu.VMEM(((pairs + 1) * (modes + EXTRA), width), F32),
            pltpu.VMEM((pairs, width), F32),
            pltpu.VMEM((pairs, width), F32),
            pitched,
        ],
        received,
        gate,
        base,
        begin,
        reach,
        q,
        product,
        state,
        joined,
        *params,
    )
    powers = lax.all_to_all(
        power, "tp", split_axis=0, concat_axis=0, tiled=True, axis_index_groups=[slice_order(tp_count)]
    )
    return call(
        functools.partial(finish_kernel, width * tp_count),
        "finish",
        shape(positions, width, kind=BF16),
        [VMEM] * 3,
        [],
        powers,
        gated,
        gain,
    )


def solution(mesh):
    in_specs = (
        P("ctx", None, "tp"),
        P(None, None, "tp"),
        P(None, "tp"),
        P(None, "tp"),
        P("tp"),
        P("tp"),
    )
    return jax.shard_map(per_device, mesh=mesh, in_specs=in_specs, out_specs=P("ctx", "tp"), check_vma=False)
```

time: 32.3 us -> 31.3 us (0.969)
  blocking collectives: 8.65 us -> 24.2 us
  starting transfers between devices: 13.4 us -> 0.09 us
  Pallas kernels: 7.21 us -> 5.59 us
  waiting for transfers between devices: 2.74 us -> 1.17 us
    all_to_all x0 -> x1, blocking collectives: none -> 15.6 us  [per_device(): lax.all_to_all(sent, 'ctx', split_axis=0, concat_axis=0, tiled=True, axis...]
    all_to_all x1 -> x0, starting transfers between devices: 13.3 us -> none  [per_device(): lax.all_to_all(sent, 'ctx', split_axis=0, concat_axis=0, tiled=True, axis...]
    pallas_call x5 -> x4, Pallas kernels: 7.21 us -> 5.59 us  [call(): pl.pallas_call(kernel, out_shape=out_shape, in_specs=in_specs, out_specs=...]
    all_to_all x1 -> x0, waiting for transfers between devices: 1.57 us -> none  [per_device(): lax.all_to_all(sent, 'ctx', split_axis=0, concat_axis=0, tiled=True, axis...]
  transfers between devices with their start and end apart: 2 -> 1, of which waited for: 2 -> 1; matrix products, arithmetic and copies ran while one was open for 0% -> 0% of each run, Pallas kernels for 6% -> 0%
where the time goes in v5:
time: 31.3 us; the launch traced here: 31.1 us
  blocking collectives  24.2 us (77%)
  Pallas kernels  5.59 us (18%)
  waiting for transfers between devices  1.17 us (4%)
    all_to_all x1, blocking collectives, per_device(): lax.all_to_all(sent, 'ctx', split_axis=0, concat_axis=0, tiled=True, axis...  15.6 us
    all_to_all x1, blocking collectives, per_device(): lax.all_to_all(power, 'tp', split_axis=0, concat_axis=0, tiled=True, axis...  8.64 us
    pallas_call x4, Pallas kernels, call(): pl.pallas_call(kernel, out_shape=out_shape, in_specs=in_specs, out_specs=...  5.59 us
    ppermute x1, waiting for transfers between devices, per_device(): lax.ppermute(rows, 'ctx', [(i, i + 1 - 2 * (i % PAIR)) for i in range(ctx...  1.17 us
  transfers between devices with their start and end apart: 1, of which 1 were waited for; matrix products, arithmetic and copies ran while one was open for 0% of the time, Pallas kernels for 0%

profile of v5, /device:TPU:2, one launch (start us, length us, event | category | flops | bytes accessed | tf_op | source)
XLA Modules:
  0.0 31.1 jit_solution(5674462456363265866)
XLA Ops:
  0.0 2.0 %states.1 = (f32[32,128]{1,0:T(8,128)S(1)}, f32[128,8,128]{2,1,0:T(8,128)S(1)}, f32[16,8,128]{2,1,0:T(8,128)S(1)}, bf16[1024,128]{1,0:T(8,128)(2,1)S(1)}, f32[3,...) custom-call(bf16[3,1024,128]{2,1,0:T(8,128)(2,1)} %bitcast.3, ...), custom_call_target="tpu_custom_call" | custom-call | tf_op jit(solution)/shard_map/states/pallas_call | solution.py:397
  2.0 0.1 collective-permute-start
  2.1 1.2 %collective-permute-done.other_ref = f32[32,128]{1,0:T(8,128)S(1)} collective-permute-done((f32[32,128]{1,0:T(8,128)S(1)}, f32[32,128]{1,0:T(8,128)S(1)}, u32[]{:S(2)}, u32[]{:S(2)}) %collective-permute-start) | collective-permute-done | bytes 16416 | tf_op jit(solution)/shard_map/ppermute | solution.py:426
  3.2 1.6 %join.1 = (bf16[16,32,128]{2,1,0:T(8,128)(2,1)S(1)}, f32[2,32,128]{2,1,0:T(8,128)S(1)}, f32[128,8,128]{2,1,0:T(8,128)S(1)}, f32[128,8,128]{2,1,0:T(8,128)S(1)}, ...) custom-call(f32[32,128]{1,0:T(8,128)S(1)} %get-tuple-element.22.own_ref, ...), custom_call_target="tpu_custom_call" | custom-call | tf_op jit(solution)/shard_map/join/pallas_call | solution.py:397
  4.8 15.6 %all_to_all.10.received_ref = bf16[16,32,128]{2,1,0:T(8,128)(2,1)S(1)} all-to-all(bf16[16,32,128]{2,1,0:T(8,128)(2,1)S(1)} %get-tuple-element.30), channel_id=1, replica_groups={{160,0,64,192,16,48,128,80,112,208,240,32,144,176,96,224},{168,8,72,200..., dimensions={0} | all-to-all | bytes 262144 | tf_op jit(solution)/shard_map/all_to_all | solution.py:443
  20.4 1.0 %carry.1 = (f32[8,8,128]{2,1,0:T(8,128)S(1)}, f32[1088,128]{1,0:T(8,128)S(1)}) custom-call(bf16[16,32,128]{2,1,0:T(8,128)(2,1)S(1)} %all_to_all.10.received_ref, f32[128,8,128]{2,1,0:T(8,128)S(1)} %get-tuple-element.31.gate_ref, f32[128,8,128]{2,1,0:T(8,128)S(1)} %get-tuple-element.32.base_ref, f32[16,8,128]{2,1,0:T(8,128)S(1)} %get-tuple-element.33.begin_ref, ...), custom_call_target="tpu_custom_call" | custom-call | tf_op jit(solution)/shard_map/carry/pallas_call | solution.py:397
  21.5 8.6 %all_to_all.11.power_ref = f32[8,8,128]{2,1,0:T(8,128)S(1)} all-to-all(f32[8,8,128]{2,1,0:T(8,128)S(1)} %get-tuple-element.36), channel_id=1, replica_groups={{5,0,1,2,3,4,6,7},{13,8,9,10,11,12,14,15},{21,16,17,18,19,20,22,23},{29..., dimensions={0} | all-to-all | bytes 65536 | tf_op jit(solution)/shard_map/all_to_all | solution.py:467
  30.1 1.0 %finish.1 = bf16[1024,128]{1,0:T(8,128)(2,1)} custom-call(f32[8,8,128]{2,1,0:T(8,128)S(1)} %all_to_all.11.power_ref, f32[1088,128]{1,0:T(8,128)S(1)} %get-tuple-element.37.gated_ref, f32[1,128]{1,0:T(1,128)S(1)} %get-tuple-element.38.gain_ref), custom_call_target="tpu_custom_call" | custom-call | tf_op jit(solution)/shard_map/finish/pallas_call | solution.py:397
Async XLA Ops:
  2.0 1.3 %collective-permute-start = (f32[32,128]{1,0:T(8,128)S(1)}, f32[32,128]{1,0:T(8,128)S(1)}, u32[]{:S(2)}, u32[]{:S(2)}) collective-permute-start(f32[32,128]{1,0:T(8,128)S(1)} %get-tuple-element.22.own_ref), channel_id=1, source_target_pairs={{0,8},{8,0},{16,24},{24,16},{32,40},{40,32},{48,56},{56,48},{64,72... | collective-permute-start | bytes 49160 | tf_op jit(solution)/shard_map/ppermute | solution.py:426

commit v6 on v5

--- a/solution.py
+++ b/solution.py
@@ -24,6 +24,7 @@
 
 K_LAST, V_LAST, Q_LAST, K_FIRST, V_FIRST = 0, 2, 4, 6, 8
 EXTRA = 16
+EDGE = 8
 
 
 def first_then(first, members, distance):
@@ -39,6 +40,16 @@
         return around(a // GRID, b // GRID, max(pairs // GRID, 1)) + 2 * around(a % GRID, b % GRID, GRID)
 
     return first_then(FIRST_PAIR % pairs, pairs, distance)
+
+
+def ctx_groups(pairs, slices):
+    def index(pair, half, piece):
+        return (pair * PAIR + half) * slices + piece
+
+    groups = [[index(p, PAIR - 1, piece) for p in pair_order(pairs)] for piece in range(slices)]
+    rest = [(p % GRID, p // GRID // 2, -index(p, 0, piece)) for p in range(pairs) for piece in range(slices)]
+    rest = [-i for *_, i in sorted(rest)]
+    return groups + [rest[i : i + pairs] for i in range(0, len(rest), pairs)]
 
 
 def slice_order(slices):
@@ -246,11 +257,7 @@
     sent_ref, pair_ref, *refs,
 ):
     positions = q_half.shape[0]
-    upper = lax.rem(lax.axis_index(axis), PAIR) == 1
-    own = own_ref[...]
-    other = other_ref[...]
-    below = jnp.where(upper, other, own)
-    above = jnp.where(upper, own, other)
+    below, above = other_ref[...], own_ref[...]
     pair_ref[0] = below
     pair_ref[1] = above
     first, second = pair_boundary(modes, taps_ref, pair_ref.at[0], pair_ref.at[1])
@@ -268,45 +275,74 @@
         local_work(modes, axis, q_half, product_ref, state_ref, pair_ref, *params, *refs)
 
 
+def enter_kernel(
+    modes, axis, received_ref, q_half, product_ref, state_ref, pair_ref, taps_ref, decays_ref, residues_ref, skip_ref, *refs
+):
+    enter_ref, local_refs, (rows_ref, first_ref, second_ref, q_ref) = refs[0], refs[1:5], refs[5:]
+    positions = q_half.shape[0]
+    device = lax.axis_index(axis)
+    pair = device // PAIR
+    upper = lax.rem(device, PAIR) == 1
+
+    @pl.when(jnp.logical_not(jnp.logical_or(upper, starts_early(axis))))
+    def _():
+        params = (taps_ref, decays_ref, residues_ref, skip_ref)
+        local_work(modes, axis, q_half, product_ref, state_ref, pair_ref, *params, *local_refs, q_ref)
+
+    enter_ref[...] = jnp.zeros_like(enter_ref)
+
+    @pl.when(upper)
+    def _():
+        pairs = received_ref.shape[0]
+        pitch = modes + EXTRA
+        rows_ref[0:pitch, :] = jnp.zeros((pitch, LANES), F32)
+        for slot, e in enumerate(pair_order(pairs)):
+            rows_ref[pitch * (e + 1) : pitch * (e + 2), :] = received_ref[slot].astype(F32)
+
+        def of_all(row, block):
+            return tuple(rows_ref[pl.ds(pitch * block + modes + row + i, pairs, stride=pitch), :] for i in range(2))
+
+        last = [of_all(row, 0) for row in (K_LAST, V_LAST)]
+        begun = [of_all(row, 1) for row in (K_FIRST, V_FIRST)]
+        first_ref[...], second_ref[...] = boundary(taps_ref, last, begun)
+
+        rates = decays_ref[...]
+        length = PAIR * positions
+        across = jnp.exp(-float(length) * rates)
+        late_first = jnp.exp(-float(length - 1) * rates)
+        late_second = jnp.exp(-float(length - 2) * rates)
+        state = jnp.zeros((modes, LANES), F32)
+        for e in range(pairs - 1):
+            sent = rows_ref[pitch * (e + 1) : pitch * (e + 1) + modes, :]
+            sent = sent + late_first * first_ref[e : e + 1, :] + late_second * second_ref[e : e + 1, :]
+            state = jnp.where(e < pair, across * state + sent, state)
+        first, second = first_ref[pl.ds(pair, 1), :], second_ref[pl.ds(pair, 1), :]
+        enter_ref[:modes, :] = state + jnp.exp(rates) * first + jnp.exp(2.0 * rates) * second
+        enter_ref[modes : modes + 1, :] = first
+        enter_ref[modes + 1 : modes + 2, :] = second
+        for i in range(2):
+            enter_ref[modes + 2 + i : modes + 3 + i, :] = rows_ref[pl.ds(pair * pitch + modes + Q_LAST + i, 1), :]
+        enter_ref[modes + 4 :, :] = jnp.zeros((EDGE - 4, LANES), F32)
+
+
 def carry_kernel(
-    modes, axis, received_ref, gate_ref, base_ref, begin_ref, reach_ref, q_half, product_ref, state_ref, pair_ref,
-    taps_ref, decays_ref, residues_ref, skip_ref, power_ref, gated_ref, rows_ref, first_ref, second_ref, q_ref,
+    modes, axis, own_ref, other_ref, *refs
 ):
+    early_locals, locals_, refs = refs[:4], refs[4:8], refs[8:]
+    q_half, product_ref, state_ref, pair_ref, taps_ref, decays_ref, residues_ref, skip_ref, *refs = refs
+    power_ref, gated_ref, enter_ref, q_ref = refs
     run = product_ref.shape[0]
     positions = run * CHUNKS
-    pairs = received_ref.shape[0]
-    device = lax.axis_index(axis)
-    pair = device // PAIR
-    inside = lax.rem(device, PAIR).astype(F32)
-    pitch = modes + EXTRA
-    rows_ref[0:pitch, :] = jnp.zeros((pitch, LANES), F32)
-    for slot, e in enumerate(pair_order(pairs)):
-        rows_ref[pitch * (e + 1) : pitch * (e + 2), :] = received_ref[slot].astype(F32)
-
-    def of_all(row, block):
-        return tuple(rows_ref[pl.ds(pitch * block + modes + row + i, pairs, stride=pitch), :] for i in range(2))
-
-    last = [of_all(row, 0) for row in (K_LAST, V_LAST)]
-    begun = [of_all(row, 1) for row in (K_FIRST, V_FIRST)]
-    first_ref[...], second_ref[...] = boundary(taps_ref, last, begun)
-
+    upper = lax.rem(lax.axis_index(axis), PAIR) == 1
+    inside = lax.rem(lax.axis_index(axis), PAIR).astype(F32)
+    enter_ref[...] = jnp.where(upper, own_ref[...], other_ref[...])
     rates = decays_ref[...]
-    length = PAIR * positions
-    across = jnp.exp(-float(length) * rates)
-    late_first = jnp.exp(-float(length - 1) * rates)
-    late_second = jnp.exp(-float(length - 2) * rates)
-    state = jnp.zeros((modes, LANES), F32)
-    for e in range(pairs - 1):
-        sent = rows_ref[pitch * (e + 1) : pitch * (e + 1) + modes, :]
-        sent = sent + late_first * first_ref[e : e + 1, :] + late_second * second_ref[e : e + 1, :]
-        state = jnp.where(e < pair, across * state + sent, state)
-    first, second = first_ref[pl.ds(pair, 1), :], second_ref[pl.ds(pair, 1), :]
-    state = state + jnp.exp(rates) * first + jnp.exp(2.0 * rates) * second
-
+    state = enter_ref[:modes, :]
+    first, second, far, near = (enter_ref[modes + i : modes + i + 1, :] for i in range(4))
     weights = mode_weights(decays_ref, residues_ref)
     lower = 1.0 - inside
-    far, near = (lower * rows_ref[pl.ds(pair * pitch + modes + Q_LAST + i, 1), :] for i in range(2))
-    gate_more, base_more = edge_gains(taps_ref, skip_ref, rates, weights, lower * first, lower * second, far, near)
+    edge = (lower * row for row in (first, second, far, near))
+    gate_more, base_more = edge_gains(taps_ref, skip_ref, rates, weights, *edge)
     factors = split(jnp.exp(-rates))
 
     def put(j, gate, base, terms, more):
@@ -319,8 +355,9 @@
             held = step(j, held, (gains[0][j], gains[1][j]))
         lax.fori_loop(2, run, lambda j, held: step(j, held, None), held, unroll=unroll)
 
-    @pl.when(starts_early(axis))
-    def _():
+    early = starts_early(axis)
+
+    def from_local(gate_ref, base_ref, begin_ref, reach_ref):
         def step(j, carried, more):
             carried = tuple(a * g for a, g in zip(factors, carried))
             put(j, gate_ref[j], base_ref[j], list(carried), more)
@@ -329,7 +366,15 @@
         carried = tuple(begin_ref[m] + reach_ref[m] * over_sublanes(state[m : m + 1, :]) for m in range(modes))
         over_steps(step, carried, (gate_more, base_more), 14)
 
-    @pl.when(jnp.logical_not(starts_early(axis)))
+    @pl.when(early)
+    def _():
+        from_local(*early_locals)
+
+    @pl.when(jnp.logical_not(jnp.logical_or(early, upper)))
+    def _():
+        from_local(*locals_)
+
+    @pl.when(jnp.logical_and(upper, jnp.logical_not(early)))
     def _():
         taps, before = load_gate(q_ref, q_half, taps_ref)
         skip = over_sublanes(skip_ref[...])
@@ -423,10 +468,11 @@
         ],
         *[pltpu.with_memory_space_constraint(s, pltpu.HBM) for s in sources],
     )
-    other = lax.ppermute(rows, "ctx", [(i, i + 1 - 2 * (i % PAIR)) for i in range(ctx_count)])
+    partners = [(i, i + 1 - 2 * (i % PAIR)) for i in range(ctx_count)]
+    other = lax.ppermute(rows, "ctx", partners)
     params = (short_filter, decays, residues, skip)
     pitched = pltpu.VMEM((PITCH * CHUNKS, width), F32)
-    sent, joined, gate, base, begin, reach = call(
+    sent, joined, *early_locals = call(
         functools.partial(join_kernel, modes, "ctx"),
         "join",
         (shape(pairs, modes + EXTRA, width, kind=BF16), shape(PAIR, modes + EXTRA, width), block, block, table, table),
@@ -439,14 +485,16 @@
         state,
         *params,
     )
-    groups = [[PAIR * i + h for i in pair_order(pairs)] for h in range(PAIR)]
-    received = lax.all_to_all(sent, "ctx", split_axis=0, concat_axis=0, tiled=True, axis_index_groups=groups)
-
-    power, gated = call(
-        functools.partial(carry_kernel, modes, "ctx"),
-        "carry",
-        (shape(tp_count, CHUNKS, run), shape(SPAN * CHUNKS, width)),
-        [VMEM] * 13,
+    received = lax.all_to_all(
+        sent, ("ctx", "tp"), split_axis=0, concat_axis=0, tiled=True, axis_index_groups=ctx_groups(pairs, tp_count)
+    )
+    enter_shape = shape(modes + EDGE, width)
+    local_shapes = (block, block, table, table)
+    enter, *locals_ = call(
+        functools.partial(enter_kernel, modes, "ctx"),
+        "enter",
+        (enter_shape, *local_shapes),
+        [VMEM] * 9,
         [
             pltpu.VMEM(((pairs + 1) * (modes + EXTRA), width), F32),
             pltpu.VMEM((pairs, width), F32),
@@ -454,10 +502,23 @@
             pitched,
         ],
         received,
-        gate,
-        base,
-        begin,
-        reach,
+        q,
+        product,
+        state,
+        joined,
+        *params,
+    )
+    entered = lax.ppermute(enter, "ctx", partners)
+    power, gated = call(
+        functools.partial(carry_kernel, modes, "ctx"),
+        "carry",
+        (shape(tp_count, CHUNKS, run), shape(SPAN * CHUNKS, width)),
+        [VMEM] * 18,
+        [pltpu.VMEM((modes + EDGE, width), F32), pitched],
+        enter,
+        entered,
+        *early_locals,
+        *locals_,
         q,
         product,
         state,

time: 31.3 us -> 30.3 us (0.968)
  blocking collectives: 24.2 us -> 19.6 us
  starting transfers between devices: 0.09 us -> 2.8 us
  waiting for transfers between devices: 1.17 us -> 2 us
    all_to_all x1, blocking collectives: 15.6 us -> 10.8 us  [per_device(): lax.all_to_all(sent, ('ctx', 'tp'), split_axis=0, concat_axis=0, tiled=Tr...]
    ppermute x1 -> x2, starting transfers between devices: 0.09 us -> 2.8 us  [the longest x1 2.71 us: per_device(): entered = lax.ppermute(enter, 'ctx', partners)]
    ppermute x1 -> x2, waiting for transfers between devices: 1.17 us -> 2 us  [the longest x1 1.17 us: per_device(): other = lax.ppermute(rows, 'ctx', partners)]
    pallas_call x4 -> x5, Pallas kernels: 5.59 us -> 5.5 us  [call(): pl.pallas_call(kernel, out_shape=out_shape, in_specs=in_specs, out_specs=...]
  transfers between devices with their start and end apart: 1 -> 2, of which waited for: 1 -> 2; matrix products, arithmetic and copies ran while one was open for 0% -> 0% of each run, Pallas kernels for 0% -> 0%
where the time goes in v6:
time: 30.3 us; the launch traced here: 30 us
  blocking collectives  19.6 us (65%)
  Pallas kernels  5.5 us (18%)
  starting transfers between devices  2.8 us (9%)
  waiting for transfers between devices  2 us (7%)
    all_to_all x1, blocking collectives, per_device(): lax.all_to_all(sent, ('ctx', 'tp'), split_axis=0, concat_axis=0, tiled=Tr...  10.8 us
    all_to_all x1, blocking collectives, per_device(): lax.all_to_all(power, 'tp', split_axis=0, concat_axis=0, tiled=True, axis...  8.77 us
    pallas_call x5, Pallas kernels, call(): pl.pallas_call(kernel, out_shape=out_shape, in_specs=in_specs, out_specs=...  5.5 us
    ppermute x1, starting transfers between devices, per_device(): entered = lax.ppermute(enter, 'ctx', partners)  2.71 us
    ppermute x1, waiting for transfers between devices, per_device(): other = lax.ppermute(rows, 'ctx', partners)  1.17 us
    ppermute x1, waiting for transfers between devices, per_device(): entered = lax.ppermute(enter, 'ctx', partners)  0.83 us
  transfers between devices with their start and end apart: 2, of which 2 were waited for; matrix products, arithmetic and copies ran while one was open for 0% of the time, Pallas kernels for 0%

profile of v6, /device:TPU:2, one launch (start us, length us, event | category | flops | bytes accessed | tf_op | source)
XLA Modules:
  0.0 30.0 jit_solution(8169776829693436366)
XLA Ops:
  0.0 2.0 %states.1 = (f32[32,128]{1,0:T(8,128)S(1)}, f32[128,8,128]{2,1,0:T(8,128)S(1)}, f32[16,8,128]{2,1,0:T(8,128)S(1)}, bf16[1024,128]{1,0:T(8,128)(2,1)S(1)}, f32[3,...) custom-call(bf16[3,1024,128]{2,1,0:T(8,128)(2,1)} %bitcast.3, ...), custom_call_target="tpu_custom_call" | custom-call | tf_op jit(solution)/shard_map/states/pallas_call | solution.py:442
  2.0 0.1 collective-permute-start
  2.1 1.2 %collective-permute-done.other_ref = f32[32,128]{1,0:T(8,128)S(1)} collective-permute-done((f32[32,128]{1,0:T(8,128)S(1)}, f32[32,128]{1,0:T(8,128)S(1)}, u32[]{:S(2)}, u32[]{:S(2)}) %collective-permute-start) | collective-permute-done | bytes 16416 | tf_op jit(solution)/shard_map/ppermute | solution.py:472
  3.2 1.6 %join.1 = (bf16[16,32,128]{2,1,0:T(8,128)(2,1)S(1)}, f32[2,32,128]{2,1,0:T(8,128)S(1)}, f32[128,8,128]{2,1,0:T(8,128)S(1)}, f32[128,8,128]{2,1,0:T(8,128)S(1)}, ...) custom-call(f32[32,128]{1,0:T(8,128)S(1)} %get-tuple-element.27.own_ref, ...), custom_call_target="tpu_custom_call" | custom-call | tf_op jit(solution)/shard_map/join/pallas_call | solution.py:442
  4.8 10.8 %all_to_all.10.received_ref = bf16[16,32,128]{2,1,0:T(8,128)(2,1)S(1)} all-to-all(bf16[16,32,128]{2,1,0:T(8,128)(2,1)S(1)} %get-tuple-element.35), channel_id=1, replica_groups={{168,8,72,200,24,56,136,88,120,216,248,40,152,184,104,232},{169,9,73,20..., dimensions={0} | all-to-all | bytes 262144 | tf_op jit(solution)/shard_map/all_to_all | solution.py:488
  15.7 2.7 %collective-permute-start.1 = (f32[24,128]{1,0:T(8,128)S(1)}, f32[24,128]{1,0:T(8,128)S(1)}, u32[]{:S(2)}, u32[]{:S(2)}) collective-permute-start(f32[24,128]{1,0:T(8,128)S(1)} %get-tuple-element.37.own_ref), channel_id=1, source_target_pairs={{0,8},{8,0},{16,24},{24,16},{32,40},{40,32},{48,56},{56,48},{64,72... | collective-permute-start | bytes 36872 | tf_op jit(solution)/shard_map/ppermute | solution.py:511
  18.4 0.8 %collective-permute-done.1.other_ref = f32[24,128]{1,0:T(8,128)S(1)} collective-permute-done((f32[24,128]{1,0:T(8,128)S(1)}, f32[24,128]{1,0:T(8,128)S(1)}, u32[]{:S(2)}, u32[]{:S(2)}) %collective-permute-start.1) | collective-permute-done | bytes 12320 | tf_op jit(solution)/shard_map/ppermute | solution.py:511
  19.2 1.0 %carry.1 = (f32[8,8,128]{2,1,0:T(8,128)S(1)}, f32[1088,128]{1,0:T(8,128)S(1)}) custom-call(f32[24,128]{1,0:T(8,128)S(1)} %get-tuple-element.37.own_ref, f32[24,128]{1,0:T(8,128)S(1)} %collective-permute-done.1.other_ref, f32[128,8,128]{2,1,0:T(8,128)S(1)} %get-tuple-element.38.refs_0_, f32[128,8,128]{2,1,0:T(8,128)S(1)} %get-tuple-element.39.refs_1_, ...), custom_call_target="tpu_custom_call" | custom-call | tf_op jit(solution)/shard_map/carry/pallas_call | solution.py:442
  20.2 8.8 %all_to_all.11.power_ref = f32[8,8,128]{2,1,0:T(8,128)S(1)} all-to-all(f32[8,8,128]{2,1,0:T(8,128)S(1)} %get-tuple-element.46), channel_id=1, replica_groups={{5,0,1,2,3,4,6,7},{13,8,9,10,11,12,14,15},{21,16,17,18,19,20,22,23},{29..., dimensions={0} | all-to-all | bytes 65536 | tf_op jit(solution)/shard_map/all_to_all | solution.py:528
  28.9 1.0 %finish.1 = bf16[1024,128]{1,0:T(8,128)(2,1)} custom-call(f32[8,8,128]{2,1,0:T(8,128)S(1)} %all_to_all.11.power_ref, f32[1088,128]{1,0:T(8,128)S(1)} %get-tuple-element.47.gated_ref, f32[1,128]{1,0:T(1,128)S(1)} %get-tuple-element.48.gain_ref), custom_call_target="tpu_custom_call" | custom-call | tf_op jit(solution)/shard_map/finish/pallas_call | solution.py:442
  (1 shorter events, 0.0 us)
Async XLA Ops:
  2.0 1.3 %collective-permute-start = (f32[32,128]{1,0:T(8,128)S(1)}, f32[32,128]{1,0:T(8,128)S(1)}, u32[]{:S(2)}, u32[]{:S(2)}) collective-permute-start(f32[32,128]{1,0:T(8,128)S(1)} %get-tuple-element.27.own_ref), channel_id=1, source_target_pairs={{0,8},{8,0},{16,24},{24,16},{32,40},{40,32},{48,56},{56,48},{64,72... | collective-permute-start | bytes 49160 | tf_op jit(solution)/shard_map/ppermute | solution.py:472
  15.7 3.5 %collective-permute-start.1 = (f32[24,128]{1,0:T(8,128)S(1)}, f32[24,128]{1,0:T(8,128)S(1)}, u32[]{:S(2)}, u32[]{:S(2)}) collective-permute-start(f32[24,128]{1,0:T(8,128)S(1)} %get-tuple-element.37.own_ref), channel_id=1, source_target_pairs={{0,8},{8,0},{16,24},{24,16},{32,40},{40,32},{48,56},{56,48},{64,72... | collective-permute-start | bytes 36872 | tf_op jit(solution)/shard_map/ppermute | solution.py:511

commit v7 on v6

--- a/solution.py
+++ b/solution.py
@@ -461,8 +461,8 @@
         [
             pltpu.VMEM((positions, width), BF16),
             pltpu.VMEM((positions, width), BF16),
-            pltpu.VMEM((PITCH * CHUNKS, width), F32),
-            pltpu.VMEM((PITCH * CHUNKS, width), F32),
+            pltpu.VMEM((PITCH * (CHUNKS + 1), width), F32),
+            pltpu.VMEM((PITCH * (CHUNKS + 1), width), F32),
             pltpu.VMEM((3, modes, width), F32),
             pltpu.SemaphoreType.DMA((8,)),
         ],
@@ -471,7 +471,7 @@
     partners = [(i, i + 1 - 2 * (i % PAIR)) for i in range(ctx_count)]
     other = lax.ppermute(rows, "ctx", partners)
     params = (short_filter, decays, residues, skip)
-    pitched = pltpu.VMEM((PITCH * CHUNKS, width), F32)
+    pitched = pltpu.VMEM((PITCH * (CHUNKS + 1), width), F32)
     sent, joined, *early_locals = call(
         functools.partial(join_kernel, modes, "ctx"),
         "join",
@@ -496,7 +496,7 @@
         (enter_shape, *local_shapes),
         [VMEM] * 9,
         [
-            pltpu.VMEM(((pairs + 1) * (modes + EXTRA), width), F32),
+            pltpu.VMEM(((pairs + 2) * (modes + EXTRA), width), F32),
             pltpu.VMEM((pairs, width), F32),
             pltpu.VMEM((pairs, width), F32),
             pitched,
@@ -512,7 +512,7 @@
     power, gated = call(
         functools.partial(carry_kernel, modes, "ctx"),
         "carry",
-        (shape(tp_count, CHUNKS, run), shape(SPAN * CHUNKS, width)),
+        (shape(tp_count, CHUNKS, run), shape(SPAN * (CHUNKS + 1), width)),
         [VMEM] * 18,
         [pltpu.VMEM((modes + EDGE, width), F32), pitched],
         enter,

time: 30.3 us -> 30.3 us (level)
  no operation moved by 1% of the time
where the time goes in v7:
time: 30.3 us; the launch traced here: 30 us
  blocking collectives  19.6 us (65%)
  Pallas kernels  5.51 us (18%)
  starting transfers between devices  2.79 us (9%)
  waiting for transfers between devices  2 us (7%)
    all_to_all x1, blocking collectives, per_device(): lax.all_to_all(sent, ('ctx', 'tp'), split_axis=0, concat_axis=0, tiled=Tr...  10.8 us
    all_to_all x1, blocking collectives, per_device(): lax.all_to_all(power, 'tp', split_axis=0, concat_axis=0, tiled=True, axis...  8.77 us
    pallas_call x5, Pallas kernels, call(): pl.pallas_call(kernel, out_shape=out_shape, in_specs=in_specs, out_specs=...  5.51 us
    ppermute x1, starting transfers between devices, per_device(): entered = lax.ppermute(enter, 'ctx', partners)  2.69 us
    ppermute x1, waiting for transfers between devices, per_device(): other = lax.ppermute(rows, 'ctx', partners)  1.17 us
    ppermute x1, waiting for transfers between devices, per_device(): entered = lax.ppermute(enter, 'ctx', partners)  0.83 us
  transfers between devices with their start and end apart: 2, of which 2 were waited for; matrix products, arithmetic and copies ran while one was open for 0% of the time, Pallas kernels for 0%

profile of v7, /device:TPU:2, one launch (start us, length us, event | category | flops | bytes accessed | tf_op | source)
XLA Modules:
  0.0 30.0 jit_solution(14999163375698814458)
XLA Ops:
  0.0 2.0 %states.1 = (f32[32,128]{1,0:T(8,128)S(1)}, f32[128,8,128]{2,1,0:T(8,128)S(1)}, f32[16,8,128]{2,1,0:T(8,128)S(1)}, bf16[1024,128]{1,0:T(8,128)(2,1)S(1)}, f32[3,...) custom-call(bf16[3,1024,128]{2,1,0:T(8,128)(2,1)} %bitcast.3, ...), custom_call_target="tpu_custom_call" | custom-call | tf_op jit(solution)/shard_map/states/pallas_call | solution.py:442
  2.0 0.1 collective-permute-start
  2.1 1.2 %collective-permute-done.other_ref = f32[32,128]{1,0:T(8,128)S(1)} collective-permute-done((f32[32,128]{1,0:T(8,128)S(1)}, f32[32,128]{1,0:T(8,128)S(1)}, u32[]{:S(2)}, u32[]{:S(2)}) %collective-permute-start) | collective-permute-done | bytes 16416 | tf_op jit(solution)/shard_map/ppermute | solution.py:472
  3.2 1.6 %join.1 = (bf16[16,32,128]{2,1,0:T(8,128)(2,1)S(1)}, f32[2,32,128]{2,1,0:T(8,128)S(1)}, f32[128,8,128]{2,1,0:T(8,128)S(1)}, f32[128,8,128]{2,1,0:T(8,128)S(1)}, ...) custom-call(f32[32,128]{1,0:T(8,128)S(1)} %get-tuple-element.27.own_ref, ...), custom_call_target="tpu_custom_call" | custom-call | tf_op jit(solution)/shard_map/join/pallas_call | solution.py:442
  4.8 10.8 %all_to_all.10.received_ref = bf16[16,32,128]{2,1,0:T(8,128)(2,1)S(1)} all-to-all(bf16[16,32,128]{2,1,0:T(8,128)(2,1)S(1)} %get-tuple-element.35), channel_id=1, replica_groups={{168,8,72,200,24,56,136,88,120,216,248,40,152,184,104,232},{169,9,73,20..., dimensions={0} | all-to-all | bytes 262144 | tf_op jit(solution)/shard_map/all_to_all | solution.py:488
  15.7 2.7 %collective-permute-start.1 = (f32[24,128]{1,0:T(8,128)S(1)}, f32[24,128]{1,0:T(8,128)S(1)}, u32[]{:S(2)}, u32[]{:S(2)}) collective-permute-start(f32[24,128]{1,0:T(8,128)S(1)} %get-tuple-element.37.own_ref), channel_id=1, source_target_pairs={{0,8},{8,0},{16,24},{24,16},{32,40},{40,32},{48,56},{56,48},{64,72... | collective-permute-start | bytes 36872 | tf_op jit(solution)/shard_map/ppermute | solution.py:511
  18.4 0.8 %collective-permute-done.1.other_ref = f32[24,128]{1,0:T(8,128)S(1)} collective-permute-done((f32[24,128]{1,0:T(8,128)S(1)}, f32[24,128]{1,0:T(8,128)S(1)}, u32[]{:S(2)}, u32[]{:S(2)}) %collective-permute-start.1) | collective-permute-done | bytes 12320 | tf_op jit(solution)/shard_map/ppermute | solution.py:511
  19.2 1.0 %carry.1 = (f32[8,8,128]{2,1,0:T(8,128)S(1)}, f32[1224,128]{1,0:T(8,128)S(1)}) custom-call(f32[24,128]{1,0:T(8,128)S(1)} %get-tuple-element.37.own_ref, f32[24,128]{1,0:T(8,128)S(1)} %collective-permute-done.1.other_ref, f32[128,8,128]{2,1,0:T(8,128)S(1)} %get-tuple-element.38.refs_0_, f32[128,8,128]{2,1,0:T(8,128)S(1)} %get-tuple-element.39.refs_1_, ...), custom_call_target="tpu_custom_call" | custom-call | tf_op jit(solution)/shard_map/carry/pallas_call | solution.py:442
  20.2 8.8 %all_to_all.11.power_ref = f32[8,8,128]{2,1,0:T(8,128)S(1)} all-to-all(f32[8,8,128]{2,1,0:T(8,128)S(1)} %get-tuple-element.46), channel_id=1, replica_groups={{5,0,1,2,3,4,6,7},{13,8,9,10,11,12,14,15},{21,16,17,18,19,20,22,23},{29..., dimensions={0} | all-to-all | bytes 65536 | tf_op jit(solution)/shard_map/all_to_all | solution.py:528
  28.9 1.0 %finish.1 = bf16[1024,128]{1,0:T(8,128)(2,1)} custom-call(f32[8,8,128]{2,1,0:T(8,128)S(1)} %all_to_all.11.power_ref, f32[1224,128]{1,0:T(8,128)S(1)} %get-tuple-element.47.gated_ref, f32[1,128]{1,0:T(1,128)S(1)} %get-tuple-element.48.gain_ref), custom_call_target="tpu_custom_call" | custom-call | tf_op jit(solution)/shard_map/finish/pallas_call | solution.py:442
  (1 shorter events, 0.0 us)
Async XLA Ops:
  2.0 1.3 %collective-permute-start = (f32[32,128]{1,0:T(8,128)S(1)}, f32[32,128]{1,0:T(8,128)S(1)}, u32[]{:S(2)}, u32[]{:S(2)}) collective-permute-start(f32[32,128]{1,0:T(8,128)S(1)} %get-tuple-element.27.own_ref), channel_id=1, source_target_pairs={{0,8},{8,0},{16,24},{24,16},{32,40},{40,32},{48,56},{56,48},{64,72... | collective-permute-start | bytes 49160 | tf_op jit(solution)/shard_map/ppermute | solution.py:472
  15.7 3.5 %collective-permute-start.1 = (f32[24,128]{1,0:T(8,128)S(1)}, f32[24,128]{1,0:T(8,128)S(1)}, u32[]{:S(2)}, u32[]{:S(2)}) collective-permute-start(f32[24,128]{1,0:T(8,128)S(1)} %get-tuple-element.37.own_ref), channel_id=1, source_target_pairs={{0,8},{8,0},{16,24},{24,16},{32,40},{40,32},{48,56},{56,48},{64,72... | collective-permute-start | bytes 36872 | tf_op jit(solution)/shard_map/ppermute | solution.py:511

commit v8 on v7

--- a/solution.py
+++ b/solution.py
@@ -325,24 +325,40 @@
         enter_ref[modes + 4 :, :] = jnp.zeros((EDGE - 4, LANES), F32)
 
 
-def carry_kernel(
-    modes, axis, own_ref, other_ref, *refs
-):
-    early_locals, locals_, refs = refs[:4], refs[4:8], refs[8:]
-    q_half, product_ref, state_ref, pair_ref, taps_ref, decays_ref, residues_ref, skip_ref, *refs = refs
-    power_ref, gated_ref, enter_ref, q_ref = refs
-    run = product_ref.shape[0]
+def carry_kernel(modes, axis, half, *refs):
+    mine = lax.rem(lax.axis_index(axis), PAIR) == half
+    if half == 0:
+        *refs, power_in_ref, power_ref, gated_ref = refs
+
+        @pl.when(jnp.logical_not(mine))
+        def _():
+            power_ref[...] = power_in_ref[...]
+
+        refs = (*refs, power_ref, gated_ref)
+
+    @pl.when(mine)
+    def _():
+        carry_work(modes, axis, half, *refs)
+
+
+def carry_work(modes, axis, half, enter_ref, *refs):
+    early_locals, refs = refs[:4], refs[4:]
+    if half:
+        (q_half, product_ref, state_ref, pair_ref), refs = refs[:4], refs[4:]
+        taps_ref, decays_ref, residues_ref, skip_ref, power_ref, gated_ref, q_ref = refs
+    else:
+        locals_, refs = refs[:4], refs[4:]
+        taps_ref, decays_ref, residues_ref, skip_ref, power_ref, gated_ref = refs
+    run = early_locals[0].shape[0]
     positions = run * CHUNKS
-    upper = lax.rem(lax.axis_index(axis), PAIR) == 1
-    inside = lax.rem(lax.axis_index(axis), PAIR).astype(F32)
-    enter_ref[...] = jnp.where(upper, own_ref[...], other_ref[...])
     rates = decays_ref[...]
     state = enter_ref[:modes, :]
-    first, second, far, near = (enter_ref[modes + i : modes + i + 1, :] for i in range(4))
     weights = mode_weights(decays_ref, residues_ref)
-    lower = 1.0 - inside
-    edge = (lower * row for row in (first, second, far, near))
-    gate_more, base_more = edge_gains(taps_ref, skip_ref, rates, weights, *edge)
+    if half:
+        edges = from_lower(modes, axis, pair_ref, taps_ref, decays_ref, residues_ref, skip_ref)
+    else:
+        edge = (enter_ref[modes + i : modes + i + 1, :] for i in range(4))
+        gains = edge_gains(taps_ref, skip_ref, rates, weights, *edge)
     factors = split(jnp.exp(-rates))
 
     def put(j, gate, base, terms, more):
@@ -352,7 +368,7 @@
 
     def over_steps(step, held, gains, unroll):
         for j in range(2):
-            held = step(j, held, (gains[0][j], gains[1][j]))
+            held = step(j, held, gains and (gains[0][j], gains[1][j]))
         lax.fori_loop(2, run, lambda j, held: step(j, held, None), held, unroll=unroll)
 
     early = starts_early(axis)
@@ -364,23 +380,22 @@
             return carried
 
         carried = tuple(begin_ref[m] + reach_ref[m] * over_sublanes(state[m : m + 1, :]) for m in range(modes))
-        over_steps(step, carried, (gate_more, base_more), 14)
+        over_steps(step, carried, None if half else gains, 14)
 
     @pl.when(early)
     def _():
         from_local(*early_locals)
 
-    @pl.when(jnp.logical_not(jnp.logical_or(early, upper)))
+    @pl.when(jnp.logical_not(early))
     def _():
-        from_local(*locals_)
-
-    @pl.when(jnp.logical_and(upper, jnp.logical_not(early)))
-    def _():
+        if not half:
+            from_local(*locals_)
+            return
         taps, before = load_gate(q_ref, q_half, taps_ref)
         skip = over_sublanes(skip_ref[...])
         spread = split(weights)
-        arrived, gate_gain, base_gain = from_lower(modes, axis, pair_ref, taps_ref, decays_ref, residues_ref, skip_ref)
-        arrived = arrived + jnp.exp(-rates * (inside * float(positions))) * state
+        arrived, *more_gains = edges
+        arrived = arrived + jnp.exp(-rates * float(positions)) * state
         states = tuple(
             state_ref[m] + fades(decays_ref, run, m) * over_sublanes(arrived[m : m + 1, :]) for m in range(modes)
         )
@@ -394,8 +409,7 @@
             put(j, gate, skip * product, [w * h for w, h in zip(spread, states)], more)
             return q0, q1, states
 
-        gains = tuple([a + b for a, b in zip(*both)] for both in ((gate_gain, gate_more), (base_gain, base_more)))
-        over_steps(step, (*before, states), gains, 6)
+        over_steps(step, (*before, states), more_gains, 6)
 
     ones = jnp.ones((LANES, LANES), BF16)
     lane = lax.broadcasted_iota(jnp.int32, (CHUNKS, LANES), 1)
@@ -412,18 +426,24 @@
     power_ref[...] = jnp.broadcast_to(power[None], power_ref.shape)
 
 
-def finish_kernel(channels, power_ref, gated_ref, gain_ref, mixed_ref):
+def finish_kernel(channels, axis, power_ref, upper_ref, lower_ref, gain_ref, mixed_ref):
     run = mixed_ref.shape[0] // CHUNKS
     tiles = run // CHUNKS
     inverse = lax.rsqrt(jnp.sum(power_ref[...], 0) / channels + 1e-05)
     gain = over_sublanes(gain_ref[...])
-    for s in range(CHUNKS):
-        for i in range(0, tiles, 2):
-            halves = []
-            for h in (i, i + 1):
-                gated = gated_ref[s * SPAN + h * CHUNKS : s * SPAN + (h + 1) * CHUNKS, :]
-                halves.append(gated * gain * inverse[:, s * tiles + h : s * tiles + h + 1])
-            mixed_ref[s * run + i * CHUNKS : s * run + (i + 2) * CHUNKS, :] = jnp.concatenate(halves, 0).astype(BF16)
+
+    def scale(gated_ref):
+        for s in range(CHUNKS):
+            for i in range(0, tiles, 2):
+                halves = []
+                for h in (i, i + 1):
+                    gated = gated_ref[s * SPAN + h * CHUNKS : s * SPAN + (h + 1) * CHUNKS, :]
+                    halves.append(gated * gain * inverse[:, s * tiles + h : s * tiles + h + 1])
+                rows = slice(s * run + i * CHUNKS, s * run + (i + 2) * CHUNKS)
+                mixed_ref[rows, :] = jnp.concatenate(halves, 0).astype(BF16)
+
+    for half, ref in enumerate((lower_ref, upper_ref)):
+        pl.when(lax.rem(lax.axis_index(axis), PAIR) == half)(functools.partial(scale, ref))
 
 
 def per_device(projections, short_filter, residues, decays, skip, gain):
@@ -509,33 +529,45 @@
         *params,
     )
     entered = lax.ppermute(enter, "ctx", partners)
-    power, gated = call(
-        functools.partial(carry_kernel, modes, "ctx"),
-        "carry",
-        (shape(tp_count, CHUNKS, run), shape(SPAN * (CHUNKS + 1), width)),
-        [VMEM] * 18,
-        [pltpu.VMEM((modes + EDGE, width), F32), pitched],
+    carry_shapes = (shape(tp_count, CHUNKS, run), shape(SPAN * (CHUNKS + 1), width))
+    power, upper_gated = call(
+        functools.partial(carry_kernel, modes, "ctx", 1),
+        "upper",
+        carry_shapes,
+        [VMEM] * 13,
+        [pitched],
         enter,
-        entered,
         *early_locals,
-        *locals_,
         q,
         product,
         state,
         joined,
         *params,
     )
+    power, lower_gated = call(
+        functools.partial(carry_kernel, modes, "ctx", 0),
+        "lower",
+        carry_shapes,
+        [VMEM] * 14,
+        [],
+        entered,
+        *early_locals,
+        *locals_,
+        *params,
+        power,
+    )
     powers = lax.all_to_all(
         power, "tp", split_axis=0, concat_axis=0, tiled=True, axis_index_groups=[slice_order(tp_count)]
     )
     return call(
-        functools.partial(finish_kernel, width * tp_count),
+        functools.partial(finish_kernel, width * tp_count, "ctx"),
         "finish",
         shape(positions, width, kind=BF16),
-        [VMEM] * 3,
+        [VMEM] * 4,
         [],
         powers,
-        gated,
+        upper_gated,
+        lower_gated,
         gain,
     )
 

time: 30.3 us -> 30.1 us (level)
    pallas_call x5 -> x6, Pallas kernels: 5.51 us -> 5.48 us  [call(): pl.pallas_call(kernel, out_shape=out_shape, in_specs=in_specs, out_specs=...]
where the time goes in v8:
time: 30.1 us; the launch traced here: 29.9 us
  blocking collectives  19.6 us (65%)
  Pallas kernels  5.48 us (18%)
  starting transfers between devices  2.8 us (9%)
  waiting for transfers between devices  2 us (7%)
    all_to_all x1, blocking collectives, per_device(): lax.all_to_all(sent, ('ctx', 'tp'), split_axis=0, concat_axis=0, tiled=Tr...  10.8 us
    all_to_all x1, blocking collectives, per_device(): lax.all_to_all(power, 'tp', split_axis=0, concat_axis=0, tiled=True, axis...  8.78 us
    pallas_call x6, Pallas kernels, call(): pl.pallas_call(kernel, out_shape=out_shape, in_specs=in_specs, out_specs=...  5.48 us
    ppermute x1, starting transfers between devices, per_device(): entered = lax.ppermute(enter, 'ctx', partners)  2.71 us
    ppermute x1, waiting for transfers between devices, per_device(): other = lax.ppermute(rows, 'ctx', partners)  1.17 us
    ppermute x1, waiting for transfers between devices, per_device(): entered = lax.ppermute(enter, 'ctx', partners)  0.83 us
  transfers between devices with their start and end apart: 2, of which 2 were waited for; matrix products, arithmetic and copies ran while one was open for 0% of the time, Pallas kernels for 0%

profile of v8, /device:TPU:2, one launch (start us, length us, event | category | flops | bytes accessed | tf_op | source)
XLA Modules:
  0.0 29.9 jit_solution(18037199364355215255)
XLA Ops:
  0.0 2.0 %states.1 = (f32[32,128]{1,0:T(8,128)S(1)}, f32[128,8,128]{2,1,0:T(8,128)S(1)}, f32[16,8,128]{2,1,0:T(8,128)S(1)}, bf16[1024,128]{1,0:T(8,128)(2,1)S(1)}, f32[3,...) custom-call(bf16[3,1024,128]{2,1,0:T(8,128)(2,1)} %bitcast.3, ...), custom_call_target="tpu_custom_call" | custom-call | tf_op jit(solution)/shard_map/states/pallas_call | solution.py:462
  2.0 0.1 collective-permute-start
  2.1 1.2 %collective-permute-done.other_ref = f32[32,128]{1,0:T(8,128)S(1)} collective-permute-done((f32[32,128]{1,0:T(8,128)S(1)}, f32[32,128]{1,0:T(8,128)S(1)}, u32[]{:S(2)}, u32[]{:S(2)}) %collective-permute-start) | collective-permute-done | bytes 16416 | tf_op jit(solution)/shard_map/ppermute | solution.py:492
  3.2 1.6 %join.1 = (bf16[16,32,128]{2,1,0:T(8,128)(2,1)S(1)}, f32[2,32,128]{2,1,0:T(8,128)S(1)}, f32[128,8,128]{2,1,0:T(8,128)S(1)}, f32[128,8,128]{2,1,0:T(8,128)S(1)}, ...) custom-call(f32[32,128]{1,0:T(8,128)S(1)} %get-tuple-element.29.own_ref, ...), custom_call_target="tpu_custom_call" | custom-call | tf_op jit(solution)/shard_map/join/pallas_call | solution.py:462
  4.8 10.8 %all_to_all.10.received_ref = bf16[16,32,128]{2,1,0:T(8,128)(2,1)S(1)} all-to-all(bf16[16,32,128]{2,1,0:T(8,128)(2,1)S(1)} %get-tuple-element.37), channel_id=1, replica_groups={{168,8,72,200,24,56,136,88,120,216,248,40,152,184,104,232},{169,9,73,20..., dimensions={0} | all-to-all | bytes 262144 | tf_op jit(solution)/shard_map/all_to_all | solution.py:508
  15.7 2.7 %collective-permute-start.1 = (f32[24,128]{1,0:T(8,128)S(1)}, f32[24,128]{1,0:T(8,128)S(1)}, u32[]{:S(2)}, u32[]{:S(2)}) collective-permute-start(f32[24,128]{1,0:T(8,128)S(1)} %get-tuple-element.39.refs_0_), channel_id=1, source_target_pairs={{0,8},{8,0},{16,24},{24,16},{32,40},{40,32},{48,56},{56,48},{64,72... | collective-permute-start | bytes 36872 | tf_op jit(solution)/shard_map/ppermute | solution.py:531
  18.4 0.8 %collective-permute-done.1.refs_0_ = f32[24,128]{1,0:T(8,128)S(1)} collective-permute-done((f32[24,128]{1,0:T(8,128)S(1)}, f32[24,128]{1,0:T(8,128)S(1)}, u32[]{:S(2)}, u32[]{:S(2)}) %collective-permute-start.1) | collective-permute-done | bytes 12320 | tf_op jit(solution)/shard_map/ppermute | solution.py:531
  19.2 0.9 %lower.1 = (f32[8,8,128]{2,1,0:T(8,128)S(1)}, f32[1224,128]{1,0:T(8,128)S(1)}) custom-call(f32[24,128]{1,0:T(8,128)S(1)} %collective-permute-done.1.refs_0_, f32[128,8,128]{2,1,0:T(8,128)S(1)} %get-tuple-element.40.refs_1_, f32[128,8,128]{2,1,0:T(8,128)S(1)} %get-tuple-element.41.refs_2_, f32[16,8,128]{2,1,0:T(8,128)S(1)} %get-tuple-element.42.refs_3_, ...), custom_call_target="tpu_custom_call" | custom-call | tf_op jit(solution)/shard_map/lower/pallas_call | solution.py:462
  20.1 8.8 %all_to_all.11.power_ref = f32[8,8,128]{2,1,0:T(8,128)S(1)} all-to-all(f32[8,8,128]{2,1,0:T(8,128)S(1)} %get-tuple-element.49), channel_id=1, replica_groups={{5,0,1,2,3,4,6,7},{13,8,9,10,11,12,14,15},{21,16,17,18,19,20,22,23},{29..., dimensions={0} | all-to-all | bytes 65536 | tf_op jit(solution)/shard_map/all_to_all | solution.py:559
  28.9 1.0 %finish.1 = bf16[1024,128]{1,0:T(8,128)(2,1)} custom-call(f32[8,8,128]{2,1,0:T(8,128)S(1)} %all_to_all.11.power_ref, f32[1224,128]{1,0:T(8,128)S(1)} %get-tuple-element.50.upper_ref, f32[1224,128]{1,0:T(8,128)S(1)} %get-tuple-element.51.lower_ref, f32[1,128]{1,0:T(1,128)S(1)} %get-tuple-element.52.gain_ref), custom_call_target="tpu_custom_call" | custom-call | tf_op jit(solution)/shard_map/finish/pallas_call | solution.py:462
  (2 shorter events, 0.0 us)
Async XLA Ops:
  2.0 1.3 %collective-permute-start = (f32[32,128]{1,0:T(8,128)S(1)}, f32[32,128]{1,0:T(8,128)S(1)}, u32[]{:S(2)}, u32[]{:S(2)}) collective-permute-start(f32[32,128]{1,0:T(8,128)S(1)} %get-tuple-element.29.own_ref), channel_id=1, source_target_pairs={{0,8},{8,0},{16,24},{24,16},{32,40},{40,32},{48,56},{56,48},{64,72... | collective-permute-start | bytes 49160 | tf_op jit(solution)/shard_map/ppermute | solution.py:492
  15.7 3.5 %collective-permute-start.1 = (f32[24,128]{1,0:T(8,128)S(1)}, f32[24,128]{1,0:T(8,128)S(1)}, u32[]{:S(2)}, u32[]{:S(2)}) collective-permute-start(f32[24,128]{1,0:T(8,128)S(1)} %get-tuple-element.39.refs_0_), channel_id=1, source_target_pairs={{0,8},{8,0},{16,24},{24,16},{32,40},{40,32},{48,56},{56,48},{64,72... | collective-permute-start | bytes 36872 | tf_op jit(solution)/shard_map/ppermute | solution.py:531

commit v9 on v8

--- a/solution.py
+++ b/solution.py
@@ -380,7 +380,7 @@
             return carried
 
         carried = tuple(begin_ref[m] + reach_ref[m] * over_sublanes(state[m : m + 1, :]) for m in range(modes))
-        over_steps(step, carried, None if half else gains, 14)
+        over_steps(step, carried, None if half else gains, 42)
 
     @pl.when(early)
     def _():
@@ -418,9 +418,7 @@
     for s in range(CHUNKS):
         gated = gated_ref[s * SPAN : s * SPAN + run, :]
         square = gated * gated
-        high = square.astype(BF16)
-        low = (square - high.astype(F32)).astype(BF16)
-        sums = jnp.dot(high, ones, preferred_element_type=F32) + jnp.dot(low, ones, preferred_element_type=F32)
+        sums = jnp.dot(square.astype(BF16), ones, preferred_element_type=F32)
         for i in range(tiles):
             power = jnp.where(lane == s * tiles + i, sums[i * CHUNKS : (i + 1) * CHUNKS, :], power)
     power_ref[...] = jnp.broadcast_to(power[None], power_ref.shape)

time: 30.1 us -> 30 us (level)
  no operation moved by 1% of the time
where the time goes in v9:
time: 30 us; the launch traced here: 29.8 us
  blocking collectives  19.6 us (65%)
  Pallas kernels  5.38 us (18%)
  starting transfers between devices  2.8 us (9%)
  waiting for transfers between devices  2 us (7%)
    all_to_all x1, blocking collectives, per_device(): lax.all_to_all(sent, ('ctx', 'tp'), split_axis=0, concat_axis=0, tiled=Tr...  10.8 us
    all_to_all x1, blocking collectives, per_device(): lax.all_to_all(power, 'tp', split_axis=0, concat_axis=0, tiled=True, axis...  8.77 us
    pallas_call x6, Pallas kernels, call(): pl.pallas_call(kernel, out_shape=out_shape, in_specs=in_specs, out_specs=...  5.38 us
    ppermute x1, starting transfers between devices, per_device(): entered = lax.ppermute(enter, 'ctx', partners)  2.71 us
    ppermute x1, waiting for transfers between devices, per_device(): other = lax.ppermute(rows, 'ctx', partners)  1.17 us
    ppermute x1, waiting for transfers between devices, per_device(): entered = lax.ppermute(enter, 'ctx', partners)  0.83 us
  transfers between devices with their start and end apart: 2, of which 2 were waited for; matrix products, arithmetic and copies ran while one was open for 0% of the time, Pallas kernels for 0%

profile of v9, /device:TPU:2, one launch (start us, length us, event | category | flops | bytes accessed | tf_op | source)
XLA Modules:
  0.0 29.8 jit_solution(15203361875388728336)
XLA Ops:
  0.0 2.0 %states.1 = (f32[32,128]{1,0:T(8,128)S(1)}, f32[128,8,128]{2,1,0:T(8,128)S(1)}, f32[16,8,128]{2,1,0:T(8,128)S(1)}, bf16[1024,128]{1,0:T(8,128)(2,1)S(1)}, f32[3,...) custom-call(bf16[3,1024,128]{2,1,0:T(8,128)(2,1)} %bitcast.3, ...), custom_call_target="tpu_custom_call" | custom-call | tf_op jit(solution)/shard_map/states/pallas_call | solution.py:460
  2.0 0.1 collective-permute-start
  2.1 1.2 %collective-permute-done.other_ref = f32[32,128]{1,0:T(8,128)S(1)} collective-permute-done((f32[32,128]{1,0:T(8,128)S(1)}, f32[32,128]{1,0:T(8,128)S(1)}, u32[]{:S(2)}, u32[]{:S(2)}) %collective-permute-start) | collective-permute-done | bytes 16416 | tf_op jit(solution)/shard_map/ppermute | solution.py:490
  3.2 1.6 %join.1 = (bf16[16,32,128]{2,1,0:T(8,128)(2,1)S(1)}, f32[2,32,128]{2,1,0:T(8,128)S(1)}, f32[128,8,128]{2,1,0:T(8,128)S(1)}, f32[128,8,128]{2,1,0:T(8,128)S(1)}, ...) custom-call(f32[32,128]{1,0:T(8,128)S(1)} %get-tuple-element.29.own_ref, ...), custom_call_target="tpu_custom_call" | custom-call | tf_op jit(solution)/shard_map/join/pallas_call | solution.py:460
  4.8 10.8 %all_to_all.10.received_ref = bf16[16,32,128]{2,1,0:T(8,128)(2,1)S(1)} all-to-all(bf16[16,32,128]{2,1,0:T(8,128)(2,1)S(1)} %get-tuple-element.37), channel_id=1, replica_groups={{168,8,72,200,24,56,136,88,120,216,248,40,152,184,104,232},{169,9,73,20..., dimensions={0} | all-to-all | bytes 262144 | tf_op jit(solution)/shard_map/all_to_all | solution.py:506
  15.7 2.7 %collective-permute-start.1 = (f32[24,128]{1,0:T(8,128)S(1)}, f32[24,128]{1,0:T(8,128)S(1)}, u32[]{:S(2)}, u32[]{:S(2)}) collective-permute-start(f32[24,128]{1,0:T(8,128)S(1)} %get-tuple-element.39.refs_0_), channel_id=1, source_target_pairs={{0,8},{8,0},{16,24},{24,16},{32,40},{40,32},{48,56},{56,48},{64,72... | collective-permute-start | bytes 36872 | tf_op jit(solution)/shard_map/ppermute | solution.py:529
  18.4 0.8 %collective-permute-done.1.refs_0_ = f32[24,128]{1,0:T(8,128)S(1)} collective-permute-done((f32[24,128]{1,0:T(8,128)S(1)}, f32[24,128]{1,0:T(8,128)S(1)}, u32[]{:S(2)}, u32[]{:S(2)}) %collective-permute-start.1) | collective-permute-done | bytes 12320 | tf_op jit(solution)/shard_map/ppermute | solution.py:529
  19.2 0.8 %lower.1 = (f32[8,8,128]{2,1,0:T(8,128)S(1)}, f32[1224,128]{1,0:T(8,128)S(1)}) custom-call(f32[24,128]{1,0:T(8,128)S(1)} %collective-permute-done.1.refs_0_, f32[128,8,128]{2,1,0:T(8,128)S(1)} %get-tuple-element.40.refs_1_, f32[128,8,128]{2,1,0:T(8,128)S(1)} %get-tuple-element.41.refs_2_, f32[16,8,128]{2,1,0:T(8,128)S(1)} %get-tuple-element.42.refs_3_, ...), custom_call_target="tpu_custom_call" | custom-call | tf_op jit(solution)/shard_map/lower/pallas_call | solution.py:460
  20.0 8.8 %all_to_all.11.power_ref = f32[8,8,128]{2,1,0:T(8,128)S(1)} all-to-all(f32[8,8,128]{2,1,0:T(8,128)S(1)} %get-tuple-element.49), channel_id=1, replica_groups={{5,0,1,2,3,4,6,7},{13,8,9,10,11,12,14,15},{21,16,17,18,19,20,22,23},{29..., dimensions={0} | all-to-all | bytes 65536 | tf_op jit(solution)/shard_map/all_to_all | solution.py:557
  28.8 1.0 %finish.1 = bf16[1024,128]{1,0:T(8,128)(2,1)} custom-call(f32[8,8,128]{2,1,0:T(8,128)S(1)} %all_to_all.11.power_ref, f32[1224,128]{1,0:T(8,128)S(1)} %get-tuple-element.50.upper_ref, f32[1224,128]{1,0:T(8,128)S(1)} %get-tuple-element.51.lower_ref, f32[1,128]{1,0:T(1,128)S(1)} %get-tuple-element.52.gain_ref), custom_call_target="tpu_custom_call" | custom-call | tf_op jit(solution)/shard_map/finish/pallas_call | solution.py:460
  (2 shorter events, 0.0 us)
Async XLA Ops:
  2.0 1.3 %collective-permute-start = (f32[32,128]{1,0:T(8,128)S(1)}, f32[32,128]{1,0:T(8,128)S(1)}, u32[]{:S(2)}, u32[]{:S(2)}) collective-permute-start(f32[32,128]{1,0:T(8,128)S(1)} %get-tuple-element.29.own_ref), channel_id=1, source_target_pairs={{0,8},{8,0},{16,24},{24,16},{32,40},{40,32},{48,56},{56,48},{64,72... | collective-permute-start | bytes 49160 | tf_op jit(solution)/shard_map/ppermute | solution.py:490
  15.7 3.5 %collective-permute-start.1 = (f32[24,128]{1,0:T(8,128)S(1)}, f32[24,128]{1,0:T(8,128)S(1)}, u32[]{:S(2)}, u32[]{:S(2)}) collective-permute-start(f32[24,128]{1,0:T(8,128)S(1)} %get-tuple-element.39.refs_0_), channel_id=1, source_target_pairs={{0,8},{8,0},{16,24},{24,16},{32,40},{40,32},{48,56},{56,48},{64,72... | collective-permute-start | bytes 36872 | tf_op jit(solution)/shard_map/ppermute | solution.py:529

commit v10 on v9

--- a/solution.py
+++ b/solution.py
@@ -179,8 +179,12 @@
     return residues_ref[...] * jnp.sqrt(2.0 * decays_ref[...])
 
 
-def edge_gains(taps_ref, skip_ref, rates, weights, first, second, far, near):
-    early = jnp.sum(weights * jnp.exp(rates), 0, keepdims=True) * second
+def early_weight(decays_ref, residues_ref):
+    return jnp.sum(mode_weights(decays_ref, residues_ref) * jnp.exp(decays_ref[...]), 0, keepdims=True)
+
+
+def edge_gains(taps_ref, skip_ref, weight, first, second, far, near):
+    early = weight * second
     skip = skip_ref[...]
     gate = (taps_ref[0, 1:2, :] * near + taps_ref[0, 2:3, :] * far, taps_ref[0, 2:3, :] * near)
     return gate, (skip * first - early, skip * second)
@@ -192,8 +196,8 @@
     first, second = (inside * p for p in pair_boundary(modes, taps_ref, pair_ref.at[0], pair_ref.at[1]))
     state = inside * pair_ref[0, :modes, :] + jnp.exp(rates) * first + jnp.exp(2.0 * rates) * second
     far, near = (inside * row for row in two_rows(pair_ref.at[0], modes + Q_LAST))
-    weights = mode_weights(decays_ref, residues_ref)
-    return state, *edge_gains(taps_ref, skip_ref, rates, weights, first, second, far, near)
+    weight = early_weight(decays_ref, residues_ref)
+    return state, *edge_gains(taps_ref, skip_ref, weight, first, second, far, near)
 
 
 def at_top(block, row):
@@ -290,6 +294,11 @@
         local_work(modes, axis, q_half, product_ref, state_ref, pair_ref, *params, *local_refs, q_ref)
 
     enter_ref[...] = jnp.zeros_like(enter_ref)
+
+    @pl.when(jnp.logical_not(upper))
+    def _():
+        enter_ref[:modes, :] = jnp.exp(-decays_ref[...])
+        enter_ref[modes : modes + 1, :] = early_weight(decays_ref, residues_ref)
 
     @pl.when(upper)
     def _():
@@ -347,19 +356,20 @@
         (q_half, product_ref, state_ref, pair_ref), refs = refs[:4], refs[4:]
         taps_ref, decays_ref, residues_ref, skip_ref, power_ref, gated_ref, q_ref = refs
     else:
-        locals_, refs = refs[:4], refs[4:]
+        (table_ref, *locals_), refs = refs[:5], refs[5:]
         taps_ref, decays_ref, residues_ref, skip_ref, power_ref, gated_ref = refs
     run = early_locals[0].shape[0]
     positions = run * CHUNKS
     rates = decays_ref[...]
     state = enter_ref[:modes, :]
-    weights = mode_weights(decays_ref, residues_ref)
     if half:
+        weights = mode_weights(decays_ref, residues_ref)
         edges = from_lower(modes, axis, pair_ref, taps_ref, decays_ref, residues_ref, skip_ref)
+        factors = split(jnp.exp(-rates))
     else:
         edge = (enter_ref[modes + i : modes + i + 1, :] for i in range(4))
-        gains = edge_gains(taps_ref, skip_ref, rates, weights, *edge)
-    factors = split(jnp.exp(-rates))
+        gains = edge_gains(taps_ref, skip_ref, table_ref[modes : modes + 1, :], *edge)
+        factors = split(table_ref[:modes, :])
 
     def put(j, gate, base, terms, more):
         if more is not None:
@@ -546,10 +556,11 @@
         functools.partial(carry_kernel, modes, "ctx", 0),
         "lower",
         carry_shapes,
-        [VMEM] * 14,
+        [VMEM] * 15,
         [],
         entered,
         *early_locals,
+        enter,
         *locals_,
         *params,
         power,

time: 30 us -> 30 us (level)
  no operation moved by 1% of the time
where the time goes in v10:
time: 30 us; the launch traced here: 29.8 us
  blocking collectives  19.6 us (65%)
  Pallas kernels  5.38 us (18%)
  starting transfers between devices  2.78 us (9%)
  waiting for transfers between devices  2 us (7%)
    all_to_all x1, blocking collectives, per_device(): lax.all_to_all(sent, ('ctx', 'tp'), split_axis=0, concat_axis=0, tiled=Tr...  10.8 us
    all_to_all x1, blocking collectives, per_device(): lax.all_to_all(power, 'tp', split_axis=0, concat_axis=0, tiled=True, axis...  8.78 us
    pallas_call x6, Pallas kernels, call(): pl.pallas_call(kernel, out_shape=out_shape, in_specs=in_specs, out_specs=...  5.38 us
    ppermute x1, starting transfers between devices, per_device(): entered = lax.ppermute(enter, 'ctx', partners)  2.69 us
    ppermute x1, waiting for transfers between devices, per_device(): other = lax.ppermute(rows, 'ctx', partners)  1.17 us
    ppermute x1, waiting for transfers between devices, per_device(): entered = lax.ppermute(enter, 'ctx', partners)  0.83 us
  transfers between devices with their start and end apart: 2, of which 2 were waited for; matrix products, arithmetic and copies ran while one was open for 0% of the time, Pallas kernels for 0%

profile of v10, /device:TPU:2, one launch (start us, length us, event | category | flops | bytes accessed | tf_op | source)
XLA Modules:
  0.0 29.8 jit_solution(17682925570883597355)
XLA Ops:
  0.0 2.0 %states.1 = (f32[32,128]{1,0:T(8,128)S(1)}, f32[128,8,128]{2,1,0:T(8,128)S(1)}, f32[16,8,128]{2,1,0:T(8,128)S(1)}, bf16[1024,128]{1,0:T(8,128)(2,1)S(1)}, f32[3,...) custom-call(bf16[3,1024,128]{2,1,0:T(8,128)(2,1)} %bitcast.3, ...), custom_call_target="tpu_custom_call" | custom-call | tf_op jit(solution)/shard_map/states/pallas_call | solution.py:470
  2.0 0.1 collective-permute-start
  2.1 1.2 %collective-permute-done.other_ref = f32[32,128]{1,0:T(8,128)S(1)} collective-permute-done((f32[32,128]{1,0:T(8,128)S(1)}, f32[32,128]{1,0:T(8,128)S(1)}, u32[]{:S(2)}, u32[]{:S(2)}) %collective-permute-start) | collective-permute-done | bytes 16416 | tf_op jit(solution)/shard_map/ppermute | solution.py:500
  3.2 1.6 %join.1 = (bf16[16,32,128]{2,1,0:T(8,128)(2,1)S(1)}, f32[2,32,128]{2,1,0:T(8,128)S(1)}, f32[128,8,128]{2,1,0:T(8,128)S(1)}, f32[128,8,128]{2,1,0:T(8,128)S(1)}, ...) custom-call(f32[32,128]{1,0:T(8,128)S(1)} %get-tuple-element.29.own_ref, ...), custom_call_target="tpu_custom_call" | custom-call | tf_op jit(solution)/shard_map/join/pallas_call | solution.py:470
  4.8 10.8 %all_to_all.10.received_ref = bf16[16,32,128]{2,1,0:T(8,128)(2,1)S(1)} all-to-all(bf16[16,32,128]{2,1,0:T(8,128)(2,1)S(1)} %get-tuple-element.37), channel_id=1, replica_groups={{168,8,72,200,24,56,136,88,120,216,248,40,152,184,104,232},{169,9,73,20..., dimensions={0} | all-to-all | bytes 262144 | tf_op jit(solution)/shard_map/all_to_all | solution.py:516
  15.7 2.7 %collective-permute-start.1 = (f32[24,128]{1,0:T(8,128)S(1)}, f32[24,128]{1,0:T(8,128)S(1)}, u32[]{:S(2)}, u32[]{:S(2)}) collective-permute-start(f32[24,128]{1,0:T(8,128)S(1)} %get-tuple-element.39.refs_0_.refs_5_), channel_id=1, source_target_pairs={{0,8},{8,0},{16,24},{24,16},{32,40},{40,32},{48,56},{56,48},{64,72... | collective-permute-start | bytes 36872 | tf_op jit(solution)/shard_map/ppermute | solution.py:539
  18.4 0.8 %collective-permute-done.1.refs_0_ = f32[24,128]{1,0:T(8,128)S(1)} collective-permute-done((f32[24,128]{1,0:T(8,128)S(1)}, f32[24,128]{1,0:T(8,128)S(1)}, u32[]{:S(2)}, u32[]{:S(2)}) %collective-permute-start.1) | collective-permute-done | bytes 12320 | tf_op jit(solution)/shard_map/ppermute | solution.py:539
  19.2 0.8 %lower.1 = (f32[8,8,128]{2,1,0:T(8,128)S(1)}, f32[1224,128]{1,0:T(8,128)S(1)}) custom-call(f32[24,128]{1,0:T(8,128)S(1)} %collective-permute-done.1.refs_0_, f32[128,8,128]{2,1,0:T(8,128)S(1)} %get-tuple-element.40.refs_1_, f32[128,8,128]{2,1,0:T(8,128)S(1)} %get-tuple-element.41.refs_2_, f32[16,8,128]{2,1,0:T(8,128)S(1)} %get-tuple-element.42.refs_3_, ...), custom_call_target="tpu_custom_call" | custom-call | tf_op jit(solution)/shard_map/lower/pallas_call | solution.py:470
  20.0 8.8 %all_to_all.11.power_ref = f32[8,8,128]{2,1,0:T(8,128)S(1)} all-to-all(f32[8,8,128]{2,1,0:T(8,128)S(1)} %get-tuple-element.49), channel_id=1, replica_groups={{5,0,1,2,3,4,6,7},{13,8,9,10,11,12,14,15},{21,16,17,18,19,20,22,23},{29..., dimensions={0} | all-to-all | bytes 65536 | tf_op jit(solution)/shard_map/all_to_all | solution.py:568
  28.8 1.0 %finish.1 = bf16[1024,128]{1,0:T(8,128)(2,1)} custom-call(f32[8,8,128]{2,1,0:T(8,128)S(1)} %all_to_all.11.power_ref, f32[1224,128]{1,0:T(8,128)S(1)} %get-tuple-element.50.upper_ref, f32[1224,128]{1,0:T(8,128)S(1)} %get-tuple-element.51.lower_ref, f32[1,128]{1,0:T(1,128)S(1)} %get-tuple-element.52.gain_ref), custom_call_target="tpu_custom_call" | custom-call | tf_op jit(solution)/shard_map/finish/pallas_call | solution.py:470
  (2 shorter events, 0.0 us)
Async XLA Ops:
  2.0 1.3 %collective-permute-start = (f32[32,128]{1,0:T(8,128)S(1)}, f32[32,128]{1,0:T(8,128)S(1)}, u32[]{:S(2)}, u32[]{:S(2)}) collective-permute-start(f32[32,128]{1,0:T(8,128)S(1)} %get-tuple-element.29.own_ref), channel_id=1, source_target_pairs={{0,8},{8,0},{16,24},{24,16},{32,40},{40,32},{48,56},{56,48},{64,72... | collective-permute-start | bytes 49160 | tf_op jit(solution)/shard_map/ppermute | solution.py:500
  15.7 3.5 %collective-permute-start.1 = (f32[24,128]{1,0:T(8,128)S(1)}, f32[24,128]{1,0:T(8,128)S(1)}, u32[]{:S(2)}, u32[]{:S(2)}) collective-permute-start(f32[24,128]{1,0:T(8,128)S(1)} %get-tuple-element.39.refs_0_.refs_5_), channel_id=1, source_target_pairs={{0,8},{8,0},{16,24},{24,16},{32,40},{40,32},{48,56},{56,48},{64,72... | collective-permute-start | bytes 36872 | tf_op jit(solution)/shard_map/ppermute | solution.py:539

commit v11 on v9

--- a/solution.py
+++ b/solution.py
@@ -424,13 +424,14 @@
     power_ref[...] = jnp.broadcast_to(power[None], power_ref.shape)
 
 
-def finish_kernel(channels, axis, power_ref, upper_ref, lower_ref, gain_ref, mixed_ref):
+def finish_kernel(channels, axis, power_ref, upper_ref, lower_ref, gain_ref, mixed_hbm, mixed_ref, semaphores):
     run = mixed_ref.shape[0] // CHUNKS
     tiles = run // CHUNKS
     inverse = lax.rsqrt(jnp.sum(power_ref[...], 0) / channels + 1e-05)
     gain = over_sublanes(gain_ref[...])
 
     def scale(gated_ref):
+        copies = []
         for s in range(CHUNKS):
             for i in range(0, tiles, 2):
                 halves = []
@@ -439,6 +440,12 @@
                     halves.append(gated * gain * inverse[:, s * tiles + h : s * tiles + h + 1])
                 rows = slice(s * run + i * CHUNKS, s * run + (i + 2) * CHUNKS)
                 mixed_ref[rows, :] = jnp.concatenate(halves, 0).astype(BF16)
+            if s % 2:
+                part = pl.ds((s - 1) * run, 2 * run)
+                copies.append(pltpu.make_async_copy(mixed_ref.at[part], mixed_hbm.at[part], semaphores.at[s // 2]))
+                copies[-1].start()
+        for copy in copies:
+            copy.wait()
 
     for half, ref in enumerate((lower_ref, upper_ref)):
         pl.when(lax.rem(lax.axis_index(axis), PAIR) == half)(functools.partial(scale, ref))
@@ -456,12 +463,12 @@
     def shape(*extent, kind=F32):
         return jax.ShapeDtypeStruct(extent, kind)
 
-    def call(kernel, name, out_shape, in_specs, scratch, *operands):
+    def call(kernel, name, out_shape, in_specs, scratch, *operands, out_specs=None):
         return pl.pallas_call(
             kernel,
             out_shape=out_shape,
             in_specs=in_specs,
-            out_specs=jax.tree.map(lambda _: VMEM, out_shape),
+            out_specs=out_specs or jax.tree.map(lambda _: VMEM, out_shape),
             scratch_shapes=scratch,
             compiler_params=pltpu.CompilerParams(vmem_limit_bytes=VMEM_LIMIT),
             name=name,
@@ -562,11 +569,12 @@
         "finish",
         shape(positions, width, kind=BF16),
         [VMEM] * 4,
-        [],
+        [pltpu.VMEM((positions, width), BF16), pltpu.SemaphoreType.DMA((CHUNKS // 2,))],
         powers,
         upper_gated,
         lower_gated,
         gain,
+        out_specs=ANY,
     )
 
 

time: 30 us -> 30 us (level)
  no operation moved by 1% of the time
where the time goes in v11:
time: 30 us; the launch traced here: 29.8 us
  blocking collectives  19.6 us (65%)
  Pallas kernels  5.34 us (18%)
  starting transfers between devices  2.8 us (9%)
  waiting for transfers between devices  2 us (7%)
    all_to_all x1, blocking collectives, per_device(): lax.all_to_all(sent, ('ctx', 'tp'), split_axis=0, concat_axis=0, tiled=Tr...  10.8 us
    all_to_all x1, blocking collectives, per_device(): lax.all_to_all(power, 'tp', split_axis=0, concat_axis=0, tiled=True, axis...  8.77 us
    pallas_call x6, Pallas kernels, call(): pl.pallas_call(kernel, out_shape=out_shape, in_specs=in_specs, out_specs=...  5.34 us
    ppermute x1, starting transfers between devices, per_device(): entered = lax.ppermute(enter, 'ctx', partners)  2.71 us
    ppermute x1, waiting for transfers between devices, per_device(): other = lax.ppermute(rows, 'ctx', partners)  1.17 us
    ppermute x1, waiting for transfers between devices, per_device(): entered = lax.ppermute(enter, 'ctx', partners)  0.83 us
  transfers between devices with their start and end apart: 2, of which 2 were waited for; matrix products, arithmetic and copies ran while one was open for 0% of the time, Pallas kernels for 0%

profile of v11, /device:TPU:2, one launch (start us, length us, event | category | flops | bytes accessed | tf_op | source)
XLA Modules:
  0.0 29.8 jit_solution(10847958097818323524)
XLA Ops:
  0.0 2.0 %states.1 = (f32[32,128]{1,0:T(8,128)S(1)}, f32[128,8,128]{2,1,0:T(8,128)S(1)}, f32[16,8,128]{2,1,0:T(8,128)S(1)}, bf16[1024,128]{1,0:T(8,128)(2,1)S(1)}, f32[3,...) custom-call(bf16[3,1024,128]{2,1,0:T(8,128)(2,1)} %bitcast.3, ...), custom_call_target="tpu_custom_call" | custom-call | tf_op jit(solution)/shard_map/states/pallas_call | solution.py:467
  2.0 0.1 collective-permute-start
  2.1 1.2 %collective-permute-done.other_ref = f32[32,128]{1,0:T(8,128)S(1)} collective-permute-done((f32[32,128]{1,0:T(8,128)S(1)}, f32[32,128]{1,0:T(8,128)S(1)}, u32[]{:S(2)}, u32[]{:S(2)}) %collective-permute-start) | collective-permute-done | bytes 16416 | tf_op jit(solution)/shard_map/ppermute | solution.py:497
  3.2 1.6 %join.1 = (bf16[16,32,128]{2,1,0:T(8,128)(2,1)S(1)}, f32[2,32,128]{2,1,0:T(8,128)S(1)}, f32[128,8,128]{2,1,0:T(8,128)S(1)}, f32[128,8,128]{2,1,0:T(8,128)S(1)}, ...) custom-call(f32[32,128]{1,0:T(8,128)S(1)} %get-tuple-element.29.own_ref, ...), custom_call_target="tpu_custom_call" | custom-call | tf_op jit(solution)/shard_map/join/pallas_call | solution.py:467
  4.8 10.8 %all_to_all.10.received_ref = bf16[16,32,128]{2,1,0:T(8,128)(2,1)S(1)} all-to-all(bf16[16,32,128]{2,1,0:T(8,128)(2,1)S(1)} %get-tuple-element.37), channel_id=1, replica_groups={{168,8,72,200,24,56,136,88,120,216,248,40,152,184,104,232},{169,9,73,20..., dimensions={0} | all-to-all | bytes 262144 | tf_op jit(solution)/shard_map/all_to_all | solution.py:513
  15.7 2.7 %collective-permute-start.1 = (f32[24,128]{1,0:T(8,128)S(1)}, f32[24,128]{1,0:T(8,128)S(1)}, u32[]{:S(2)}, u32[]{:S(2)}) collective-permute-start(f32[24,128]{1,0:T(8,128)S(1)} %get-tuple-element.39.refs_0_), channel_id=1, source_target_pairs={{0,8},{8,0},{16,24},{24,16},{32,40},{40,32},{48,56},{56,48},{64,72... | collective-permute-start | bytes 36872 | tf_op jit(solution)/shard_map/ppermute | solution.py:536
  18.4 0.8 %collective-permute-done.1.refs_0_ = f32[24,128]{1,0:T(8,128)S(1)} collective-permute-done((f32[24,128]{1,0:T(8,128)S(1)}, f32[24,128]{1,0:T(8,128)S(1)}, u32[]{:S(2)}, u32[]{:S(2)}) %collective-permute-start.1) | collective-permute-done | bytes 12320 | tf_op jit(solution)/shard_map/ppermute | solution.py:536
  19.2 0.8 %lower.1 = (f32[8,8,128]{2,1,0:T(8,128)S(1)}, f32[1224,128]{1,0:T(8,128)S(1)}) custom-call(f32[24,128]{1,0:T(8,128)S(1)} %collective-permute-done.1.refs_0_, f32[128,8,128]{2,1,0:T(8,128)S(1)} %get-tuple-element.40.refs_1_, f32[128,8,128]{2,1,0:T(8,128)S(1)} %get-tuple-element.41.refs_2_, f32[16,8,128]{2,1,0:T(8,128)S(1)} %get-tuple-element.42.refs_3_, ...), custom_call_target="tpu_custom_call" | custom-call | tf_op jit(solution)/shard_map/lower/pallas_call | solution.py:467
  20.0 8.8 %all_to_all.11.power_ref = f32[8,8,128]{2,1,0:T(8,128)S(1)} all-to-all(f32[8,8,128]{2,1,0:T(8,128)S(1)} %get-tuple-element.49), channel_id=1, replica_groups={{5,0,1,2,3,4,6,7},{13,8,9,10,11,12,14,15},{21,16,17,18,19,20,22,23},{29..., dimensions={0} | all-to-all | bytes 65536 | tf_op jit(solution)/shard_map/all_to_all | solution.py:564
  28.8 1.0 %finish.1 = bf16[1024,128]{1,0:T(8,128)(2,1)} custom-call(f32[8,8,128]{2,1,0:T(8,128)S(1)} %all_to_all.11.power_ref, f32[1224,128]{1,0:T(8,128)S(1)} %get-tuple-element.50.upper_ref, f32[1224,128]{1,0:T(8,128)S(1)} %get-tuple-element.51.lower_ref, f32[1,128]{1,0:T(1,128)S(1)} %get-tuple-element.52.gain_ref), custom_call_target="tpu_custom_call" | custom-call | tf_op jit(solution)/shard_map/finish/pallas_call | solution.py:467
  (2 shorter events, 0.0 us)
Async XLA Ops:
  2.0 1.3 %collective-permute-start = (f32[32,128]{1,0:T(8,128)S(1)}, f32[32,128]{1,0:T(8,128)S(1)}, u32[]{:S(2)}, u32[]{:S(2)}) collective-permute-start(f32[32,128]{1,0:T(8,128)S(1)} %get-tuple-element.29.own_ref), channel_id=1, source_target_pairs={{0,8},{8,0},{16,24},{24,16},{32,40},{40,32},{48,56},{56,48},{64,72... | collective-permute-start | bytes 49160 | tf_op jit(solution)/shard_map/ppermute | solution.py:497
  15.7 3.5 %collective-permute-start.1 = (f32[24,128]{1,0:T(8,128)S(1)}, f32[24,128]{1,0:T(8,128)S(1)}, u32[]{:S(2)}, u32[]{:S(2)}) collective-permute-start(f32[24,128]{1,0:T(8,128)S(1)} %get-tuple-element.39.refs_0_), channel_id=1, source_target_pairs={{0,8},{8,0},{16,24},{24,16},{32,40},{40,32},{48,56},{56,48},{64,72... | collective-permute-start | bytes 36872 | tf_op jit(solution)/shard_map/ppermute | solution.py:536
